TPU v7x, 32 devices: a whole 2x2x4 slice. The times are simulated.
32 devices in a mesh: rows: 8 (over y, x, core), reg: 4 (over z).
Axes of the slice: x: 2, y: 2, z: 4, core: 2. Of those that a mesh axis runs over, the one named last changes fastest.
Arguments:
- snapshots: bfloat16 [65536, 1024], P('rows', 'reg'), may hold values from -6 to 6
- rates: bfloat16 [65536, 1024], P('rows', 'reg'), may hold values from -6 to 6
- basis: bfloat16 [65536, 128], P('rows'), may hold values from -0.0234375 to 0.0234375
Outputs:
- gram: float32 [8384, 8384], P('rows', 'reg')
- rhs: float32 [8384, 128], P('rows')
All inputs are finite; a program needn't handle non-finite values.
Results may differ from a plain program's by a relative error of at most 0.0042.
Values may be sent and summed in bfloat16 or wider, within the bound.
No kernel may reach another device: no remote copies, remote signals or barrier semaphores. Data moves between devices by JAX's collectives and lax.ppermute only.
A program may use at most 128 MiB of HBM per device.

v0:
```python
import jax
import jax.numpy as jnp
import numpy as np
from jax import lax
from jax.sharding import PartitionSpec as P


def feature_block(extended, left_table, right_table, start, count):
    left_rows = lax.dynamic_slice_in_dim(left_table, start, count, 0)
    right_rows = lax.dynamic_slice_in_dim(right_table, start, count, 0)
    product = jnp.take(extended, left_rows, axis=0) * jnp.take(extended, right_rows, axis=0)
    return product.astype(jnp.bfloat16)


def per_device(snapshots, rates, basis):
    rank = basis.shape[1]
    width = rank + rank * (rank + 1) // 2
    local_time = snapshots.shape[1]
    total_time = local_time * lax.axis_size("reg")
    row_width = width // lax.axis_size("rows")
    col_width = width // lax.axis_size("reg")
    row_start = lax.axis_index("rows") * row_width
    col_start = lax.axis_index("reg") * col_width
    part_states = jnp.einsum("nr,nt->rt", basis, snapshots, preferred_element_type=jnp.float32)
    part_rates = jnp.einsum("nr,nt->rt", basis, rates, preferred_element_type=jnp.float32)
    states, moments = lax.psum((part_states, part_rates), "rows")
    every_state = lax.all_gather(states, "reg", axis=1, tiled=True)
    pair_i, pair_j = np.triu_indices(rank)
    left_table = jnp.asarray(np.concatenate([np.arange(rank), pair_i]).astype(np.int32))
    right_table = jnp.asarray(np.concatenate([np.full(rank, rank), pair_j]).astype(np.int32))
    extended = jnp.concatenate([every_state, jnp.ones((1, total_time), jnp.float32)], axis=0)
    row_all = feature_block(extended, left_table, right_table, row_start, row_width)
    col_feat = feature_block(extended, left_table, right_table, col_start, col_width)
    gram = lax.dot_general(
        row_all, col_feat, (((1,), (1,)), ((), ())), preferred_element_type=jnp.float32
    )
    row_feat = lax.dynamic_slice_in_dim(row_all, lax.axis_index("reg") * local_time, local_time, 1)
    rate_half = moments.astype(jnp.bfloat16)
    rhs_part = lax.dot_general(
        row_feat, rate_half, (((1,), (1,)), ((), ())), preferred_element_type=jnp.float32
    )
    rhs = lax.psum(rhs_part, "reg")
    return (gram / float(total_time), rhs / float(total_time))


def solution(mesh):
    return jax.shard_map(
        per_device,
        mesh=mesh,
        in_specs=(P("rows", "reg"), P("rows", "reg"), P("rows", None)),
        out_specs=(P("rows", "reg"), P("rows", None)),
        check_vma=False,
    )
```

profile of v0, /device:TPU:0, one launch (start us, length us, event | category | flops | bytes accessed | tf_op | source)
XLA Modules:
  0.0 163.3 jit_solution(7059911273961515719)
XLA Ops:
  7.2 0.0 copy-start
  7.2 0.0 copy-start.2
  7.2 0.0 copy-start.3
  7.2 0.0 all-reduce.5.cloned.1.call-start
  7.2 1.5 copy-done
  8.8 3.7 %fusion.11 = f32[128,256]{1,0:T(8,128)} fusion(bf16[8192,128]{1,0:T(8,128)(2,1)S(1)} %copy-done, bf16[8192,256]{1,0:T(8,128)(2,1)} %param.9), kind=kOutput, calls=%fused_computation.30 | convolution fusion | flops 536870912 | bytes 6422528 | tf_op jit(solution)/shard_map/nr,nt->rt/dot_general | solution.py:24
  12.4 0.0 all-reduce.5.cloned.1.call-update
  12.5 0.0 all-reduce.7.cloned.1.call-start
  12.5 0.0 copy-done.2
  12.5 0.0 copy-done.3
  12.5 0.1 compare_select_fusion.2
  12.6 0.1 compare_and_fusion.2
  12.7 0.1 compare_select_fusion
  12.8 0.1 compare_and_fusion
  12.9 3.0 %fusion.12 = f32[128,256]{1,0:T(8,128)S(1)} fusion(bf16[8192,128]{1,0:T(8,128)(2,1)S(1)} %copy-done, bf16[8192,256]{1,0:T(8,128)(2,1)} %param.10), kind=kOutput, calls=%fused_computation.31 | convolution fusion | flops 536870912 | bytes 6422528 | tf_op jit(solution)/shard_map/nr,nt->rt/dot_general | solution.py:25
  16.0 26.8 %all-reduce.8 = bf16[128,256]{1,0:T(8,128)(2,1)S(1)} all-reduce(f32[128,256]{1,0:T(8,128)S(1)} %fusion.12), channel_id=1, replica_groups=mesh['rows'=8,'reg'=4] {'rows'}, use_global_device_ids=true, to_apply=%region_1.4 | all-reduce | flops 32768 | bytes 196608 | tf_op jit(solution)/shard_map/psum | solution.py:26
  42.8 25.6 %all-reduce.5.cloned.1.call-done = f32[128,256]{1,0:T(8,128)} async-done(((f32[128,256]{1,0:T(8,128)}), f32[128,256]{1,0:T(8,128)}) %all-reduce.5.cloned.1.call-update) | async-done | bytes 131088 | tf_op jit(solution)/shard_map/psum | solution.py:26
  68.4 15.2 %all_gather.3 = f32[128,1024]{1,0:T(8,128)S(1)} all-gather(f32[128,256]{1,0:T(8,128)} %all-reduce.5.cloned.1.call-done), channel_id=1, replica_groups=mesh['rows'=8,'reg'=4] {'reg'}, dimensions={1}, use_global_device_ids=true | all-gather | bytes 655360 | tf_op jit(solution)/shard_map/all_gather | solution.py:27
  83.6 4.9 %gather_fusion = f32[1048,1024]{1,0:T(8,128)} fusion(f32[129,1024]{1,0:T(8,128)S(1)} %concatenate.3, s32[2048]{0:T(1024)S(1)} %pad_clamp_fusion.3), kind=kCustom, calls=%fused_computation.clone | custom fusion | bytes 8589408 | tf_op jit(solution)/shard_map/jit(_take)/gather | solution.py:11
  88.5 4.8 %gather_fusion.1 = f32[1048,1024]{1,0:T(8,128)} fusion(f32[129,1024]{1,0:T(8,128)S(1)} %concatenate.3, s32[2048]{0:T(1024)S(1)} %pad_clamp_fusion.2), kind=kCustom, calls=%fused_computation.2.clone | custom fusion | bytes 8589408 | tf_op jit(solution)/shard_map/jit(_take)/gather | solution.py:11
  93.3 8.1 %gather_fusion.2 = f32[2096,1024]{1,0:T(8,128)} fusion(f32[129,1024]{1,0:T(8,128)S(1)} %concatenate.3, s32[3072]{0:T(1024)S(1)} %pad_clamp_fusion.1), kind=kCustom, calls=%fused_computation.1.clone | custom fusion | bytes 17178816 | tf_op jit(solution)/shard_map/jit(_take)/gather | solution.py:11
  101.3 8.0 %gather_fusion.3 = f32[2096,1024]{1,0:T(8,128)} fusion(f32[129,1024]{1,0:T(8,128)S(1)} %concatenate.3, s32[3072]{0:T(1024)S(1)} %pad_clamp_fusion), kind=kCustom, calls=%fused_computation.3.clone | custom fusion | bytes 17178816 | tf_op jit(solution)/shard_map/jit(_take)/gather | solution.py:11
  109.3 4.0 %fusion.3 = bf16[1048,1024]{1,0:T(8,128)(2,1)S(1)} fusion(f32[1048,1024]{1,0:T(8,128)} %gather_fusion.1, f32[1048,1024]{1,0:T(8,128)} %gather_fusion, pred[1048]{0:T(1024)(128)(4,1)S(1)} %get-tuple-element.6, pred[1048]{0:T(1024)(128)(4,1)S(1)} %get-tuple-element.7), kind=kLoop, calls=%fused_computation.9 | loop fusion | flops 4292608 | bytes 10733616 | tf_op jit(solution)/shard_map/convert_element_type | solution.py:12
  113.3 0.0 copy-start.1
  113.3 1.4 copy-done.1
  114.7 1.1 fusion.6
  115.8 0.0 all-reduce.7.cloned.1.call-update
  115.8 13.1 %convolution_multiply_fusion = f32[1048,2096]{1,0:T(8,128)} fusion(bf16[1048,1024]{1,0:T(8,128)(2,1)} %copy-done.1, f32[2096,1024]{1,0:T(8,128)} %gather_fusion.3, f32[2096,1024]{1,0:T(8,128)} %gather_fusion.2, pred[2096]{0:T(1024)(128)(4,1)S(1)} %get-tuple-element.10, pred[2096]{0:T(1024)(128)(4,1)S(1)} %get-tuple-element.11), kind=kOutput, calls=%fused_computation.4 | convolution fusion | flops 4509434880 | bytes 28107360 | tf_op jit(solution)/shard_map/dot_general | solution.py:34
  128.9 25.6 %all-reduce.7.cloned.1.call-done = f32[1048,128]{1,0:T(8,128)} async-done(((f32[1048,128]{1,0:T(8,128)}), f32[1048,128]{1,0:T(8,128)}) %all-reduce.7.cloned.1.call-update) | async-done | bytes 536592 | tf_op jit(solution)/shard_map/psum | solution.py:42
  154.6 1.9 %broadcast_multiply_fusion = f32[1048,128]{1,0:T(8,128)} fusion(f32[1048,128]{1,0:T(8,128)} %all-reduce.7.cloned.1.call-done), kind=kLoop, calls=%fused_computation.14 | loop fusion | flops 134144 | bytes 1073152 | tf_op jit(solution)/shard_map/div | solution.py:43
  (5 shorter events, 0.1 us)
Async XLA Ops:
  7.2 1.6 copy-start
  7.2 5.3 %copy-start.2 = (s32[8384]{0:T(1024)S(1)}, s32[8384]{0:T(1024)}, u32[]{:S(2)}) copy-start(s32[8384]{0:T(1024)} %constant.52.clone) | copy-start | bytes 100612
  7.2 5.3 %copy-start.3 = (s32[8384]{0:T(1024)S(1)}, s32[8384]{0:T(1024)}, u32[]{:S(2)}) copy-start(s32[8384]{0:T(1024)} %constant.53.clone) | copy-start | bytes 100612
  7.2 61.2 %all-reduce.5.cloned.1.call-start = ((), (), s32[]{:S(2)}) async-start(), calls=%async_computation | async-start | bytes 262144 | tf_op jit(solution)/shard_map/psum | solution.py:26
  12.5 142.1 %all-reduce.7.cloned.1.call-start = ((), (), s32[]{:S(2)}) async-start(), calls=%async_computation.1 | async-start | bytes 1073152 | tf_op jit(solution)/shard_map/psum | solution.py:42
  113.3 1.4 copy-start.1
Sparse Core Ops, SparseCore 0:
  12.6 55.7 all-reduce.4
  115.9 38.5 all-reduce.6
where the time goes:
time: 164 us; the launch traced here: 163 us
  waiting for transfers between devices  51.3 us (31%)
  blocking collectives  42 us (26%)
  local copies, waits for them, and re-layouts  28.6 us (17%)
  matrix products  20.9 us (13%)
  between operations  14.2 us (9%)
  other arithmetic  6.2 us (4%)
    psum x1, blocking collectives, per_device(): states, moments = lax.psum((part_states, part_rates), 'rows')  26.8 us
    psum x1, waiting for transfers between devices, per_device(): states, moments = lax.psum((part_states, part_rates), 'rows')  25.6 us
    psum x1, waiting for transfers between devices, per_device(): rhs = lax.psum(rhs_part, 'reg')  25.6 us
    all_gather x1, blocking collectives, per_device(): every_state = lax.all_gather(states, 'reg', axis=1, tiled=True)  15.2 us
    dot_general x1, matrix products, per_device(): lax.dot_general(row_all, col_feat, (((1,), (1,)), ((), ())), preferred_el...  13.1 us
    gather x2, local copies, waits for them, and re-layouts, feature_block(): jnp.take(extended, left_rows, axis=0)  12.9 us
    gather x2, local copies, waits for them, and re-layouts, feature_block(): jnp.take(extended, right_rows, axis=0)  12.8 us
    convert_element_type x1, other arithmetic, feature_block(): return product.astype(jnp.bfloat16)  3.97 us
  transfers between devices with their start and end apart: 2, of which 2 were waited for; matrix products, arithmetic and copies ran while one was open for 10% of the time, Pallas kernels for 0%

commit v1 on v0

v1 whole, which is shorter than its diff:
```python
import functools

import jax
import jax.numpy as jnp
from jax import lax
from jax.experimental import pallas as pl
from jax.experimental.pallas import tpu as pltpu
from jax.sharding import PartitionSpec as P

TILE = 256
MIB = 1 << 20


def round_up(value, step):
    return (value + step - 1) // step * step


def partners(size):
    if size & (size - 1) == 0:
        return [[(i, i ^ k) for i in range(size)] for k in range(1, size)]
    return [[(i, (i + k) % size) for i in range(size)] for k in range(1, size)]


def project_kernel(place, basis_ref, snap_ref, rate_ref, keep_ref, send_ref, acc):
    step = pl.program_id(0)
    half = acc.shape[1] // 2
    contract = (((0,), (0,)), ((), ()))
    left = basis_ref[...]
    part_states = lax.dot_general(left, snap_ref[...], contract, preferred_element_type=jnp.float32)
    part_rates = lax.dot_general(left, rate_ref[...], contract, preferred_element_type=jnp.float32)

    @pl.when(step == 0)
    def _():
        acc[0] = part_states
        acc[1] = part_rates

    @pl.when(step > 0)
    def _():
        acc[0] += part_states
        acc[1] += part_rates

    @pl.when(step == pl.num_programs(0) - 1)
    def _():
        mine = pl.multiple_of(place[0] * half, half)
        other = pl.multiple_of(half - place[0] * half, half)
        for part in range(2):
            keep_ref[part] = acc[part, pl.ds(mine, half), :]
            send_ref[part] = acc[part, pl.ds(other, half), :]


def project(place, basis, snapshots, rates):
    rows, rank = basis.shape
    times = snapshots.shape[1]
    chunk = rows
    while chunk > 1024 and chunk % 2 == 0:
        chunk //= 2
    out = jax.ShapeDtypeStruct((2, rank // 2, times), jnp.float32)
    return pl.pallas_call(
        project_kernel,
        grid_spec=pltpu.PrefetchScalarGridSpec(
            num_scalar_prefetch=1,
            grid=(rows // chunk,),
            in_specs=[
                pl.BlockSpec((chunk, rank), lambda i, s: (i, 0)),
                pl.BlockSpec((chunk, times), lambda i, s: (i, 0)),
                pl.BlockSpec((chunk, times), lambda i, s: (i, 0)),
            ],
            out_specs=[pl.BlockSpec((2, rank // 2, times), lambda i, s: (0, 0, 0))] * 2,
            scratch_shapes=[pltpu.VMEM((2, rank, times), jnp.float32)],
        ),
        out_shape=[out, out],
        compiler_params=pltpu.CompilerParams(vmem_limit_bytes=24 * MIB),
        cost_estimate=pl.CostEstimate(
            flops=4 * rows * rank * times, bytes_accessed=2 * rows * (rank + 2 * times), transcendentals=0
        ),
        name="project",
    )(place, basis, snapshots, rates)


def combine_kernel(*refs):
    out_ref = refs[-1]
    total = refs[0][...]
    for ref in refs[1:-1]:
        total = total + ref[...]
    half = total.shape[1]
    states = total[0]
    high = states.astype(jnp.bfloat16)
    out_ref[0:half] = high
    out_ref[half : 2 * half] = (states - high.astype(jnp.float32)).astype(jnp.bfloat16)
    out_ref[2 * half :] = total[1].astype(jnp.bfloat16)


def combine(parts):
    _, half, times = parts[0].shape
    return pl.pallas_call(
        combine_kernel,
        out_shape=jax.ShapeDtypeStruct((3 * half, times), jnp.bfloat16),
        name="combine",
    )(*parts)


def feature_rows(first, count, rank, states):
    shape = (count, rank)
    feature = first + lax.broadcasted_iota(jnp.int32, shape, 0)
    lane = lax.broadcasted_iota(jnp.int32, shape, 1)
    run_start = rank + lane * rank - (lane * (lane - 1)) // 2
    run_end = run_start + rank - lane
    in_run = (feature >= run_start) & (feature < run_end)
    shift = jnp.sum(jnp.where(in_run, run_start - lane, 0), axis=1, keepdims=True)
    left = in_run.astype(jnp.float32).astype(jnp.bfloat16)
    right = (lane == feature - shift).astype(jnp.float32).astype(jnp.bfloat16)
    pick = functools.partial(jnp.dot, preferred_element_type=jnp.float32)
    left_rows = pick(jnp.concatenate([left, left], axis=1), states)
    right_rows = pick(jnp.concatenate([right, right], axis=1), states)
    linear = (feature[:, :1] < rank).astype(jnp.float32)
    return ((left_rows + linear) * right_rows).astype(jnp.bfloat16)


def gram_kernel(slabs, total_time, place, *refs):
    own, other = refs[:slabs], refs[slabs : 2 * slabs]
    gram_ref, rhs_ref, states, moments, row_feat, col_feat = refs[2 * slabs :]
    step = pl.program_id(0)
    rank = moments.shape[0]
    half, local = rank // 2, own[0].shape[1]
    row_width = gram_ref.shape[0]
    last = pl.num_programs(0) - 1

    @pl.when(step == 0)
    def _():
        for side, pieces in ((0, own), (1, other)):
            at = (place[0] + side) % 2 * half
            for k, piece in enumerate(pieces):
                columns = slice(k * local, (k + 1) * local)
                states[pl.ds(pl.multiple_of(at, half), half), columns] = piece[0:half]
                states[pl.ds(pl.multiple_of(rank + at, half), half), columns] = piece[half : 2 * half]
                moments[pl.ds(pl.multiple_of(at, half), half), columns] = piece[2 * half :]
        for low in range(0, row_feat.shape[0], TILE):
            count = min(TILE, row_feat.shape[0] - low)
            row_feat[low : low + count] = feature_rows(place[1] + low, count, rank, states[...])

    col_feat[...] = feature_rows(place[2] + step * TILE, TILE, rank, states[...])

    @pl.when(step == last)
    def _():
        col_feat[TILE - rank :] = moments[...]

    product = lax.dot_general(
        row_feat[...], col_feat[...], (((1,), (1,)), ((), ())), preferred_element_type=jnp.float32
    )[:row_width]
    product = product / float(total_time)
    gram_ref[...] = product

    @pl.when(step == last)
    def _():
        rhs_ref[...] = product[:, TILE - rank :]


def gram_and_rhs(place, own, other, rank, row_width, col_width):
    slabs = len(own)
    local = own[0].shape[1]
    total_time = slabs * local
    tiles = (col_width + rank + TILE - 1) // TILE
    row_pad = round_up(row_width, 16)
    piece = pl.BlockSpec((3 * rank // 2, local), lambda i, s: (0, 0))
    return pl.pallas_call(
        functools.partial(gram_kernel, slabs, total_time),
        grid_spec=pltpu.PrefetchScalarGridSpec(
            num_scalar_prefetch=1,
            grid=(tiles,),
            in_specs=[piece] * (2 * slabs),
            out_specs=[
                pl.BlockSpec((row_width, TILE), lambda i, s: (0, i)),
                pl.BlockSpec((row_width, rank), lambda i, s: (0, 0)),
            ],
            scratch_shapes=[
                pltpu.VMEM((2 * rank, total_time), jnp.bfloat16),
                pltpu.VMEM((rank, total_time), jnp.bfloat16),
                pltpu.VMEM((row_pad, total_time), jnp.bfloat16),
                pltpu.VMEM((TILE, total_time), jnp.bfloat16),
            ],
        ),
        out_shape=[
            jax.ShapeDtypeStruct((row_width, col_width), jnp.float32),
            jax.ShapeDtypeStruct((row_width, rank), jnp.float32),
        ],
        compiler_params=pltpu.CompilerParams(vmem_limit_bytes=40 * MIB),
        cost_estimate=pl.CostEstimate(
            flops=2 * row_width * (col_width + rank) * total_time,
            bytes_accessed=4 * row_width * (col_width + rank),
            transcendentals=0,
        ),
        name="gram",
    )(place, *own, *other)


def per_device(snapshots, rates, basis):
    rank = basis.shape[1]
    width = rank + rank * (rank + 1) // 2
    size_rows, size_reg = lax.axis_size("rows"), lax.axis_size("reg")
    row_width, col_width = width // size_rows, width // size_reg
    row_at, reg_at = lax.axis_index("rows"), lax.axis_index("reg")
    place = jnp.stack([row_at % 2, row_at * row_width, reg_at * col_width]).astype(jnp.int32)
    swap = [(i, i ^ 1) for i in range(size_rows)]
    keep, send = project(place, basis, snapshots, rates)
    chip = keep + lax.ppermute(send, "rows", swap)
    plane = [[(2 * a + c, 2 * b + c) for a, b in perm for c in range(2)] for perm in partners(size_rows // 2)]
    mine = combine([chip] + [lax.ppermute(chip, "rows", perm) for perm in plane])
    own = [mine] + [lax.ppermute(mine, "reg", perm) for perm in partners(size_reg)]
    other = [lax.ppermute(piece, "rows", swap) for piece in own]
    return tuple(gram_and_rhs(place, own, other, rank, row_width, col_width))


def solution(mesh):
    return jax.shard_map(
        per_device,
        mesh=mesh,
        in_specs=(P("rows", "reg"), P("rows", "reg"), P("rows", None)),
        out_specs=(P("rows", "reg"), P("rows", None)),
        check_vma=False,
    )
```

time: 164 us -> 55.2 us (0.34)
  blocking collectives: 42 us -> 0 us
  waiting for transfers between devices: 51.3 us -> 16.2 us
  matrix products: 20.9 us -> 0 us
  local copies, waits for them, and re-layouts: 28.6 us -> 7.9 us
  Pallas kernels: 0 us -> 20.1 us
  between operations: 14.2 us -> 0.68 us
  starting transfers between devices: 0.08 us -> 9.94 us
  other arithmetic: 6.2 us -> 0.09 us
    psum x2 -> x0, waiting for transfers between devices: 51.3 us -> none  [the longest x1 25.6 us: per_device(): states, moments = lax.psum((part_states, part_rates), 'rows')]
    psum x1 -> x0, blocking collectives: 26.8 us -> none  [per_device(): states, moments = lax.psum((part_states, part_rates), 'rows')]
    gather x4 -> x0, local copies, waits for them, and re-layouts: 25.7 us -> none  [the longest x2 12.9 us: feature_block(): jnp.take(extended, left_rows, axis=0)]
    dot_general x4 -> x0, matrix products: 20.9 us -> none  [the longest x1 13.1 us: per_device(): lax.dot_general(row_all, col_feat, (((1,), (1,)), ((), ())), preferred_el...]
    pallas_call x0 -> x3, Pallas kernels: none -> 20.1 us  [the longest x1 14.9 us: gram_and_rhs(): pl.pallas_call(functools.partial(gram_kernel, slabs, total_time), grid_sp...]
    ppermute x0 -> x11, waiting for transfers between devices: none -> 16.2 us  [the longest x3 8.06 us: per_device(): lax.ppermute(mine, 'reg', perm)]
    all_gather x1 -> x0, blocking collectives: 15.2 us -> none  [per_device(): every_state = lax.all_gather(states, 'reg', axis=1, tiled=True)]
    ppermute x0 -> x11, starting transfers between devices: none -> 9.94 us  [the longest x3 4.52 us: per_device(): lax.ppermute(chip, 'rows', perm)]
  transfers between devices with their start and end apart: 2 -> 11, of which waited for: 2 -> 8; matrix products, arithmetic and copies ran while one was open for 10% -> 0% of each run, Pallas kernels for 0% -> 0%
where the time goes in v1:
time: 55.2 us; the launch traced here: 55 us
  Pallas kernels  20.1 us (36%)
  waiting for transfers between devices  16.2 us (29%)
  starting transfers between devices  9.94 us (18%)
  local copies, waits for them, and re-layouts  7.9 us (14%)
  between operations  0.68 us (1%)
    pallas_call x1, Pallas kernels, gram_and_rhs(): pl.pallas_call(functools.partial(gram_kernel, slabs, total_time), grid_sp...  14.9 us
    ppermute x3, waiting for transfers between devices, per_device(): lax.ppermute(mine, 'reg', perm)  8.06 us
    unnamed x16, local copies, waits for them, and re-layouts  7.9 us
    ppermute x3, waiting for transfers between devices, per_device(): lax.ppermute(chip, 'rows', perm)  6.25 us
    ppermute x3, starting transfers between devices, per_device(): lax.ppermute(chip, 'rows', perm)  4.52 us
    ppermute x3, starting transfers between devices, per_device(): lax.ppermute(mine, 'reg', perm)  4.39 us
    pallas_call x1, Pallas kernels, project(): pl.pallas_call(project_kernel, grid_spec=pltpu.PrefetchScalarGridSpec(num...  3.46 us
    pallas_call x1, Pallas kernels, combine(): pl.pallas_call(combine_kernel, out_shape=jax.ShapeDtypeStruct((3 * half,...  1.76 us
  transfers between devices with their start and end apart: 11, of which 8 were waited for; matrix products, arithmetic and copies ran while one was open for 0% of the time, Pallas kernels for 0%

profile of v1, /device:TPU:0, one launch (start us, length us, event | category | flops | bytes accessed | tf_op | source)
XLA Modules:
  0.0 55.0 jit_solution(6626214929660306293)
XLA Ops:
  0.6 0.1 pad_add_fusion.place
  0.7 0.0 copy-start
  0.7 2.2 %copy-done = bf16[8192,256]{1,0:T(8,128)(2,1)S(1)} copy-done((bf16[8192,256]{1,0:T(8,128)(2,1)S(1)}, bf16[8192,256]{1,0:T(8,128)(2,1)}, u32[]{:S(2)}) %copy-start) | copy-done | bytes 4194328
  2.9 0.0 copy-start.1
  2.9 2.2 %copy-done.1 = bf16[8192,256]{1,0:T(8,128)(2,1)S(1)} copy-done((bf16[8192,256]{1,0:T(8,128)(2,1)S(1)}, bf16[8192,256]{1,0:T(8,128)(2,1)}, u32[]{:S(2)}) %copy-start.1) | copy-done | bytes 4194328
  5.1 0.0 copy-start.2
  5.1 1.6 %copy-done.2 = bf16[8192,128]{1,0:T(8,128)(2,1)S(1)} copy-done((bf16[8192,128]{1,0:T(8,128)(2,1)S(1)}, bf16[8192,128]{1,0:T(8,128)(2,1)}, u32[]{:S(2)}) %copy-start.2) | copy-done | bytes 2097176
  6.7 3.5 %project.1 = (f32[2,64,256]{2,1,0:T(8,128)S(1)}, f32[2,64,256]{2,1,0:T(8,128)S(1)}) custom-call(s32[3]{0:T(128)S(1)} %pad_add_fusion.place, bf16[8192,128]{1,0:T(8,128)(2,1)S(1)} %copy-done.2, bf16[8192,256]{1,0:T(8,128)(2,1)S(1)} %copy-done, bf16[8192,256]{1,0:T(8,128)(2,1)S(1)} %copy-done.1), custom_call_target="tpu_custom_call" | custom-call | flops 1073741824 | bytes 10485760 | tf_op jit(solution)/shard_map/project/pallas_call | solution.py:58
  10.2 0.5 collective-permute-start
  10.7 1.0 %collective-permute-done = f32[2,64,256]{2,1,0:T(8,128)S(1)} collective-permute-done((f32[2,64,256]{2,1,0:T(8,128)S(1)}, f32[2,64,256]{2,1,0:T(8,128)S(1)}, u32[]{:S(2)}, u32[]{:S(2)}) %collective-permute-start) | collective-permute-done | bytes 131104 | tf_op jit(solution)/shard_map/ppermute | solution.py:205
  11.7 0.0 copy-start.4
  11.7 3.9 %collective-permute-start.3 = (f32[2,64,256]{2,1,0:T(8,128)S(1)}, f32[2,64,256]{2,1,0:T(8,128)S(1)}, u32[]{:S(2)}, u32[]{:S(2)}) collective-permute-start(f32[2,64,256]{2,1,0:T(8,128)S(1)} %add.8.refs_0_), channel_id=1, source_target_pairs={{0,24},{4,28},{8,16},{12,20},{16,8},{20,12},{24,0},{28,4},{1,25},{... | collective-permute-start | bytes 393224 | tf_op jit(solution)/shard_map/ppermute | solution.py:207
  15.6 0.5 collective-permute-start.2
  16.1 0.1 collective-permute-start.1
  16.2 3.3 %collective-permute-done.3.refs_3_ = f32[2,64,256]{2,1,0:T(8,128)S(1)} collective-permute-done((f32[2,64,256]{2,1,0:T(8,128)S(1)}, f32[2,64,256]{2,1,0:T(8,128)S(1)}, u32[]{:S(2)}, u32[]{:S(2)}) %collective-permute-start.3) | collective-permute-done | bytes 131104 | tf_op jit(solution)/shard_map/ppermute | solution.py:207
  19.5 0.0 copy-start.5
  19.5 2.7 %collective-permute-done.2.refs_2_ = f32[2,64,256]{2,1,0:T(8,128)S(1)} collective-permute-done((f32[2,64,256]{2,1,0:T(8,128)S(1)}, f32[2,64,256]{2,1,0:T(8,128)S(1)}, u32[]{:S(2)}, u32[]{:S(2)}) %collective-permute-start.2) | collective-permute-done | bytes 131104 | tf_op jit(solution)/shard_map/ppermute | solution.py:207
  22.2 0.0 copy-start.6
  22.2 0.3 collective-permute-done.1.refs_1_
  22.5 0.0 copy-done.4
  22.5 0.0 copy-done.5
  22.5 0.4 copy-done.6
  22.8 0.0 copy-start.7
  22.8 0.7 %copy-done.7 = f32[2,64,256]{2,1,0:T(8,128)} copy-done((f32[2,64,256]{2,1,0:T(8,128)}, f32[2,64,256]{2,1,0:T(8,128)S(1)}, u32[]{:S(2)}) %copy-start.7) | copy-done | bytes 131096
  23.5 1.8 %combine.1.refs_0_ = bf16[192,256]{1,0:T(8,128)(2,1)} custom-call(f32[2,64,256]{2,1,0:T(8,128)} %copy-done.4, f32[2,64,256]{2,1,0:T(8,128)} %copy-done.7, f32[2,64,256]{2,1,0:T(8,128)} %copy-done.6, f32[2,64,256]{2,1,0:T(8,128)} %copy-done.5), custom_call_target="tpu_custom_call" | custom-call | tf_op jit(solution)/shard_map/combine/pallas_call | solution.py:95
  25.3 3.8 %collective-permute-start.6 = (bf16[192,256]{1,0:T(8,128)(2,1)}, bf16[192,256]{1,0:T(8,128)(2,1)S(1)}, u32[]{:S(2)}, u32[]{:S(2)}) collective-permute-start(bf16[192,256]{1,0:T(8,128)(2,1)} %combine.1.refs_0_), channel_id=1, source_target_pairs={{0,3},{1,2},{2,1},{3,0},{4,7},{5,6},{6,5},{7,4},{8,11},{9,10},{10,... | collective-permute-start | bytes 294920 | tf_op jit(solution)/shard_map/ppermute | solution.py:208
  29.0 0.0 collective-permute-start.5
  29.1 0.6 %collective-permute-start.4 = (bf16[192,256]{1,0:T(8,128)(2,1)}, bf16[192,256]{1,0:T(8,128)(2,1)S(1)}, u32[]{:S(2)}, u32[]{:S(2)}) collective-permute-start(bf16[192,256]{1,0:T(8,128)(2,1)} %combine.1.refs_0_), channel_id=1, source_target_pairs={{0,1},{1,0},{2,3},{3,2},{4,5},{5,4},{6,7},{7,6},{8,9},{9,8},{10,11... | collective-permute-start | bytes 294920 | tf_op jit(solution)/shard_map/ppermute | solution.py:208
  29.6 0.0 collective-permute-start.7
  29.6 3.3 %collective-permute-done.6.refs_3_ = bf16[192,256]{1,0:T(8,128)(2,1)S(1)} collective-permute-done((bf16[192,256]{1,0:T(8,128)(2,1)}, bf16[192,256]{1,0:T(8,128)(2,1)S(1)}, u32[]{:S(2)}, u32[]{:S(2)}) %collective-permute-start.6) | collective-permute-done | bytes 98336 | tf_op jit(solution)/shard_map/ppermute | solution.py:208
  33.0 0.0 collective-permute-start.10
  33.0 4.7 %collective-permute-done.5.refs_2_ = bf16[192,256]{1,0:T(8,128)(2,1)S(1)} collective-permute-done((bf16[192,256]{1,0:T(8,128)(2,1)}, bf16[192,256]{1,0:T(8,128)(2,1)S(1)}, u32[]{:S(2)}, u32[]{:S(2)}) %collective-permute-start.5) | collective-permute-done | bytes 98336 | tf_op jit(solution)/shard_map/ppermute | solution.py:208
  37.7 0.0 collective-permute-start.9
  37.7 0.0 collective-permute-done.4.refs_1_
  37.7 0.5 collective-permute-start.8
  38.2 0.0 collective-permute-done.7.refs_4_
  38.2 0.0 collective-permute-done.10.refs_7_
  38.2 0.8 %collective-permute-done.9.refs_6_ = bf16[192,256]{1,0:T(8,128)(2,1)S(1)} collective-permute-done((bf16[192,256]{1,0:T(8,128)(2,1)S(1)}, bf16[192,256]{1,0:T(8,128)(2,1)S(1)}, u32[]{:S(2)}, u32[]{:S(2)}) %collective-permute-start.9) | collective-permute-done | bytes 98336 | tf_op jit(solution)/shard_map/ppermute | solution.py:209
  39.0 0.2 collective-permute-done.8.refs_5_
  39.2 0.0 copy-start.3
  39.2 0.9 %copy-done.3 = bf16[192,256]{1,0:T(8,128)(2,1)S(1)} copy-done((bf16[192,256]{1,0:T(8,128)(2,1)S(1)}, bf16[192,256]{1,0:T(8,128)(2,1)}, u32[]{:S(2)}) %copy-start.3) | copy-done | bytes 98328
  40.1 14.9 %gram.1 = (f32[1048,2096]{1,0:T(8,128)}, f32[1048,128]{1,0:T(8,128)}) custom-call(s32[3]{0:T(128)S(1)} %pad_add_fusion.place, bf16[192,256]{1,0:T(8,128)(2,1)S(1)} %copy-done.3, bf16[192,256]{1,0:T(8,128)(2,1)S(1)} %collective-permute-done.4.refs_1_, bf16[192,256]{1,0:T(8,128)(2,1)S(1)} %collective-permute-done.5.refs_2_, ...), custom_call_target="tpu_custom_call" | custom-call | flops 4773380096 | bytes 9323008 | tf_op jit(solution)/shard_map/gram/pallas_call | solution.py:165
  (1 shorter events, 0.0 us)
Async XLA Ops:
  0.7 2.2 %copy-start = (bf16[8192,256]{1,0:T(8,128)(2,1)S(1)}, bf16[8192,256]{1,0:T(8,128)(2,1)}, u32[]{:S(2)}) copy-start(bf16[8192,256]{1,0:T(8,128)(2,1)} %snap_ref.1) | copy-start | bytes 12582916
  2.9 2.2 %copy-start.1 = (bf16[8192,256]{1,0:T(8,128)(2,1)S(1)}, bf16[8192,256]{1,0:T(8,128)(2,1)}, u32[]{:S(2)}) copy-start(bf16[8192,256]{1,0:T(8,128)(2,1)} %rate_ref.1) | copy-start | bytes 12582916
  5.1 1.6 %copy-start.2 = (bf16[8192,128]{1,0:T(8,128)(2,1)S(1)}, bf16[8192,128]{1,0:T(8,128)(2,1)}, u32[]{:S(2)}) copy-start(bf16[8192,128]{1,0:T(8,128)(2,1)} %basis_ref.1) | copy-start | bytes 6291460
  10.2 1.5 %collective-permute-start = (f32[2,64,256]{2,1,0:T(8,128)S(1)}, f32[2,64,256]{2,1,0:T(8,128)S(1)}, u32[]{:S(2)}, u32[]{:S(2)}) collective-permute-start(f32[2,64,256]{2,1,0:T(8,128)S(1)} %get-tuple-element.5), channel_id=1, source_target_pairs={{0,4},{4,0},{8,12},{12,8},{16,20},{20,16},{24,28},{28,24},{1,5},{5... | collective-permute-start | bytes 393224 | tf_op jit(solution)/shard_map/ppermute | solution.py:205
  11.7 10.8 %copy-start.4 = (f32[2,64,256]{2,1,0:T(8,128)}, f32[2,64,256]{2,1,0:T(8,128)S(1)}, u32[]{:S(2)}) copy-start(f32[2,64,256]{2,1,0:T(8,128)S(1)} %add.8.refs_0_) | copy-start | bytes 393220
  11.7 7.8 %collective-permute-start.3 = (f32[2,64,256]{2,1,0:T(8,128)S(1)}, f32[2,64,256]{2,1,0:T(8,128)S(1)}, u32[]{:S(2)}, u32[]{:S(2)}) collective-permute-start(f32[2,64,256]{2,1,0:T(8,128)S(1)} %add.8.refs_0_), channel_id=1, source_target_pairs={{0,24},{4,28},{8,16},{12,20},{16,8},{20,12},{24,0},{28,4},{1,25},{... | collective-permute-start | bytes 393224 | tf_op jit(solution)/shard_map/ppermute | solution.py:207
  15.6 6.6 %collective-permute-start.2 = (f32[2,64,256]{2,1,0:T(8,128)S(1)}, f32[2,64,256]{2,1,0:T(8,128)S(1)}, u32[]{:S(2)}, u32[]{:S(2)}) collective-permute-start(f32[2,64,256]{2,1,0:T(8,128)S(1)} %add.8.refs_0_), channel_id=1, source_target_pairs={{0,16},{4,20},{8,24},{12,28},{16,0},{20,4},{24,8},{28,12},{1,17},{... | collective-permute-start | bytes 393224 | tf_op jit(solution)/shard_map/ppermute | solution.py:207
  16.1 6.4 %collective-permute-start.1 = (f32[2,64,256]{2,1,0:T(8,128)S(1)}, f32[2,64,256]{2,1,0:T(8,128)S(1)}, u32[]{:S(2)}, u32[]{:S(2)}) collective-permute-start(f32[2,64,256]{2,1,0:T(8,128)S(1)} %add.8.refs_0_), channel_id=1, source_target_pairs={{0,8},{4,12},{8,0},{12,4},{16,24},{20,28},{24,16},{28,20},{1,9},{5... | collective-permute-start | bytes 393224 | tf_op jit(solution)/shard_map/ppermute | solution.py:207
  19.5 3.0 %copy-start.5 = (f32[2,64,256]{2,1,0:T(8,128)}, f32[2,64,256]{2,1,0:T(8,128)S(1)}, u32[]{:S(2)}) copy-start(f32[2,64,256]{2,1,0:T(8,128)S(1)} %collective-permute-done.3.refs_3_) | copy-start | bytes 393220
  22.2 0.7 %copy-start.6 = (f32[2,64,256]{2,1,0:T(8,128)}, f32[2,64,256]{2,1,0:T(8,128)S(1)}, u32[]{:S(2)}) copy-start(f32[2,64,256]{2,1,0:T(8,128)S(1)} %collective-permute-done.2.refs_2_) | copy-start | bytes 393220
  22.8 0.7 %copy-start.7 = (f32[2,64,256]{2,1,0:T(8,128)}, f32[2,64,256]{2,1,0:T(8,128)S(1)}, u32[]{:S(2)}) copy-start(f32[2,64,256]{2,1,0:T(8,128)S(1)} %collective-permute-done.1.refs_1_) | copy-start | bytes 393220
  25.3 7.7 %collective-permute-start.6 = (bf16[192,256]{1,0:T(8,128)(2,1)}, bf16[192,256]{1,0:T(8,128)(2,1)S(1)}, u32[]{:S(2)}, u32[]{:S(2)}) collective-permute-start(bf16[192,256]{1,0:T(8,128)(2,1)} %combine.1.refs_0_), channel_id=1, source_target_pairs={{0,3},{1,2},{2,1},{3,0},{4,7},{5,6},{6,5},{7,4},{8,11},{9,10},{10,... | collective-permute-start | bytes 294920 | tf_op jit(solution)/shard_map/ppermute | solution.py:208
  29.0 8.7 %collective-permute-start.5 = (bf16[192,256]{1,0:T(8,128)(2,1)}, bf16[192,256]{1,0:T(8,128)(2,1)S(1)}, u32[]{:S(2)}, u32[]{:S(2)}) collective-permute-start(bf16[192,256]{1,0:T(8,128)(2,1)} %combine.1.refs_0_), channel_id=1, source_target_pairs={{0,2},{1,3},{2,0},{3,1},{4,6},{5,7},{6,4},{7,5},{8,10},{9,11},{10,... | collective-permute-start | bytes 294920 | tf_op jit(solution)/shard_map/ppermute | solution.py:208
  29.1 8.7 %collective-permute-start.4 = (bf16[192,256]{1,0:T(8,128)(2,1)}, bf16[192,256]{1,0:T(8,128)(2,1)S(1)}, u32[]{:S(2)}, u32[]{:S(2)}) collective-permute-start(bf16[192,256]{1,0:T(8,128)(2,1)} %combine.1.refs_0_), channel_id=1, source_target_pairs={{0,1},{1,0},{2,3},{3,2},{4,5},{5,4},{6,7},{7,6},{8,9},{9,8},{10,11... | collective-permute-start | bytes 294920 | tf_op jit(solution)/shard_map/ppermute | solution.py:208
  29.6 8.6 %collective-permute-start.7 = (bf16[192,256]{1,0:T(8,128)(2,1)}, bf16[192,256]{1,0:T(8,128)(2,1)S(1)}, u32[]{:S(2)}, u32[]{:S(2)}) collective-permute-start(bf16[192,256]{1,0:T(8,128)(2,1)} %combine.1.refs_0_), channel_id=1, source_target_pairs={{0,4},{4,0},{8,12},{12,8},{16,20},{20,16},{24,28},{28,24},{1,5},{5... | collective-permute-start | bytes 294920 | tf_op jit(solution)/shard_map/ppermute | solution.py:209
  33.0 5.2 %collective-permute-start.10 = (bf16[192,256]{1,0:T(8,128)(2,1)S(1)}, bf16[192,256]{1,0:T(8,128)(2,1)S(1)}, u32[]{:S(2)}, u32[]{:S(2)}) collective-permute-start(bf16[192,256]{1,0:T(8,128)(2,1)S(1)} %collective-permute-done.6.refs_3_), channel_id=1, source_target_pairs={{0,4},{4,0},{8,12},{12,8},{16,20},{20,16},{24,28},{28,24},{1,5},{5... | collective-permute-start | bytes 294920 | tf_op jit(solution)/shard_map/ppermute | solution.py:209
  37.7 1.3 %collective-permute-start.9 = (bf16[192,256]{1,0:T(8,128)(2,1)S(1)}, bf16[192,256]{1,0:T(8,128)(2,1)S(1)}, u32[]{:S(2)}, u32[]{:S(2)}) collective-permute-start(bf16[192,256]{1,0:T(8,128)(2,1)S(1)} %collective-permute-done.5.refs_2_), channel_id=1, source_target_pairs={{0,4},{4,0},{8,12},{12,8},{16,20},{20,16},{24,28},{28,24},{1,5},{5... | collective-permute-start | bytes 294920 | tf_op jit(solution)/shard_map/ppermute | solution.py:209
  37.7 1.5 %collective-permute-start.8 = (bf16[192,256]{1,0:T(8,128)(2,1)S(1)}, bf16[192,256]{1,0:T(8,128)(2,1)S(1)}, u32[]{:S(2)}, u32[]{:S(2)}) collective-permute-start(bf16[192,256]{1,0:T(8,128)(2,1)S(1)} %collective-permute-done.4.refs_1_), channel_id=1, source_target_pairs={{0,4},{4,0},{8,12},{12,8},{16,20},{20,16},{24,28},{28,24},{1,5},{5... | collective-permute-start | bytes 294920 | tf_op jit(solution)/shard_map/ppermute | solution.py:209
  39.2 0.9 %copy-start.3 = (bf16[192,256]{1,0:T(8,128)(2,1)S(1)}, bf16[192,256]{1,0:T(8,128)(2,1)}, u32[]{:S(2)}) copy-start(bf16[192,256]{1,0:T(8,128)(2,1)} %combine.1.refs_0_) | copy-start | bytes 294916

commit v2 on v0

v2 whole, which is shorter than its diff:
```python
import functools

import jax
import jax.numpy as jnp
from jax import lax
from jax.experimental import pallas as pl
from jax.experimental.pallas import tpu as pltpu
from jax.sharding import PartitionSpec as P

TILE = 256
EARLY = 2
BLOCK = 272
CHUNKS = 8
MIB = 1 << 20


def round_up(value, step):
    return (value + step - 1) // step * step


def partners(size):
    if size & (size - 1) == 0:
        return [[(i, i ^ k) for i in range(size)] for k in range(1, size)]
    return [[(i, (i + k) % size) for i in range(size)] for k in range(1, size)]


WHOLE = pl.BlockSpec(memory_space=pltpu.VMEM)
ANYWHERE = pl.BlockSpec(memory_space=pl.ANY)
SCALARS = pl.BlockSpec(memory_space=pltpu.SMEM)


def in_hbm(array):
    return pltpu.with_memory_space_constraint(array, pltpu.HBM)


def in_vmem(array):
    return pltpu.with_memory_space_constraint(array, pltpu.VMEM)


def project_kernel(chunks, basis_hbm, snap_hbm, rate_hbm, keep_ref, send_ref, basis, snap, rate, acc, sems):
    rows = basis.shape[0] // chunks
    half = acc.shape[1] // 2
    copies = []
    for c in range(chunks):
        part = pl.ds(c * rows, rows)
        copies.append(
            [
                pltpu.make_async_copy(source.at[part], target.at[part], sems.at[k, c])
                for k, (source, target) in enumerate(((basis_hbm, basis), (snap_hbm, snap), (rate_hbm, rate)))
            ]
        )
        for copy in copies[-1]:
            copy.start()
    for c in range(chunks):
        for copy in copies[c]:
            copy.wait()
        part = pl.ds(c * rows, rows)
        left = basis[part, :].T
        for k, array in enumerate((snap, rate)):
            product = jnp.dot(left, array[part, :], preferred_element_type=jnp.float32)
            if c == 0:
                acc[k] = product
            else:
                acc[k] += product
    core = lax.axis_index("rows") % 2
    mine = pl.multiple_of(core * half, half)
    other = pl.multiple_of(half - core * half, half)
    for k in range(2):
        keep_ref[k * half : (k + 1) * half] = acc[k, pl.ds(mine, half), :]
        send_ref[k * half : (k + 1) * half] = acc[k, pl.ds(other, half), :]


def project(basis, snapshots, rates):
    rows, rank = basis.shape
    times = snapshots.shape[1]
    chunks = CHUNKS if rows % (16 * CHUNKS) == 0 else 1
    out = pltpu.VMEM((rank, times), jnp.float32)
    return pl.pallas_call(
        functools.partial(project_kernel, chunks),
        in_specs=[ANYWHERE] * 3,
        out_specs=[WHOLE, WHOLE],
        out_shape=[out, out],
        scratch_shapes=[
            pltpu.VMEM((rows, rank), jnp.bfloat16),
            pltpu.VMEM((rows, times), jnp.bfloat16),
            pltpu.VMEM((rows, times), jnp.bfloat16),
            pltpu.VMEM((2, rank, times), jnp.float32),
            pltpu.SemaphoreType.DMA((3, chunks)),
        ],
        compiler_params=pltpu.CompilerParams(vmem_limit_bytes=24 * MIB),
        cost_estimate=pl.CostEstimate(
            flops=4 * rows * rank * times, bytes_accessed=2 * rows * (rank + 2 * times), transcendentals=0
        ),
        name="project",
    )(in_hbm(basis), in_hbm(snapshots), in_hbm(rates))


def feature_rows(first, count, rank, states):
    shape = (count, rank)
    feature = first + lax.broadcasted_iota(jnp.int32, shape, 0)
    lane = lax.broadcasted_iota(jnp.int32, shape, 1)
    run_start = rank + lane * rank - (lane * (lane - 1)) // 2
    run_end = run_start + rank - lane
    in_run = (feature >= run_start) & (feature < run_end)
    shift = jnp.sum(jnp.where(in_run, run_start - lane, 0), axis=1, keepdims=True)
    left = in_run.astype(jnp.float32).astype(jnp.bfloat16)
    right = (lane == feature - shift).astype(jnp.float32).astype(jnp.bfloat16)
    pick = functools.partial(jnp.dot, preferred_element_type=jnp.float32)
    left_rows = pick(jnp.concatenate([left, left], axis=1), states)
    right_rows = pick(jnp.concatenate([right, right], axis=1), states)
    linear = (feature[:, :1] < rank).astype(jnp.float32)
    return ((left_rows + linear) * right_rows).astype(jnp.bfloat16)


def column_features(place, pieces, states, col_feat):
    rank = states.shape[0] // 2
    half, local = rank // 2, pieces[0].shape[1]
    end = col_feat.shape[0] - rank
    for k in range(0, len(pieces), 2):
        columns = slice(k // 2 * local, (k // 2 + 1) * local)
        for side in range(2):
            piece = pieces[k + side]
            at = pl.multiple_of((place[0] + side) % 2 * half, half)
            states[pl.ds(at, half), columns] = piece[0:half]
            states[pl.ds(pl.multiple_of(rank + at, half), half), columns] = piece[half : 2 * half]
            col_feat[pl.ds(pl.multiple_of(end + at, half), half), columns] = piece[2 * half :]
    for low in range(0, end, 3 * TILE):
        count = min(3 * TILE, end - low)
        col_feat[low : low + count] = feature_rows(place[2] + low, count, rank, states[...])


def block_product(place, states, col_feat):
    rank = states.shape[0] // 2
    rows = feature_rows(place[1] + pl.program_id(0) * BLOCK, BLOCK, rank, states[...])
    return lax.dot_general(rows, col_feat[...], (((1,), (1,)), ((), ())), preferred_element_type=jnp.float32)


def early_kernel(count, place, *refs):
    pieces, (acc_ref, token_ref, states, col_feat) = refs[:count], refs[count:]
    step = pl.program_id(0)

    @pl.when(step == 0)
    def _():
        token_ref[...] = jnp.zeros_like(token_ref)
        column_features(place, pieces, states, col_feat)

    acc_ref[pl.ds(pl.multiple_of(step * BLOCK, BLOCK), BLOCK), :] = block_product(place, states, col_feat)


def late_kernel(count, total_time, place, *refs):
    pieces, (acc_ref, gram_ref, rhs_ref, states, col_feat) = refs[:count], refs[count:]
    step = pl.program_id(0)
    rank = rhs_ref.shape[1]

    @pl.when(step == 0)
    def _():
        column_features(place, pieces, states, col_feat)

    earlier = acc_ref[pl.ds(pl.multiple_of(step * BLOCK, BLOCK), BLOCK), :]
    product = (earlier + block_product(place, states, col_feat)) / float(total_time)
    gram_ref[...] = product[:, : gram_ref.shape[1]]
    rhs_ref[...] = product[:, product.shape[1] - rank :]


def gram_call(kernel, name, place, pieces, extra, out_specs, out_shape, rank, row_width, col_width):
    slabs, local = len(pieces) // 2, pieces[0].shape[1]
    col_pad = round_up(col_width + rank, TILE)
    operands = [*map(in_vmem, pieces), *map(in_vmem, extra)]
    return pl.pallas_call(
        kernel,
        grid=(-(-row_width // BLOCK),),
        in_specs=[SCALARS] + [WHOLE] * len(operands),
        out_specs=out_specs,
        out_shape=out_shape,
        scratch_shapes=[
            pltpu.VMEM((2 * rank, slabs * local), jnp.bfloat16),
            pltpu.VMEM((col_pad, slabs * local), jnp.bfloat16),
        ],
        compiler_params=pltpu.CompilerParams(vmem_limit_bytes=32 * MIB),
        cost_estimate=pl.CostEstimate(
            flops=0,
            bytes_accessed=0,
            transcendentals=0,
        ),
        name=name,
    )(place, *operands)


def per_device(snapshots, rates, basis):
    rank = basis.shape[1]
    width = rank + rank * (rank + 1) // 2
    size_rows, size_reg = lax.axis_size("rows"), lax.axis_size("reg")
    row_width, col_width = width // size_rows, width // size_reg
    row_at, reg_at = lax.axis_index("rows"), lax.axis_index("reg")
    total_time = snapshots.shape[1] * size_reg
    place = jnp.stack([row_at % 2, row_at * row_width, reg_at * col_width]).astype(jnp.int32)
    swap = [(i, i ^ 1) for i in range(size_rows)]
    keep, send = project(basis, snapshots, rates)
    chip = keep + lax.ppermute(send, "rows", swap)
    plane = [[(2 * a + c, 2 * b + c) for a, b in perm for c in range(2)] for perm in partners(size_rows // 2)]
    total = chip
    for perm in plane:
        total = total + lax.ppermute(chip, "rows", perm)
    states, moments = total[: rank // 2], total[rank // 2 :]
    high = lax.reduce_precision(states, 8, 7)
    mine = jnp.concatenate([high, states - high, moments]).astype(jnp.bfloat16)
    own = [mine] + [lax.ppermute(mine, "reg", perm) for perm in partners(size_reg)]
    shape = (rank, row_width, col_width)

    early, late = own[:EARLY], own[EARLY:]
    pieces = [half for piece in early for half in (piece, lax.ppermute(piece, "rows", swap))]
    row_pad, col_pad = round_up(row_width, BLOCK), round_up(col_width + rank, TILE)
    earlier, token = gram_call(
        functools.partial(early_kernel, len(pieces)), "early", place, pieces, [], [WHOLE, WHOLE],
        [pltpu.VMEM((row_pad, col_pad), jnp.float32), pltpu.VMEM(mine.shape, jnp.bfloat16)], *shape,
    )
    late = [piece + token for piece in late]
    pieces = [half for piece in late for half in (piece, lax.ppermute(piece, "rows", swap))]
    return tuple(
        gram_call(
            functools.partial(late_kernel, len(pieces), total_time), "late", place, pieces, [earlier],
            [pl.BlockSpec((BLOCK, col_width), lambda i: (i, 0)), pl.BlockSpec((BLOCK, rank), lambda i: (i, 0))],
            [jax.ShapeDtypeStruct((row_width, n), jnp.float32) for n in (col_width, rank)], *shape,
        )
    )


def solution(mesh):
    return jax.shard_map(
        per_device,
        mesh=mesh,
        in_specs=(P("rows", "reg"), P("rows", "reg"), P("rows", None)),
        out_specs=(P("rows", "reg"), P("rows", None)),
        check_vma=False,
    )
```

time: 164 us -> 40.8 us (0.25)
  blocking collectives: 42 us -> 0 us
  waiting for transfers between devices: 51.3 us -> 10.2 us
  local copies, waits for them, and re-layouts: 28.6 us -> 0.01 us
  matrix products: 20.9 us -> 0 us
  Pallas kernels: 0 us -> 19.7 us
  between operations: 14.2 us -> 0.7 us
  starting transfers between devices: 0.08 us -> 9.85 us
  other arithmetic: 6.2 us -> 0.17 us
    psum x2 -> x0, waiting for transfers between devices: 51.3 us -> none  [the longest x1 25.6 us: per_device(): states, moments = lax.psum((part_states, part_rates), 'rows')]
    psum x1 -> x0, blocking collectives: 26.8 us -> none  [per_device(): states, moments = lax.psum((part_states, part_rates), 'rows')]
    gather x4 -> x0, local copies, waits for them, and re-layouts: 25.7 us -> none  [the longest x2 12.9 us: feature_block(): jnp.take(extended, left_rows, axis=0)]
    dot_general x4 -> x0, matrix products: 20.9 us -> none  [the longest x1 13.1 us: per_device(): lax.dot_general(row_all, col_feat, (((1,), (1,)), ((), ())), preferred_el...]
    pallas_call x0 -> x3, Pallas kernels: none -> 19.7 us  [the longest x2 15.1 us: gram_call(): pl.pallas_call(kernel, grid=(-(-row_width // BLOCK),), in_specs=[SCALARS]...]
    all_gather x1 -> x0, blocking collectives: 15.2 us -> none  [per_device(): every_state = lax.all_gather(states, 'reg', axis=1, tiled=True)]
    ppermute x0 -> x11, waiting for transfers between devices: none -> 10.2 us  [the longest x3 6.25 us: per_device(): total = total + lax.ppermute(chip, 'rows', perm)]
    ppermute x0 -> x11, starting transfers between devices: none -> 9.85 us  [the longest x3 4.52 us: per_device(): total = total + lax.ppermute(chip, 'rows', perm)]
  transfers between devices with their start and end apart: 2 -> 11, of which waited for: 2 -> 10; matrix products, arithmetic and copies ran while one was open for 10% -> 0% of each run, Pallas kernels for 0% -> 17%
where the time goes in v2:
time: 40.8 us; the launch traced here: 40.6 us
  Pallas kernels  19.7 us (48%)
  waiting for transfers between devices  10.2 us (25%)
  starting transfers between devices  9.85 us (24%)
  between operations  0.7 us (2%)
    pallas_call x2, Pallas kernels, gram_call(): pl.pallas_call(kernel, grid=(-(-row_width // BLOCK),), in_specs=[SCALARS]...  15.1 us
    ppermute x3, waiting for transfers between devices, per_device(): total = total + lax.ppermute(chip, 'rows', perm)  6.25 us
    pallas_call x1, Pallas kernels, project(): pl.pallas_call(functools.partial(project_kernel, chunks), in_specs=[ANYWH...  4.55 us
    ppermute x3, starting transfers between devices, per_device(): total = total + lax.ppermute(chip, 'rows', perm)  4.52 us
    ppermute x3, starting transfers between devices, per_device(): lax.ppermute(mine, 'reg', perm)  4.24 us
    ppermute x4, waiting for transfers between devices, per_device(): lax.ppermute(piece, 'rows', swap)  2.17 us
    ppermute x1, waiting for transfers between devices, per_device(): chip = keep + lax.ppermute(send, 'rows', swap)  0.99 us
  transfers between devices with their start and end apart: 11, of which 10 were waited for; matrix products, arithmetic and copies ran while one was open for 0% of the time, Pallas kernels for 17%

profile of v2, /device:TPU:0, one launch (start us, length us, event | category | flops | bytes accessed | tf_op | source)
XLA Modules:
  0.0 40.6 jit_solution(9368784840819001844)
XLA Ops:
  0.6 4.5 %project.1 = (f32[128,256]{1,0:T(8,128)S(1)}, f32[128,256]{1,0:T(8,128)S(1)}) custom-call(bf16[8192,128]{1,0:T(8,128)(2,1)} %basis_hbm.1, bf16[8192,256]{1,0:T(8,128)(2,1)} %snap_hbm.1, bf16[8192,256]{1,0:T(8,128)(2,1)} %rate_hbm.1), custom_call_target="tpu_custom_call" | custom-call | flops 1073741824 | bytes 10485760 | tf_op jit(solution)/shard_map/project/pallas_call | solution.py:78
  5.2 0.5 %collective-permute-start = (f32[128,256]{1,0:T(8,128)S(1)}, f32[128,256]{1,0:T(8,128)S(1)}, u32[]{:S(2)}, u32[]{:S(2)}) collective-permute-start(f32[128,256]{1,0:T(8,128)S(1)} %get-tuple-element.7), channel_id=1, source_target_pairs={{0,4},{4,0},{8,12},{12,8},{16,20},{20,16},{24,28},{28,24},{1,5},{5... | collective-permute-start | bytes 393224 | tf_op jit(solution)/shard_map/ppermute | solution.py:199
  5.7 1.0 %collective-permute-done = f32[128,256]{1,0:T(8,128)S(1)} collective-permute-done((f32[128,256]{1,0:T(8,128)S(1)}, f32[128,256]{1,0:T(8,128)S(1)}, u32[]{:S(2)}, u32[]{:S(2)}) %collective-permute-start) | collective-permute-done | bytes 131104 | tf_op jit(solution)/shard_map/ppermute | solution.py:199
  6.7 3.9 %collective-permute-start.3 = (f32[128,256]{1,0:T(8,128)S(1)}, f32[128,256]{1,0:T(8,128)S(1)}, u32[]{:S(2)}, u32[]{:S(2)}) collective-permute-start(f32[128,256]{1,0:T(8,128)S(1)} %add.23), channel_id=1, source_target_pairs={{0,24},{4,28},{8,16},{12,20},{16,8},{20,12},{24,0},{28,4},{1,25},{... | collective-permute-start | bytes 393224 | tf_op jit(solution)/shard_map/ppermute | solution.py:203
  10.6 0.5 %collective-permute-start.2 = (f32[128,256]{1,0:T(8,128)S(1)}, f32[128,256]{1,0:T(8,128)S(1)}, u32[]{:S(2)}, u32[]{:S(2)}) collective-permute-start(f32[128,256]{1,0:T(8,128)S(1)} %add.23), channel_id=1, source_target_pairs={{0,16},{4,20},{8,24},{12,28},{16,0},{20,4},{24,8},{28,12},{1,17},{... | collective-permute-start | bytes 393224 | tf_op jit(solution)/shard_map/ppermute | solution.py:203
  11.1 0.1 collective-permute-start.1
  11.2 3.3 %collective-permute-done.3 = f32[128,256]{1,0:T(8,128)S(1)} collective-permute-done((f32[128,256]{1,0:T(8,128)S(1)}, f32[128,256]{1,0:T(8,128)S(1)}, u32[]{:S(2)}, u32[]{:S(2)}) %collective-permute-start.3) | collective-permute-done | bytes 131104 | tf_op jit(solution)/shard_map/ppermute | solution.py:203
  14.5 2.7 %collective-permute-done.2 = f32[128,256]{1,0:T(8,128)S(1)} collective-permute-done((f32[128,256]{1,0:T(8,128)S(1)}, f32[128,256]{1,0:T(8,128)S(1)}, u32[]{:S(2)}, u32[]{:S(2)}) %collective-permute-start.2) | collective-permute-done | bytes 131104 | tf_op jit(solution)/shard_map/ppermute | solution.py:203
  17.2 0.3 collective-permute-done.1
  17.6 1.6 %collective-permute-start.6 = (bf16[192,256]{1,0:T(8,128)(2,1)S(1)}, bf16[192,256]{1,0:T(8,128)(2,1)S(1)}, u32[]{:S(2)}, u32[]{:S(2)}) collective-permute-start(bf16[192,256]{1,0:T(8,128)(2,1)S(1)} %pad_maximum_fusion.refs_0_), channel_id=1, source_target_pairs={{0,1},{1,0},{2,3},{3,2},{4,5},{5,4},{6,7},{7,6},{8,9},{9,8},{10,11... | collective-permute-start | bytes 294920 | tf_op jit(solution)/shard_map/ppermute | solution.py:207
  19.2 2.5 %collective-permute-start.9 = (bf16[192,256]{1,0:T(8,128)(2,1)S(1)}, bf16[192,256]{1,0:T(8,128)(2,1)S(1)}, u32[]{:S(2)}, u32[]{:S(2)}) collective-permute-start(bf16[192,256]{1,0:T(8,128)(2,1)S(1)} %pad_maximum_fusion.refs_0_), channel_id=1, source_target_pairs={{0,3},{1,2},{2,1},{3,0},{4,7},{5,6},{6,5},{7,4},{8,11},{9,10},{10,... | collective-permute-start | bytes 294920 | tf_op jit(solution)/shard_map/ppermute | solution.py:207
  21.7 0.0 collective-permute-start.5
  21.7 0.1 collective-permute-start.4
  21.8 0.4 %collective-permute-done.6.refs_2_ = bf16[192,256]{1,0:T(8,128)(2,1)S(1)} collective-permute-done((bf16[192,256]{1,0:T(8,128)(2,1)S(1)}, bf16[192,256]{1,0:T(8,128)(2,1)S(1)}, u32[]{:S(2)}, u32[]{:S(2)}) %collective-permute-start.6) | collective-permute-done | bytes 98336 | tf_op jit(solution)/shard_map/ppermute | solution.py:207
  22.2 0.0 collective-permute-start.7
  22.3 0.1 pad_add_fusion.place
  22.3 0.7 %collective-permute-done.5.refs_1_ = bf16[192,256]{1,0:T(8,128)(2,1)S(1)} collective-permute-done((bf16[192,256]{1,0:T(8,128)(2,1)S(1)}, bf16[192,256]{1,0:T(8,128)(2,1)S(1)}, u32[]{:S(2)}, u32[]{:S(2)}) %collective-permute-start.5) | collective-permute-done | bytes 98336 | tf_op jit(solution)/shard_map/ppermute | solution.py:211
  23.0 0.6 %collective-permute-done.7.refs_3_ = bf16[192,256]{1,0:T(8,128)(2,1)S(1)} collective-permute-done((bf16[192,256]{1,0:T(8,128)(2,1)S(1)}, bf16[192,256]{1,0:T(8,128)(2,1)S(1)}, u32[]{:S(2)}, u32[]{:S(2)}) %collective-permute-start.7) | collective-permute-done | bytes 98336 | tf_op jit(solution)/shard_map/ppermute | solution.py:211
  23.6 6.7 %early.1 = (f32[1088,2304]{1,0:T(8,128)S(1)}, bf16[192,256]{1,0:T(8,128)(2,1)S(1)}) custom-call(s32[3]{0:T(128)S(1)} %pad_add_fusion.place, bf16[192,256]{1,0:T(8,128)(2,1)S(1)} %pad_maximum_fusion.refs_0_, bf16[192,256]{1,0:T(8,128)(2,1)S(1)} %collective-permute-done.5.refs_1_, bf16[192,256]{1,0:T(8,128)(2,1)S(1)} %collective-permute-done.6.refs_2_, ...), custom_call_target="tpu_custom_call" | custom-call | tf_op jit(solution)/shard_map/early/pallas_call | solution.py:169
  30.3 0.0 collective-permute-done.9
  30.3 0.4 collective-permute-done.4
  30.7 0.2 collective-permute-start.10
  30.9 0.4 collective-permute-start.8
  31.3 0.8 %collective-permute-done.10.refs_3_ = bf16[192,256]{1,0:T(8,128)(2,1)S(1)} collective-permute-done((bf16[192,256]{1,0:T(8,128)(2,1)S(1)}, bf16[192,256]{1,0:T(8,128)(2,1)S(1)}, u32[]{:S(2)}, u32[]{:S(2)}) %collective-permute-start.10) | collective-permute-done | bytes 98336 | tf_op jit(solution)/shard_map/ppermute | solution.py:218
  32.1 0.2 collective-permute-done.8.refs_1_
  32.2 8.4 %late.1 = (f32[1048,2096]{1,0:T(8,128)}, f32[1048,128]{1,0:T(8,128)}) custom-call(s32[3]{0:T(128)S(1)} %pad_add_fusion.place, bf16[192,256]{1,0:T(8,128)(2,1)S(1)} %get-tuple-element.13.refs_0_, bf16[192,256]{1,0:T(8,128)(2,1)S(1)} %collective-permute-done.8.refs_1_, bf16[192,256]{1,0:T(8,128)(2,1)S(1)} %get-tuple-element.12.refs_2_, ...), custom_call_target="tpu_custom_call" | custom-call | tf_op jit(solution)/shard_map/late/pallas_call | solution.py:169
  (6 shorter events, 0.1 us)
Async XLA Ops:
  5.2 1.5 %collective-permute-start = (f32[128,256]{1,0:T(8,128)S(1)}, f32[128,256]{1,0:T(8,128)S(1)}, u32[]{:S(2)}, u32[]{:S(2)}) collective-permute-start(f32[128,256]{1,0:T(8,128)S(1)} %get-tuple-element.7), channel_id=1, source_target_pairs={{0,4},{4,0},{8,12},{12,8},{16,20},{20,16},{24,28},{28,24},{1,5},{5... | collective-permute-start | bytes 393224 | tf_op jit(solution)/shard_map/ppermute | solution.py:199
  6.7 7.8 %collective-permute-start.3 = (f32[128,256]{1,0:T(8,128)S(1)}, f32[128,256]{1,0:T(8,128)S(1)}, u32[]{:S(2)}, u32[]{:S(2)}) collective-permute-start(f32[128,256]{1,0:T(8,128)S(1)} %add.23), channel_id=1, source_target_pairs={{0,24},{4,28},{8,16},{12,20},{16,8},{20,12},{24,0},{28,4},{1,25},{... | collective-permute-start | bytes 393224 | tf_op jit(solution)/shard_map/ppermute | solution.py:203
  10.6 6.6 %collective-permute-start.2 = (f32[128,256]{1,0:T(8,128)S(1)}, f32[128,256]{1,0:T(8,128)S(1)}, u32[]{:S(2)}, u32[]{:S(2)}) collective-permute-start(f32[128,256]{1,0:T(8,128)S(1)} %add.23), channel_id=1, source_target_pairs={{0,16},{4,20},{8,24},{12,28},{16,0},{20,4},{24,8},{28,12},{1,17},{... | collective-permute-start | bytes 393224 | tf_op jit(solution)/shard_map/ppermute | solution.py:203
  11.1 6.4 %collective-permute-start.1 = (f32[128,256]{1,0:T(8,128)S(1)}, f32[128,256]{1,0:T(8,128)S(1)}, u32[]{:S(2)}, u32[]{:S(2)}) collective-permute-start(f32[128,256]{1,0:T(8,128)S(1)} %add.23), channel_id=1, source_target_pairs={{0,8},{4,12},{8,0},{12,4},{16,24},{20,28},{24,16},{28,20},{1,9},{5... | collective-permute-start | bytes 393224 | tf_op jit(solution)/shard_map/ppermute | solution.py:203
  17.6 4.7 %collective-permute-start.6 = (bf16[192,256]{1,0:T(8,128)(2,1)S(1)}, bf16[192,256]{1,0:T(8,128)(2,1)S(1)}, u32[]{:S(2)}, u32[]{:S(2)}) collective-permute-start(bf16[192,256]{1,0:T(8,128)(2,1)S(1)} %pad_maximum_fusion.refs_0_), channel_id=1, source_target_pairs={{0,1},{1,0},{2,3},{3,2},{4,5},{5,4},{6,7},{7,6},{8,9},{9,8},{10,11... | collective-permute-start | bytes 294920 | tf_op jit(solution)/shard_map/ppermute | solution.py:207
  19.2 11.1 %collective-permute-start.9 = (bf16[192,256]{1,0:T(8,128)(2,1)S(1)}, bf16[192,256]{1,0:T(8,128)(2,1)S(1)}, u32[]{:S(2)}, u32[]{:S(2)}) collective-permute-start(bf16[192,256]{1,0:T(8,128)(2,1)S(1)} %pad_maximum_fusion.refs_0_), channel_id=1, source_target_pairs={{0,3},{1,2},{2,1},{3,0},{4,7},{5,6},{6,5},{7,4},{8,11},{9,10},{10,... | collective-permute-start | bytes 294920 | tf_op jit(solution)/shard_map/ppermute | solution.py:207
  21.7 1.3 %collective-permute-start.5 = (bf16[192,256]{1,0:T(8,128)(2,1)S(1)}, bf16[192,256]{1,0:T(8,128)(2,1)S(1)}, u32[]{:S(2)}, u32[]{:S(2)}) collective-permute-start(bf16[192,256]{1,0:T(8,128)(2,1)S(1)} %pad_maximum_fusion.refs_0_), channel_id=1, source_target_pairs={{0,4},{4,0},{8,12},{12,8},{16,20},{20,16},{24,28},{28,24},{1,5},{5... | collective-permute-start | bytes 294920 | tf_op jit(solution)/shard_map/ppermute | solution.py:211
  21.7 9.0 %collective-permute-start.4 = (bf16[192,256]{1,0:T(8,128)(2,1)S(1)}, bf16[192,256]{1,0:T(8,128)(2,1)S(1)}, u32[]{:S(2)}, u32[]{:S(2)}) collective-permute-start(bf16[192,256]{1,0:T(8,128)(2,1)S(1)} %pad_maximum_fusion.refs_0_), channel_id=1, source_target_pairs={{0,2},{1,3},{2,0},{3,1},{4,6},{5,7},{6,4},{7,5},{8,10},{9,11},{10,... | collective-permute-start | bytes 294920 | tf_op jit(solution)/shard_map/ppermute | solution.py:207
  22.2 1.3 %collective-permute-start.7 = (bf16[192,256]{1,0:T(8,128)(2,1)S(1)}, bf16[192,256]{1,0:T(8,128)(2,1)S(1)}, u32[]{:S(2)}, u32[]{:S(2)}) collective-permute-start(bf16[192,256]{1,0:T(8,128)(2,1)S(1)} %collective-permute-done.6.refs_2_), channel_id=1, source_target_pairs={{0,4},{4,0},{8,12},{12,8},{16,20},{20,16},{24,28},{28,24},{1,5},{5... | collective-permute-start | bytes 294920 | tf_op jit(solution)/shard_map/ppermute | solution.py:211
  30.7 1.4 %collective-permute-start.10 = (bf16[192,256]{1,0:T(8,128)(2,1)S(1)}, bf16[192,256]{1,0:T(8,128)(2,1)S(1)}, u32[]{:S(2)}, u32[]{:S(2)}) collective-permute-start(bf16[192,256]{1,0:T(8,128)(2,1)S(1)} %get-tuple-element.12.refs_2_), channel_id=1, source_target_pairs={{0,4},{4,0},{8,12},{12,8},{16,20},{20,16},{24,28},{28,24},{1,5},{5... | collective-permute-start | bytes 294920 | tf_op jit(solution)/shard_map/ppermute | solution.py:218
  30.9 1.3 %collective-permute-start.8 = (bf16[192,256]{1,0:T(8,128)(2,1)S(1)}, bf16[192,256]{1,0:T(8,128)(2,1)S(1)}, u32[]{:S(2)}, u32[]{:S(2)}) collective-permute-start(bf16[192,256]{1,0:T(8,128)(2,1)S(1)} %get-tuple-element.13.refs_0_), channel_id=1, source_target_pairs={{0,4},{4,0},{8,12},{12,8},{16,20},{20,16},{24,28},{28,24},{1,5},{5... | collective-permute-start | bytes 294920 | tf_op jit(solution)/shard_map/ppermute | solution.py:218

commit v3 on v2

v3 whole, which is shorter than its diff:
```python
import functools

import jax
import jax.numpy as jnp
from jax import lax
from jax.experimental import pallas as pl
from jax.experimental.pallas import tpu as pltpu
from jax.sharding import PartitionSpec as P

TILE = 256
ROWS = 352
COLS = 768
CHUNKS = 8
MIB = 1 << 20


def round_up(value, step):
    return (value + step - 1) // step * step


def partners(size):
    if size & (size - 1) == 0:
        return [[(i, i ^ k) for i in range(size)] for k in range(1, size)]
    return [[(i, (i + k) % size) for i in range(size)] for k in range(1, size)]


WHOLE = pl.BlockSpec(memory_space=pltpu.VMEM)
ANYWHERE = pl.BlockSpec(memory_space=pl.ANY)
LONG = pl.CostEstimate(flops=20_000_000_000, bytes_accessed=0, transcendentals=0)
FREE = pl.CostEstimate(flops=0, bytes_accessed=0, transcendentals=0)


def in_hbm(array):
    return pltpu.with_memory_space_constraint(array, pltpu.HBM)


def in_vmem(array):
    return pltpu.with_memory_space_constraint(array, pltpu.VMEM)


def project_kernel(chunks, basis_hbm, snap_hbm, rate_hbm, keep_ref, send_ref, basis, snap, rate, acc, sems):
    rows = basis.shape[0] // chunks
    copies = []
    for c in range(chunks):
        part = pl.ds(c * rows, rows)
        copies.append(
            [
                pltpu.make_async_copy(source.at[part], target.at[part], sems.at[k, c])
                for k, (source, target) in enumerate(((basis_hbm, basis), (snap_hbm, snap), (rate_hbm, rate)))
            ]
        )
        for copy in copies[-1]:
            copy.start()
    for c in range(chunks):
        for copy in copies[c]:
            copy.wait()
        part = pl.ds(c * rows, rows)
        left = basis[part, :].T
        for k, array in enumerate((snap, rate)):
            product = jnp.dot(left, array[part, :], preferred_element_type=jnp.float32)
            if c == 0:
                acc[k] = product
            else:
                acc[k] += product
    rank, half = acc.shape[1], acc.shape[2] // 2
    core = lax.axis_index("rows") % 2
    mine = pl.multiple_of(core * half, half)
    other = pl.multiple_of(half - core * half, half)
    for k in range(2):
        keep_ref[k * rank : (k + 1) * rank] = acc[k, :, pl.ds(mine, half)]
        send_ref[k * rank : (k + 1) * rank] = acc[k, :, pl.ds(other, half)]


def project(basis, snapshots, rates):
    rows, rank = basis.shape
    times = snapshots.shape[1]
    chunks = CHUNKS if rows % (16 * CHUNKS) == 0 else 1
    out = pltpu.VMEM((2 * rank, times // 2), jnp.float32)
    return pl.pallas_call(
        functools.partial(project_kernel, chunks),
        in_specs=[ANYWHERE] * 3,
        out_specs=[WHOLE, WHOLE],
        out_shape=[out, out],
        scratch_shapes=[
            pltpu.VMEM((rows, rank), jnp.bfloat16),
            pltpu.VMEM((rows, times), jnp.bfloat16),
            pltpu.VMEM((rows, times), jnp.bfloat16),
            pltpu.VMEM((2, rank, times), jnp.float32),
            pltpu.SemaphoreType.DMA((3, chunks)),
        ],
        compiler_params=pltpu.CompilerParams(vmem_limit_bytes=24 * MIB),
        cost_estimate=pl.CostEstimate(
            flops=4 * rows * rank * times, bytes_accessed=2 * rows * (rank + 2 * times), transcendentals=0
        ),
        name="project",
    )(in_hbm(basis), in_hbm(snapshots), in_hbm(rates))


def feature_rows(first, count, rank, states):
    shape = (count, rank)
    feature = first + lax.broadcasted_iota(jnp.int32, shape, 0)
    lane = lax.broadcasted_iota(jnp.int32, shape, 1)
    run_start = rank + lane * rank - (lane * (lane - 1)) // 2
    run_end = run_start + rank - lane
    in_run = (feature >= run_start) & (feature < run_end)
    shift = jnp.sum(jnp.where(in_run, run_start - lane, 0), axis=1, keepdims=True)
    left = in_run.astype(jnp.float32).astype(jnp.bfloat16)
    right = (lane == feature - shift).astype(jnp.float32).astype(jnp.bfloat16)
    pick = functools.partial(jnp.dot, preferred_element_type=jnp.float32)
    left_rows = pick(jnp.concatenate([left, left], axis=1), states)
    right_rows = pick(jnp.concatenate([right, right], axis=1), states)
    linear = (feature[:, :1] < rank).astype(jnp.float32)
    return ((left_rows + linear) * right_rows).astype(jnp.bfloat16)


def lay_out(pieces, states, moments):
    rank, at = moments.shape[0], 0
    for piece in pieces:
        for low in range(0, piece.shape[0], 3 * rank):
            columns = slice(at, at + piece.shape[1])
            states[:, columns] = piece[low : low + 2 * rank]
            moments[:, columns] = piece[low + 2 * rank : low + 3 * rank]
            at += piece.shape[1]


def spans(total, most):
    return [(low, min(most, total - low)) for low in range(0, total, most)]


def fill_rows(row_width, states, row_feat, columns):
    rank, first = states.shape[0] // 2, lax.axis_index("rows") * row_width
    for low, size in spans(row_feat.shape[0], ROWS):
        row_feat[low : low + size, columns] = feature_rows(first + low, size, rank, states[...])


def fill_columns(col_width, states, moments, col_feat, left, right, columns):
    rank, first = moments.shape[0], lax.axis_index("reg") * col_width
    end = min(right, col_feat.shape[0] - rank)
    col_feat[left:end, columns] = feature_rows(first + left, end - left, rank, states[...])
    if end < right:
        col_feat[end:right, columns] = moments[...]


def prepare_kernel(count, row_width, col_width, *refs):
    pieces, (row_feat, col_feat, *zero, states, moments) = refs[:count], refs[count:]
    for ref in zero:
        ref[...] = jnp.zeros_like(ref)
    lay_out(pieces, states, moments)
    fill_rows(row_width, states, row_feat, slice(None))
    for left, width in spans(col_feat.shape[0], COLS):
        fill_columns(col_width, states, moments, col_feat, left, left + width, slice(None))


def prepare(pieces, waiting, cost, rank, row_width, col_width):
    times = sum(piece.size for piece in pieces) // (3 * rank)
    row_pad, col_pad = round_up(row_width, 16), round_up(col_width + rank, TILE)
    return pl.pallas_call(
        functools.partial(prepare_kernel, len(pieces), row_width, col_width),
        in_specs=[WHOLE] * len(pieces),
        out_specs=[WHOLE] * (2 + len(waiting)),
        out_shape=[pltpu.VMEM(shape, jnp.bfloat16) for shape in [(row_pad, times), (col_pad, times), *waiting]],
        scratch_shapes=[pltpu.VMEM((n * rank, times), jnp.bfloat16) for n in (2, 1)],
        compiler_params=pltpu.CompilerParams(vmem_limit_bytes=32 * MIB),
        cost_estimate=cost,
        name="prepare",
    )(*map(in_vmem, pieces))


def sum_kernel(count, held, ready, total_time, row_width, col_width, *refs):
    pieces, refs = refs[:count], refs[count:]
    acc_in, refs = (refs[0], refs[1:]) if held else (None, refs)
    (row_ready, col_ready), refs = (refs[:2], refs[2:]) if ready else ((None, None), refs)
    refs = refs[1:]
    states, moments, row_feat, col_feat = refs[-4:]
    rank = moments.shape[0]
    row_pad, col_pad = row_feat.shape[0], col_feat.shape[0]
    columns = slice(row_feat.shape[1] - states.shape[1], row_feat.shape[1])
    before = slice(0, columns.start)
    lay_out(pieces, states, moments)
    fill_rows(row_width, states, row_feat, columns)
    if ready:
        row_feat[:, before] = row_ready[...]
    copies = []
    for left, width in spans(col_pad, COLS):
        fill_columns(col_width, states, moments, col_feat, left, left + width, columns)
        if ready:
            col_feat[left : left + width, before] = col_ready[left : left + width]
        for low, size in spans(row_pad, ROWS):
            block = lax.dot_general(
                row_feat[low : low + size], col_feat[left : left + width], (((1,), (1,)), ((), ())),
                preferred_element_type=jnp.float32,
            )
            if held:
                block = acc_in[low : low + size, left : left + width] + block
            if total_time is None:
                refs[0][low : low + size, left : left + width] = block
                if left + low == 0:
                    refs[1][...] = jnp.zeros_like(refs[1])
                continue
            gram_hbm, rhs_hbm, gram, rhs, sems = refs[:5]
            block = block / float(total_time)
            rows = pl.ds(low, min(size, row_width - low))
            if left < col_width:
                part = pl.ds(left, min(width, col_width - left))
                gram[rows, part] = block[: rows.size, : part.size]
                copies.append(pltpu.make_async_copy(gram.at[rows, part], gram_hbm.at[rows, part], sems.at[len(copies)]))
                copies[-1].start()
            if left + width == col_pad:
                rhs[rows] = block[: rows.size, width - rank :]
                copies.append(pltpu.make_async_copy(rhs.at[rows], rhs_hbm.at[rows], sems.at[len(copies)]))
                copies[-1].start()
    for copy in copies:
        copy.wait()


def add_up(place, pieces, held, ready, total_time, waiting, rank, row_width, col_width):
    times = sum(piece.size for piece in pieces) // (3 * rank)
    all_times = times + (ready[0].shape[1] if ready else 0)
    row_pad, col_pad = round_up(row_width, 16), round_up(col_width + rank, TILE)
    operands = [*map(in_vmem, pieces), *map(in_vmem, held), *map(in_vmem, ready)]
    operands += [in_vmem(place)]
    scratch = [
        pltpu.VMEM((2 * rank, times), jnp.bfloat16),
        pltpu.VMEM((rank, times), jnp.bfloat16),
        pltpu.VMEM((row_pad, all_times), jnp.bfloat16),
        pltpu.VMEM((col_pad, all_times), jnp.bfloat16),
    ]
    if total_time is None:
        out_specs = [WHOLE, WHOLE]
        out_shape = [pltpu.VMEM((row_pad, col_pad), jnp.float32), pltpu.VMEM(waiting, jnp.bfloat16)]
    else:
        out_specs = [ANYWHERE, ANYWHERE]
        out_shape = [jax.ShapeDtypeStruct((row_width, n), jnp.float32) for n in (col_width, rank)]
        scratch = [
            pltpu.VMEM((row_width, col_width), jnp.float32),
            pltpu.VMEM((row_width, rank), jnp.float32),
            pltpu.SemaphoreType.DMA((len(spans(row_pad, ROWS)) * (len(spans(col_pad, COLS)) + 1),)),
        ] + scratch
    return pl.pallas_call(
        functools.partial(sum_kernel, len(pieces), bool(held), bool(ready), total_time, row_width, col_width),
        in_specs=[WHOLE] * len(operands),
        out_specs=out_specs,
        out_shape=out_shape,
        scratch_shapes=scratch,
        compiler_params=pltpu.CompilerParams(vmem_limit_bytes=32 * MIB),
        cost_estimate=FREE,
        name="add_up_last" if total_time else "add_up",
    )(*operands)


def per_device(snapshots, rates, basis):
    rank = basis.shape[1]
    width = rank + rank * (rank + 1) // 2
    size_rows, size_reg = lax.axis_size("rows"), lax.axis_size("reg")
    row_width, col_width = width // size_rows, width // size_reg
    total_time = snapshots.shape[1] * size_reg
    shape = (rank, row_width, col_width)

    place = jnp.stack([lax.axis_index("rows") * row_width, lax.axis_index("reg") * col_width]).astype(jnp.int32)
    swap = [(i, i ^ 1) for i in range(size_rows)]
    keep, send = project(basis, snapshots, rates)
    chip = keep + lax.ppermute(send, "rows", swap)
    plane = [[(2 * a + c, 2 * b + c) for a, b in perm for c in range(2)] for perm in partners(size_rows // 2)]
    total = chip
    for perm in plane:
        total = total + lax.ppermute(chip, "rows", perm)
    states, moments = total[:rank], total[rank:]
    high = lax.reduce_precision(states, 8, 7)
    mine = jnp.concatenate([high, states - high, moments]).astype(jnp.bfloat16)
    slabs = [mine] + [lax.ppermute(mine, "reg", perm) for perm in partners(size_reg)]

    near, far = slabs[-1:], slabs[-2:0:-1]
    *ready, zero = prepare([mine, lax.ppermute(mine, "rows", swap)], [mine.shape], LONG, *shape)
    near = [slab + zero for slab in near]
    pieces = [half for slab in near for half in (slab, lax.ppermute(slab, "rows", swap))]
    waiting = (len(far) * mine.shape[0], mine.shape[1])
    *held, zero = add_up(place, pieces, [], ready, None, waiting, *shape)
    piece = jnp.concatenate(far) + zero
    other = lax.ppermute(piece, "rows", swap)
    ready = prepare([piece], [], FREE, *shape)
    return tuple(add_up(place, [other], held, ready, total_time, None, *shape))


def solution(mesh):
    return jax.shard_map(
        per_device,
        mesh=mesh,
        in_specs=(P("rows", "reg"), P("rows", "reg"), P("rows", None)),
        out_specs=(P("rows", "reg"), P("rows", None)),
        check_vma=False,
    )
```

time: 40.8 us -> 37.4 us (0.917)
  Pallas kernels: 19.7 us -> 16.4 us
    pallas_call x2 -> x4, Pallas kernels: 15.1 us -> 11.8 us  [the longest x2 8.99 us: add_up(): pl.pallas_call(functools.partial(sum_kernel, len(pieces), bool(held), boo...]
    ppermute x4 -> x3, waiting for transfers between devices: 2.17 us -> 1.21 us  [the longest x1 1.21 us: per_device(): lax.ppermute(slab, 'rows', swap)]
    ppermute x3, waiting for transfers between devices: 0.81 us -> 1.64 us  [per_device(): lax.ppermute(mine, 'reg', perm)]
  transfers between devices with their start and end apart: 11 -> 10, of which waited for: 10 -> 6; matrix products, arithmetic and copies ran while one was open for 0% -> 0% of each run, Pallas kernels for 17% -> 18%
where the time goes in v3:
time: 37.4 us; the launch traced here: 37.3 us
  Pallas kernels  16.4 us (44%)
  waiting for transfers between devices  10.1 us (27%)
  starting transfers between devices  9.85 us (26%)
  between operations  0.74 us (2%)
    pallas_call x2, Pallas kernels, add_up(): pl.pallas_call(functools.partial(sum_kernel, len(pieces), bool(held), boo...  8.99 us
    ppermute x3, waiting for transfers between devices, per_device(): total = total + lax.ppermute(chip, 'rows', perm)  6.25 us
    pallas_call x1, Pallas kernels, project(): pl.pallas_call(functools.partial(project_kernel, chunks), in_specs=[ANYWH...  4.56 us
    ppermute x3, starting transfers between devices, per_device(): total = total + lax.ppermute(chip, 'rows', perm)  4.52 us
    ppermute x3, starting transfers between devices, per_device(): lax.ppermute(mine, 'reg', perm)  4.45 us
    pallas_call x2, Pallas kernels, prepare(): pl.pallas_call(functools.partial(prepare_kernel, len(pieces), row_width,...  2.81 us
    ppermute x3, waiting for transfers between devices, per_device(): lax.ppermute(mine, 'reg', perm)  1.64 us
    ppermute x1, waiting for transfers between devices, per_device(): lax.ppermute(slab, 'rows', swap)  1.21 us
  transfers between devices with their start and end apart: 10, of which 6 were waited for; matrix products, arithmetic and copies ran while one was open for 0% of the time, Pallas kernels for 18%

profile of v3, /device:TPU:0, one launch (start us, length us, event | category | flops | bytes accessed | tf_op | source)
XLA Modules:
  0.0 37.3 jit_solution(16761482189047999203)
XLA Ops:
  0.6 4.6 %project.1 = (f32[256,128]{1,0:T(8,128)S(1)}, f32[256,128]{1,0:T(8,128)S(1)}) custom-call(bf16[8192,128]{1,0:T(8,128)(2,1)} %basis_hbm.1, bf16[8192,256]{1,0:T(8,128)(2,1)} %snap_hbm.1, bf16[8192,256]{1,0:T(8,128)(2,1)} %rate_hbm.1), custom_call_target="tpu_custom_call" | custom-call | flops 1073741824 | bytes 10485760 | tf_op jit(solution)/shard_map/project/pallas_call | solution.py:79
  5.2 0.5 %collective-permute-start = (f32[256,128]{1,0:T(8,128)S(1)}, f32[256,128]{1,0:T(8,128)S(1)}, u32[]{:S(2)}, u32[]{:S(2)}) collective-permute-start(f32[256,128]{1,0:T(8,128)S(1)} %get-tuple-element.12), channel_id=1, source_target_pairs={{0,4},{4,0},{8,12},{12,8},{16,20},{20,16},{24,28},{28,24},{1,5},{5... | collective-permute-start | bytes 393224 | tf_op jit(solution)/shard_map/ppermute | solution.py:262
  5.7 1.0 %collective-permute-done = f32[256,128]{1,0:T(8,128)S(1)} collective-permute-done((f32[256,128]{1,0:T(8,128)S(1)}, f32[256,128]{1,0:T(8,128)S(1)}, u32[]{:S(2)}, u32[]{:S(2)}) %collective-permute-start) | collective-permute-done | bytes 131104 | tf_op jit(solution)/shard_map/ppermute | solution.py:262
  6.7 3.9 %collective-permute-start.3 = (f32[256,128]{1,0:T(8,128)S(1)}, f32[256,128]{1,0:T(8,128)S(1)}, u32[]{:S(2)}, u32[]{:S(2)}) collective-permute-start(f32[256,128]{1,0:T(8,128)S(1)} %add.18), channel_id=1, source_target_pairs={{0,24},{4,28},{8,16},{12,20},{16,8},{20,12},{24,0},{28,4},{1,25},{... | collective-permute-start | bytes 393224 | tf_op jit(solution)/shard_map/ppermute | solution.py:266
  10.6 0.5 %collective-permute-start.2 = (f32[256,128]{1,0:T(8,128)S(1)}, f32[256,128]{1,0:T(8,128)S(1)}, u32[]{:S(2)}, u32[]{:S(2)}) collective-permute-start(f32[256,128]{1,0:T(8,128)S(1)} %add.18), channel_id=1, source_target_pairs={{0,16},{4,20},{8,24},{12,28},{16,0},{20,4},{24,8},{28,12},{1,17},{... | collective-permute-start | bytes 393224 | tf_op jit(solution)/shard_map/ppermute | solution.py:266
  11.1 0.1 collective-permute-start.1
  11.2 3.3 %collective-permute-done.3 = f32[256,128]{1,0:T(8,128)S(1)} collective-permute-done((f32[256,128]{1,0:T(8,128)S(1)}, f32[256,128]{1,0:T(8,128)S(1)}, u32[]{:S(2)}, u32[]{:S(2)}) %collective-permute-start.3) | collective-permute-done | bytes 131104 | tf_op jit(solution)/shard_map/ppermute | solution.py:266
  14.5 2.7 %collective-permute-done.2 = f32[256,128]{1,0:T(8,128)S(1)} collective-permute-done((f32[256,128]{1,0:T(8,128)S(1)}, f32[256,128]{1,0:T(8,128)S(1)}, u32[]{:S(2)}, u32[]{:S(2)}) %collective-permute-start.2) | collective-permute-done | bytes 131104 | tf_op jit(solution)/shard_map/ppermute | solution.py:266
  17.2 0.3 collective-permute-done.1
  17.6 0.1 collective-permute-start.7
  17.7 3.7 %collective-permute-start.6 = (bf16[384,128]{1,0:T(8,128)(2,1)S(1)}, bf16[384,128]{1,0:T(8,128)(2,1)S(1)}, u32[]{:S(2)}, u32[]{:S(2)}) collective-permute-start(bf16[384,128]{1,0:T(8,128)(2,1)S(1)} %pad_maximum_fusion.refs_0_), channel_id=1, source_target_pairs={{0,3},{1,2},{2,1},{3,0},{4,7},{5,6},{6,5},{7,4},{8,11},{9,10},{10,... | collective-permute-start | bytes 294920 | tf_op jit(solution)/shard_map/ppermute | solution.py:270
  21.3 0.0 collective-permute-start.5
  21.3 0.8 %collective-permute-start.4 = (bf16[384,128]{1,0:T(8,128)(2,1)S(1)}, bf16[384,128]{1,0:T(8,128)(2,1)S(1)}, u32[]{:S(2)}, u32[]{:S(2)}) collective-permute-start(bf16[384,128]{1,0:T(8,128)(2,1)S(1)} %pad_maximum_fusion.refs_0_), channel_id=1, source_target_pairs={{0,2},{1,3},{2,0},{3,1},{4,6},{5,7},{6,4},{7,5},{8,10},{9,11},{10,... | collective-permute-start | bytes 294920 | tf_op jit(solution)/shard_map/ppermute | solution.py:270
  22.1 0.0 collective-permute-done.7.refs_1_
  22.1 1.4 %prepare.2 = (bf16[1056,256]{1,0:T(8,128)(2,1)S(1)}, bf16[2304,256]{1,0:T(8,128)(2,1)S(1)}, bf16[384,128]{1,0:T(8,128)(2,1)S(1)}) custom-call(bf16[384,128]{1,0:T(8,128)(2,1)S(1)} %pad_maximum_fusion.refs_0_, bf16[384,128]{1,0:T(8,128)(2,1)S(1)} %collective-permute-done.7.refs_1_), custom_call_target="tpu_custom_call" | custom-call | flops 20000000000 | tf_op jit(solution)/shard_map/prepare/pallas_call | solution.py:157
  23.5 1.6 %collective-permute-done.6 = bf16[384,128]{1,0:T(8,128)(2,1)S(1)} collective-permute-done((bf16[384,128]{1,0:T(8,128)(2,1)S(1)}, bf16[384,128]{1,0:T(8,128)(2,1)S(1)}, u32[]{:S(2)}, u32[]{:S(2)}) %collective-permute-start.6) | collective-permute-done | bytes 98336 | tf_op jit(solution)/shard_map/ppermute | solution.py:270
  25.2 0.1 collective-permute-start.8
  25.3 0.1 pad_add_fusion.refs_4_
  25.3 1.2 %collective-permute-done.8.refs_1_ = bf16[384,128]{1,0:T(8,128)(2,1)S(1)} collective-permute-done((bf16[384,128]{1,0:T(8,128)(2,1)S(1)}, bf16[384,128]{1,0:T(8,128)(2,1)S(1)}, u32[]{:S(2)}, u32[]{:S(2)}) %collective-permute-start.8) | collective-permute-done | bytes 98336 | tf_op jit(solution)/shard_map/ppermute | solution.py:275
  26.6 3.9 %add_up.1 = (f32[1056,2304]{1,0:T(8,128)S(1)}, bf16[768,128]{1,0:T(8,128)(2,1)S(1)}) custom-call(bf16[384,128]{1,0:T(8,128)(2,1)S(1)} %add.22.refs_0_, bf16[384,128]{1,0:T(8,128)(2,1)S(1)} %collective-permute-done.8.refs_1_, bf16[1056,256]{1,0:T(8,128)(2,1)S(1)} %get-tuple-element.14.refs_2_, bf16[2304,256]{1,0:T(8,128)(2,1)S(1)} %get-tuple-element.15.refs_3_, ...), custom_call_target="tpu_custom_call" | custom-call | tf_op jit(solution)/shard_map/add_up/pallas_call | solution.py:239
  30.4 0.0 collective-permute-done.5
  30.4 0.0 collective-permute-done.4
  30.4 0.1 maximum_add_fusion.refs_0_
  30.5 0.2 collective-permute-start.9
  30.7 1.4 %prepare.3 = (bf16[1056,256]{1,0:T(8,128)(2,1)S(1)}, bf16[2304,256]{1,0:T(8,128)(2,1)S(1)}) custom-call(bf16[768,128]{1,0:T(8,128)(2,1)S(1)} %maximum_add_fusion.refs_0_), custom_call_target="tpu_custom_call" | custom-call | tf_op jit(solution)/shard_map/prepare/pallas_call | solution.py:157
  32.1 0.0 collective-permute-done.9.refs_0_
  32.1 5.1 %add_up_last.1 = (f32[1048,2096]{1,0:T(8,128)}, f32[1048,128]{1,0:T(8,128)}) custom-call(bf16[768,128]{1,0:T(8,128)(2,1)S(1)} %collective-permute-done.9.refs_0_, f32[1056,2304]{1,0:T(8,128)S(1)} %get-tuple-element.17.refs_1_, bf16[1056,256]{1,0:T(8,128)(2,1)S(1)} %get-tuple-element.18.refs_2_, bf16[2304,256]{1,0:T(8,128)(2,1)S(1)} %get-tuple-element.19.refs_3_, ...), custom_call_target="tpu_custom_call" | custom-call | tf_op jit(solution)/shard_map/add_up_last/pallas_call | solution.py:239
  (6 shorter events, 0.1 us)
Async XLA Ops:
  5.2 1.5 %collective-permute-start = (f32[256,128]{1,0:T(8,128)S(1)}, f32[256,128]{1,0:T(8,128)S(1)}, u32[]{:S(2)}, u32[]{:S(2)}) collective-permute-start(f32[256,128]{1,0:T(8,128)S(1)} %get-tuple-element.12), channel_id=1, source_target_pairs={{0,4},{4,0},{8,12},{12,8},{16,20},{20,16},{24,28},{28,24},{1,5},{5... | collective-permute-start | bytes 393224 | tf_op jit(solution)/shard_map/ppermute | solution.py:262
  6.7 7.8 %collective-permute-start.3 = (f32[256,128]{1,0:T(8,128)S(1)}, f32[256,128]{1,0:T(8,128)S(1)}, u32[]{:S(2)}, u32[]{:S(2)}) collective-permute-start(f32[256,128]{1,0:T(8,128)S(1)} %add.18), channel_id=1, source_target_pairs={{0,24},{4,28},{8,16},{12,20},{16,8},{20,12},{24,0},{28,4},{1,25},{... | collective-permute-start | bytes 393224 | tf_op jit(solution)/shard_map/ppermute | solution.py:266
  10.6 6.6 %collective-permute-start.2 = (f32[256,128]{1,0:T(8,128)S(1)}, f32[256,128]{1,0:T(8,128)S(1)}, u32[]{:S(2)}, u32[]{:S(2)}) collective-permute-start(f32[256,128]{1,0:T(8,128)S(1)} %add.18), channel_id=1, source_target_pairs={{0,16},{4,20},{8,24},{12,28},{16,0},{20,4},{24,8},{28,12},{1,17},{... | collective-permute-start | bytes 393224 | tf_op jit(solution)/shard_map/ppermute | solution.py:266
  11.1 6.4 %collective-permute-start.1 = (f32[256,128]{1,0:T(8,128)S(1)}, f32[256,128]{1,0:T(8,128)S(1)}, u32[]{:S(2)}, u32[]{:S(2)}) collective-permute-start(f32[256,128]{1,0:T(8,128)S(1)} %add.18), channel_id=1, source_target_pairs={{0,8},{4,12},{8,0},{12,4},{16,24},{20,28},{24,16},{28,20},{1,9},{5... | collective-permute-start | bytes 393224 | tf_op jit(solution)/shard_map/ppermute | solution.py:266
  17.6 4.5 %collective-permute-start.7 = (bf16[384,128]{1,0:T(8,128)(2,1)S(1)}, bf16[384,128]{1,0:T(8,128)(2,1)S(1)}, u32[]{:S(2)}, u32[]{:S(2)}) collective-permute-start(bf16[384,128]{1,0:T(8,128)(2,1)S(1)} %pad_maximum_fusion.refs_0_), channel_id=1, source_target_pairs={{0,4},{4,0},{8,12},{12,8},{16,20},{20,16},{24,28},{28,24},{1,5},{5... | collective-permute-start | bytes 294920 | tf_op jit(solution)/shard_map/ppermute | solution.py:273
  17.7 7.5 %collective-permute-start.6 = (bf16[384,128]{1,0:T(8,128)(2,1)S(1)}, bf16[384,128]{1,0:T(8,128)(2,1)S(1)}, u32[]{:S(2)}, u32[]{:S(2)}) collective-permute-start(bf16[384,128]{1,0:T(8,128)(2,1)S(1)} %pad_maximum_fusion.refs_0_), channel_id=1, source_target_pairs={{0,3},{1,2},{2,1},{3,0},{4,7},{5,6},{6,5},{7,4},{8,11},{9,10},{10,... | collective-permute-start | bytes 294920 | tf_op jit(solution)/shard_map/ppermute | solution.py:270
  21.3 9.1 %collective-permute-start.5 = (bf16[384,128]{1,0:T(8,128)(2,1)S(1)}, bf16[384,128]{1,0:T(8,128)(2,1)S(1)}, u32[]{:S(2)}, u32[]{:S(2)}) collective-permute-start(bf16[384,128]{1,0:T(8,128)(2,1)S(1)} %pad_maximum_fusion.refs_0_), channel_id=1, source_target_pairs={{0,1},{1,0},{2,3},{3,2},{4,5},{5,4},{6,7},{7,6},{8,9},{9,8},{10,11... | collective-permute-start | bytes 294920 | tf_op jit(solution)/shard_map/ppermute | solution.py:270
  21.3 9.1 %collective-permute-start.4 = (bf16[384,128]{1,0:T(8,128)(2,1)S(1)}, bf16[384,128]{1,0:T(8,128)(2,1)S(1)}, u32[]{:S(2)}, u32[]{:S(2)}) collective-permute-start(bf16[384,128]{1,0:T(8,128)(2,1)S(1)} %pad_maximum_fusion.refs_0_), channel_id=1, source_target_pairs={{0,2},{1,3},{2,0},{3,1},{4,6},{5,7},{6,4},{7,5},{8,10},{9,11},{10,... | collective-permute-start | bytes 294920 | tf_op jit(solution)/shard_map/ppermute | solution.py:270
  25.2 1.4 %collective-permute-start.8 = (bf16[384,128]{1,0:T(8,128)(2,1)S(1)}, bf16[384,128]{1,0:T(8,128)(2,1)S(1)}, u32[]{:S(2)}, u32[]{:S(2)}) collective-permute-start(bf16[384,128]{1,0:T(8,128)(2,1)S(1)} %add.22.refs_0_), channel_id=1, source_target_pairs={{0,4},{4,0},{8,12},{12,8},{16,20},{20,16},{24,28},{28,24},{1,5},{5... | collective-permute-start | bytes 294920 | tf_op jit(solution)/shard_map/ppermute | solution.py:275
  30.5 1.6 %collective-permute-start.9 = (bf16[768,128]{1,0:T(8,128)(2,1)S(1)}, bf16[768,128]{1,0:T(8,128)(2,1)S(1)}, u32[]{:S(2)}, u32[]{:S(2)}) collective-permute-start(bf16[768,128]{1,0:T(8,128)(2,1)S(1)} %maximum_add_fusion.refs_0_), channel_id=1, source_target_pairs={{0,4},{4,0},{8,12},{12,8},{16,20},{20,16},{24,28},{28,24},{1,5},{5... | collective-permute-start | bytes 589832 | tf_op jit(solution)/shard_map/ppermute | solution.py:279

commit v4 on v3

--- a/solution.py
+++ b/solution.py
@@ -96,21 +96,50 @@
     )(in_hbm(basis), in_hbm(snapshots), in_hbm(rates))
 
 
-def feature_rows(first, count, rank, states):
-    shape = (count, rank)
-    feature = first + lax.broadcasted_iota(jnp.int32, shape, 0)
-    lane = lax.broadcasted_iota(jnp.int32, shape, 1)
-    run_start = rank + lane * rank - (lane * (lane - 1)) // 2
-    run_end = run_start + rank - lane
-    in_run = (feature >= run_start) & (feature < run_end)
-    shift = jnp.sum(jnp.where(in_run, run_start - lane, 0), axis=1, keepdims=True)
-    left = in_run.astype(jnp.float32).astype(jnp.bfloat16)
-    right = (lane == feature - shift).astype(jnp.float32).astype(jnp.bfloat16)
-    pick = functools.partial(jnp.dot, preferred_element_type=jnp.float32)
-    left_rows = pick(jnp.concatenate([left, left], axis=1), states)
-    right_rows = pick(jnp.concatenate([right, right], axis=1), states)
-    linear = (feature[:, :1] < rank).astype(jnp.float32)
-    return ((left_rows + linear) * right_rows).astype(jnp.bfloat16)
+def select_kernel(row_width, col_width, row_pick, col_pick, zero_ref):
+    rank = row_pick.shape[1] // 2
+    zero_ref[...] = jnp.zeros_like(zero_ref)
+    for pick, begin in (
+        (row_pick, lax.axis_index("rows") * row_width),
+        (col_pick, lax.axis_index("reg") * col_width),
+    ):
+        for low, count in spans(pick.shape[0], TILE):
+            shape = (count, rank)
+            feature = begin + low + lax.broadcasted_iota(jnp.int32, shape, 0)
+            lane = lax.broadcasted_iota(jnp.int32, shape, 1)
+            run_start = rank + lane * rank - (lane * (lane - 1)) // 2
+            run_end = run_start + rank - lane
+            in_run = (feature >= run_start) & (feature < run_end)
+            shift = jnp.sum(jnp.where(in_run, run_start - lane, 0), axis=1, keepdims=True)
+            pick[low : low + count, :rank] = in_run.astype(jnp.float32).astype(jnp.bfloat16)
+            pick[low : low + count, rank:] = (lane == feature - shift).astype(jnp.float32).astype(jnp.bfloat16)
+
+
+def select(zero, rank, row_width, col_width):
+    row_pad, col_pad = round_up(row_width, 16), round_up(col_width + rank, TILE)
+    return pl.pallas_call(
+        functools.partial(select_kernel, row_width, col_width),
+        out_specs=[WHOLE] * 3,
+        out_shape=[
+            pltpu.VMEM((row_pad, 2 * rank), jnp.bfloat16),
+            pltpu.VMEM((col_pad - rank, 2 * rank), jnp.bfloat16),
+            pltpu.VMEM(zero.shape, zero.dtype),
+        ],
+        compiler_params=pltpu.CompilerParams(vmem_limit_bytes=8 * MIB),
+        cost_estimate=LONG,
+        name="select",
+    )()
+
+
+def feature_rows(first, pick, states):
+    rank = pick.shape[1] // 2
+    left, right = pick[:, :rank], pick[:, rank:]
+    rows = [
+        jnp.dot(jnp.concatenate([one_hot, one_hot], axis=1), states, preferred_element_type=jnp.float32)
+        for one_hot in (left, right)
+    ]
+    feature = first + lax.broadcasted_iota(jnp.int32, (pick.shape[0], 1), 0)
+    return ((rows[0] + (feature < rank).astype(jnp.float32)) * rows[1]).astype(jnp.bfloat16)
 
 
 def lay_out(pieces, states, moments):
@@ -127,62 +156,61 @@
     return [(low, min(most, total - low)) for low in range(0, total, most)]
 
 
-def fill_rows(row_width, states, row_feat, columns):
-    rank, first = states.shape[0] // 2, lax.axis_index("rows") * row_width
+def fill_rows(row_width, pick, states, row_feat, columns):
+    first = lax.axis_index("rows") * row_width
     for low, size in spans(row_feat.shape[0], ROWS):
-        row_feat[low : low + size, columns] = feature_rows(first + low, size, rank, states[...])
-
-
-def fill_columns(col_width, states, moments, col_feat, left, right, columns):
-    rank, first = moments.shape[0], lax.axis_index("reg") * col_width
-    end = min(right, col_feat.shape[0] - rank)
-    col_feat[left:end, columns] = feature_rows(first + left, end - left, rank, states[...])
+        row_feat[low : low + size, columns] = feature_rows(first + low, pick[low : low + size], states[...])
+
+
+def fill_columns(col_width, pick, states, moments, col_feat, left, right, columns):
+    first, end = lax.axis_index("reg") * col_width, min(right, pick.shape[0])
+    col_feat[left:end, columns] = feature_rows(first + left, pick[left:end], states[...])
     if end < right:
         col_feat[end:right, columns] = moments[...]
 
 
 def prepare_kernel(count, row_width, col_width, *refs):
-    pieces, (row_feat, col_feat, *zero, states, moments) = refs[:count], refs[count:]
+    pieces, (row_pick, col_pick, row_feat, col_feat, *zero, states, moments) = refs[:count], refs[count:]
     for ref in zero:
         ref[...] = jnp.zeros_like(ref)
     lay_out(pieces, states, moments)
-    fill_rows(row_width, states, row_feat, slice(None))
+    fill_rows(row_width, row_pick, states, row_feat, slice(None))
     for left, width in spans(col_feat.shape[0], COLS):
-        fill_columns(col_width, states, moments, col_feat, left, left + width, slice(None))
-
-
-def prepare(pieces, waiting, cost, rank, row_width, col_width):
+        fill_columns(col_width, col_pick, states, moments, col_feat, left, left + width, slice(None))
+
+
+def prepare(picks, pieces, waiting, cost, rank, row_width, col_width):
     times = sum(piece.size for piece in pieces) // (3 * rank)
     row_pad, col_pad = round_up(row_width, 16), round_up(col_width + rank, TILE)
     return pl.pallas_call(
         functools.partial(prepare_kernel, len(pieces), row_width, col_width),
-        in_specs=[WHOLE] * len(pieces),
+        in_specs=[WHOLE] * (len(pieces) + 2),
         out_specs=[WHOLE] * (2 + len(waiting)),
         out_shape=[pltpu.VMEM(shape, jnp.bfloat16) for shape in [(row_pad, times), (col_pad, times), *waiting]],
         scratch_shapes=[pltpu.VMEM((n * rank, times), jnp.bfloat16) for n in (2, 1)],
-        compiler_params=pltpu.CompilerParams(vmem_limit_bytes=32 * MIB),
+        compiler_params=pltpu.CompilerParams(vmem_limit_bytes=12 * MIB),
         cost_estimate=cost,
         name="prepare",
-    )(*map(in_vmem, pieces))
-
-
-def sum_kernel(count, held, ready, total_time, row_width, col_width, *refs):
+    )(*map(in_vmem, pieces), *map(in_vmem, picks))
+
+
+def sum_kernel(count, extra, held, ready, total_time, row_width, col_width, *refs):
     pieces, refs = refs[:count], refs[count:]
     acc_in, refs = (refs[0], refs[1:]) if held else (None, refs)
     (row_ready, col_ready), refs = (refs[:2], refs[2:]) if ready else ((None, None), refs)
-    refs = refs[1:]
+    row_pick, col_pick, *refs = refs[extra:]
     states, moments, row_feat, col_feat = refs[-4:]
     rank = moments.shape[0]
     row_pad, col_pad = row_feat.shape[0], col_feat.shape[0]
     columns = slice(row_feat.shape[1] - states.shape[1], row_feat.shape[1])
     before = slice(0, columns.start)
     lay_out(pieces, states, moments)
-    fill_rows(row_width, states, row_feat, columns)
+    fill_rows(row_width, row_pick, states, row_feat, columns)
     if ready:
         row_feat[:, before] = row_ready[...]
     copies = []
     for left, width in spans(col_pad, COLS):
-        fill_columns(col_width, states, moments, col_feat, left, left + width, columns)
+        fill_columns(col_width, col_pick, states, moments, col_feat, left, left + width, columns)
         if ready:
             col_feat[left : left + width, before] = col_ready[left : left + width]
         for low, size in spans(row_pad, ROWS):
@@ -198,7 +226,7 @@
                     refs[1][...] = jnp.zeros_like(refs[1])
                 continue
             gram_hbm, rhs_hbm, gram, rhs, sems = refs[:5]
-            block = block / float(total_time)
+            block = block * (1 / total_time) if total_time & (total_time - 1) == 0 else block / float(total_time)
             rows = pl.ds(low, min(size, row_width - low))
             if left < col_width:
                 part = pl.ds(left, min(width, col_width - left))
@@ -213,12 +241,11 @@
         copy.wait()
 
 
-def add_up(place, pieces, held, ready, total_time, waiting, rank, row_width, col_width):
+def add_up(picks, place, pieces, held, ready, total_time, waiting, cost, rank, row_width, col_width):
     times = sum(piece.size for piece in pieces) // (3 * rank)
     all_times = times + (ready[0].shape[1] if ready else 0)
     row_pad, col_pad = round_up(row_width, 16), round_up(col_width + rank, TILE)
-    operands = [*map(in_vmem, pieces), *map(in_vmem, held), *map(in_vmem, ready)]
-    operands += [in_vmem(place)]
+    operands = [*map(in_vmem, pieces), *map(in_vmem, held), *map(in_vmem, ready), *map(in_vmem, place), *map(in_vmem, picks)]
     scratch = [
         pltpu.VMEM((2 * rank, times), jnp.bfloat16),
         pltpu.VMEM((rank, times), jnp.bfloat16),
@@ -237,13 +264,13 @@
             pltpu.SemaphoreType.DMA((len(spans(row_pad, ROWS)) * (len(spans(col_pad, COLS)) + 1),)),
         ] + scratch
     return pl.pallas_call(
-        functools.partial(sum_kernel, len(pieces), bool(held), bool(ready), total_time, row_width, col_width),
+        functools.partial(sum_kernel, len(pieces), len(place), bool(held), bool(ready), total_time, row_width, col_width),
         in_specs=[WHOLE] * len(operands),
         out_specs=out_specs,
         out_shape=out_shape,
         scratch_shapes=scratch,
-        compiler_params=pltpu.CompilerParams(vmem_limit_bytes=32 * MIB),
-        cost_estimate=FREE,
+        compiler_params=pltpu.CompilerParams(vmem_limit_bytes=(24 if total_time else 12) * MIB),
+        cost_estimate=cost,
         name="add_up_last" if total_time else "add_up",
     )(*operands)
 
@@ -264,21 +291,23 @@
     total = chip
     for perm in plane:
         total = total + lax.ppermute(chip, "rows", perm)
+    *picks, zero = select(chip, *shape)
+    total = total + zero
     states, moments = total[:rank], total[rank:]
     high = lax.reduce_precision(states, 8, 7)
     mine = jnp.concatenate([high, states - high, moments]).astype(jnp.bfloat16)
     slabs = [mine] + [lax.ppermute(mine, "reg", perm) for perm in partners(size_reg)]
 
-    near, far = slabs[-1:], slabs[-2:0:-1]
-    *ready, zero = prepare([mine, lax.ppermute(mine, "rows", swap)], [mine.shape], LONG, *shape)
-    near = [slab + zero for slab in near]
-    pieces = [half for slab in near for half in (slab, lax.ppermute(slab, "rows", swap))]
-    waiting = (len(far) * mine.shape[0], mine.shape[1])
-    *held, zero = add_up(place, pieces, [], ready, None, waiting, *shape)
-    piece = jnp.concatenate(far) + zero
-    other = lax.ppermute(piece, "rows", swap)
-    ready = prepare([piece], [], FREE, *shape)
-    return tuple(add_up(place, [other], held, ready, total_time, None, *shape))
+    near, far = slabs[-1], slabs[-2:0:-1]
+    waiting = [(n * mine.shape[0], mine.shape[1]) for n in (1, len(far))]
+    *held, zero = add_up(picks, [], [mine, lax.ppermute(mine, "rows", swap)], [], [], None, waiting[0], LONG, *shape)
+    near = near + zero
+    pieces = [near, lax.ppermute(near, "rows", swap)]
+    *held, zero = add_up(picks, [place], pieces, held, [], None, waiting[1], FREE, *shape)
+    far = jnp.concatenate(far) + zero
+    other = lax.ppermute(far, "rows", swap)
+    ready = prepare(picks, [far], [], FREE, *shape)
+    return tuple(add_up(picks, [place], [other], held, ready, total_time, None, FREE, *shape))
 
 
 def solution(mesh):

time: 37.4 us -> 36.9 us (0.987)
  waiting for transfers between devices: 10.1 us -> 9 us
  Pallas kernels: 16.4 us -> 17 us
    pallas_call x2 -> x4, Pallas kernels: 8.99 us -> 11.4 us  [the longest x3 10.3 us: add_up(): pl.pallas_call(functools.partial(sum_kernel, len(pieces), len(place), boo...]
    pallas_call x2 -> x1, Pallas kernels: 2.81 us -> 1.05 us  [prepare(): pl.pallas_call(functools.partial(prepare_kernel, len(pieces), row_width,...]
    ppermute x3, waiting for transfers between devices: 6.25 us -> 5.16 us  [per_device(): total = total + lax.ppermute(chip, 'rows', perm)]
  transfers between devices with their start and end apart: 10 -> 10, of which waited for: 6 -> 8; matrix products, arithmetic and copies ran while one was open for 0% -> 0% of each run, Pallas kernels for 18% -> 21%
where the time goes in v4:
time: 36.9 us; the launch traced here: 36.7 us
  Pallas kernels  17 us (46%)
  starting transfers between devices  9.7 us (26%)
  waiting for transfers between devices  9 us (24%)
  between operations  0.74 us (2%)
    pallas_call x3, Pallas kernels, add_up(): pl.pallas_call(functools.partial(sum_kernel, len(pieces), len(place), boo...  10.3 us
    ppermute x3, waiting for transfers between devices, per_device(): total = total + lax.ppermute(chip, 'rows', perm)  5.16 us
    pallas_call x1, Pallas kernels, project(): pl.pallas_call(functools.partial(project_kernel, chunks), in_specs=[ANYWH...  4.56 us
    ppermute x3, starting transfers between devices, per_device(): total = total + lax.ppermute(chip, 'rows', perm)  4.52 us
    ppermute x3, starting transfers between devices, per_device(): lax.ppermute(mine, 'reg', perm)  4.45 us
    ppermute x3, waiting for transfers between devices, per_device(): lax.ppermute(mine, 'reg', perm)  1.27 us
    ppermute x1, waiting for transfers between devices, per_device(): pieces = [near, lax.ppermute(near, 'rows', swap)]  1.21 us
    pallas_call x1, Pallas kernels, select(): pl.pallas_call(functools.partial(select_kernel, row_width, col_width), ou...  1.08 us
  transfers between devices with their start and end apart: 10, of which 8 were waited for; matrix products, arithmetic and copies ran while one was open for 0% of the time, Pallas kernels for 21%

profile of v4, /device:TPU:0, one launch (start us, length us, event | category | flops | bytes accessed | tf_op | source)
XLA Modules:
  0.0 36.7 jit_solution(9389222095284121775)
XLA Ops:
  0.6 4.6 %project.1 = (f32[256,128]{1,0:T(8,128)S(1)}, f32[256,128]{1,0:T(8,128)S(1)}) custom-call(bf16[8192,128]{1,0:T(8,128)(2,1)} %basis_hbm.1, bf16[8192,256]{1,0:T(8,128)(2,1)} %snap_hbm.1, bf16[8192,256]{1,0:T(8,128)(2,1)} %rate_hbm.1), custom_call_target="tpu_custom_call" | custom-call | flops 1073741824 | bytes 10485760 | tf_op jit(solution)/shard_map/project/pallas_call | solution.py:79
  5.2 0.5 %collective-permute-start = (f32[256,128]{1,0:T(8,128)S(1)}, f32[256,128]{1,0:T(8,128)S(1)}, u32[]{:S(2)}, u32[]{:S(2)}) collective-permute-start(f32[256,128]{1,0:T(8,128)S(1)} %get-tuple-element.14), channel_id=1, source_target_pairs={{0,4},{4,0},{8,12},{12,8},{16,20},{20,16},{24,28},{28,24},{1,5},{5... | collective-permute-start | bytes 393224 | tf_op jit(solution)/shard_map/ppermute | solution.py:289
  5.7 1.0 %collective-permute-done = f32[256,128]{1,0:T(8,128)S(1)} collective-permute-done((f32[256,128]{1,0:T(8,128)S(1)}, f32[256,128]{1,0:T(8,128)S(1)}, u32[]{:S(2)}, u32[]{:S(2)}) %collective-permute-start) | collective-permute-done | bytes 131104 | tf_op jit(solution)/shard_map/ppermute | solution.py:289
  6.7 3.9 %collective-permute-start.3 = (f32[256,128]{1,0:T(8,128)S(1)}, f32[256,128]{1,0:T(8,128)S(1)}, u32[]{:S(2)}, u32[]{:S(2)}) collective-permute-start(f32[256,128]{1,0:T(8,128)S(1)} %add.21), channel_id=1, source_target_pairs={{0,24},{4,28},{8,16},{12,20},{16,8},{20,12},{24,0},{28,4},{1,25},{... | collective-permute-start | bytes 393224 | tf_op jit(solution)/shard_map/ppermute | solution.py:293
  10.6 0.5 %collective-permute-start.2 = (f32[256,128]{1,0:T(8,128)S(1)}, f32[256,128]{1,0:T(8,128)S(1)}, u32[]{:S(2)}, u32[]{:S(2)}) collective-permute-start(f32[256,128]{1,0:T(8,128)S(1)} %add.21), channel_id=1, source_target_pairs={{0,16},{4,20},{8,24},{12,28},{16,0},{20,4},{24,8},{28,12},{1,17},{... | collective-permute-start | bytes 393224 | tf_op jit(solution)/shard_map/ppermute | solution.py:293
  11.1 0.1 collective-permute-start.1
  11.2 1.1 %select.1 = (bf16[1056,256]{1,0:T(8,128)(2,1)S(1)}, bf16[2176,256]{1,0:T(8,128)(2,1)S(1)}, f32[256,128]{1,0:T(8,128)S(1)}) custom-call(), custom_call_target="tpu_custom_call" | custom-call | flops 20000000000 | tf_op jit(solution)/shard_map/select/pallas_call | solution.py:120
  12.3 2.2 %collective-permute-done.3 = f32[256,128]{1,0:T(8,128)S(1)} collective-permute-done((f32[256,128]{1,0:T(8,128)S(1)}, f32[256,128]{1,0:T(8,128)S(1)}, u32[]{:S(2)}, u32[]{:S(2)}) %collective-permute-start.3) | collective-permute-done | bytes 131104 | tf_op jit(solution)/shard_map/ppermute | solution.py:293
  14.5 2.7 %collective-permute-done.2 = f32[256,128]{1,0:T(8,128)S(1)} collective-permute-done((f32[256,128]{1,0:T(8,128)S(1)}, f32[256,128]{1,0:T(8,128)S(1)}, u32[]{:S(2)}, u32[]{:S(2)}) %collective-permute-start.2) | collective-permute-done | bytes 131104 | tf_op jit(solution)/shard_map/ppermute | solution.py:293
  17.2 0.3 collective-permute-done.1
  17.6 0.1 collective-permute-start.7
  17.7 3.7 %collective-permute-start.6 = (bf16[384,128]{1,0:T(8,128)(2,1)S(1)}, bf16[384,128]{1,0:T(8,128)(2,1)S(1)}, u32[]{:S(2)}, u32[]{:S(2)}) collective-permute-start(bf16[384,128]{1,0:T(8,128)(2,1)S(1)} %pad_maximum_fusion.refs_0_), channel_id=1, source_target_pairs={{0,3},{1,2},{2,1},{3,0},{4,7},{5,6},{6,5},{7,4},{8,11},{9,10},{10,... | collective-permute-start | bytes 294920 | tf_op jit(solution)/shard_map/ppermute | solution.py:299
  21.3 0.0 collective-permute-start.5
  21.3 0.8 %collective-permute-start.4 = (bf16[384,128]{1,0:T(8,128)(2,1)S(1)}, bf16[384,128]{1,0:T(8,128)(2,1)S(1)}, u32[]{:S(2)}, u32[]{:S(2)}) collective-permute-start(bf16[384,128]{1,0:T(8,128)(2,1)S(1)} %pad_maximum_fusion.refs_0_), channel_id=1, source_target_pairs={{0,2},{1,3},{2,0},{3,1},{4,6},{5,7},{6,4},{7,5},{8,10},{9,11},{10,... | collective-permute-start | bytes 294920 | tf_op jit(solution)/shard_map/ppermute | solution.py:299
  22.1 0.0 collective-permute-done.7.refs_1_
  22.1 2.6 %add_up.2 = (f32[1056,2304]{1,0:T(8,128)S(1)}, bf16[384,128]{1,0:T(8,128)(2,1)S(1)}) custom-call(bf16[384,128]{1,0:T(8,128)(2,1)S(1)} %pad_maximum_fusion.refs_0_, bf16[384,128]{1,0:T(8,128)(2,1)S(1)} %collective-permute-done.7.refs_1_, bf16[1056,256]{1,0:T(8,128)(2,1)S(1)} %get-tuple-element.16.refs_2_.refs_4_.refs_1_.refs_5_, ...), custom_call_target="tpu_custom_call" | custom-call | flops 20000000000 | tf_op jit(solution)/shard_map/add_up/pallas_call | solution.py:266
  24.8 0.4 %collective-permute-done.6 = bf16[384,128]{1,0:T(8,128)(2,1)S(1)} collective-permute-done((bf16[384,128]{1,0:T(8,128)(2,1)S(1)}, bf16[384,128]{1,0:T(8,128)(2,1)S(1)}, u32[]{:S(2)}, u32[]{:S(2)}) %collective-permute-start.6) | collective-permute-done | bytes 98336 | tf_op jit(solution)/shard_map/ppermute | solution.py:299
  25.2 0.1 collective-permute-start.8
  25.3 0.1 pad_add_fusion.refs_3_.refs_4_
  25.4 1.2 %collective-permute-done.8.refs_1_ = bf16[384,128]{1,0:T(8,128)(2,1)S(1)} collective-permute-done((bf16[384,128]{1,0:T(8,128)(2,1)S(1)}, bf16[384,128]{1,0:T(8,128)(2,1)S(1)}, u32[]{:S(2)}, u32[]{:S(2)}) %collective-permute-start.8) | collective-permute-done | bytes 98336 | tf_op jit(solution)/shard_map/ppermute | solution.py:305
  26.6 2.8 %add_up.3 = (f32[1056,2304]{1,0:T(8,128)S(1)}, bf16[768,128]{1,0:T(8,128)(2,1)S(1)}) custom-call(bf16[384,128]{1,0:T(8,128)(2,1)S(1)} %add.26.refs_0_, bf16[384,128]{1,0:T(8,128)(2,1)S(1)} %collective-permute-done.8.refs_1_, f32[1056,2304]{1,0:T(8,128)S(1)} %get-tuple-element.19.refs_2_, s32[2]{0:T(128)S(1)} %pad_add_fusion.refs_3_.refs_4_, ...), custom_call_target="tpu_custom_call" | custom-call | tf_op jit(solution)/shard_map/add_up/pallas_call | solution.py:266
  29.3 0.0 collective-permute-done.5
  29.3 0.9 %collective-permute-done.4 = bf16[384,128]{1,0:T(8,128)(2,1)S(1)} collective-permute-done((bf16[384,128]{1,0:T(8,128)(2,1)S(1)}, bf16[384,128]{1,0:T(8,128)(2,1)S(1)}, u32[]{:S(2)}, u32[]{:S(2)}) %collective-permute-start.4) | collective-permute-done | bytes 98336 | tf_op jit(solution)/shard_map/ppermute | solution.py:299
  30.2 0.1 maximum_add_fusion.refs_0_
  30.3 0.1 collective-permute-start.9
  30.3 1.1 %prepare.1 = (bf16[1056,256]{1,0:T(8,128)(2,1)S(1)}, bf16[2304,256]{1,0:T(8,128)(2,1)S(1)}) custom-call(bf16[768,128]{1,0:T(8,128)(2,1)S(1)} %maximum_add_fusion.refs_0_, bf16[1056,256]{1,0:T(8,128)(2,1)S(1)} %get-tuple-element.16.refs_2_.refs_4_.refs_1_.refs_5_, bf16[2176,256]{1,0:T(8,128)(2,1)S(1)} %get-tuple-element.17.refs_3_.refs_5_.refs_2_.refs_6_), custom_call_target="tpu_custom_call" | custom-call | tf_op jit(solution)/shard_map/prepare/pallas_call | solution.py:185
  31.4 0.4 %collective-permute-done.9.refs_0_ = bf16[768,128]{1,0:T(8,128)(2,1)S(1)} collective-permute-done((bf16[768,128]{1,0:T(8,128)(2,1)S(1)}, bf16[768,128]{1,0:T(8,128)(2,1)S(1)}, u32[]{:S(2)}, u32[]{:S(2)}) %collective-permute-start.9) | collective-permute-done | bytes 196640 | tf_op jit(solution)/shard_map/ppermute | solution.py:308
  31.8 4.9 %add_up_last.1 = (f32[1048,2096]{1,0:T(8,128)}, f32[1048,128]{1,0:T(8,128)}) custom-call(bf16[768,128]{1,0:T(8,128)(2,1)S(1)} %collective-permute-done.9.refs_0_, f32[1056,2304]{1,0:T(8,128)S(1)} %get-tuple-element.21.refs_1_, bf16[1056,256]{1,0:T(8,128)(2,1)S(1)} %get-tuple-element.22.refs_2_, bf16[2304,256]{1,0:T(8,128)(2,1)S(1)} %get-tuple-element.23.refs_3_, ...), custom_call_target="tpu_custom_call" | custom-call | tf_op jit(solution)/shard_map/add_up_last/pallas_call | solution.py:266
  (6 shorter events, 0.1 us)
Async XLA Ops:
  5.2 1.5 %collective-permute-start = (f32[256,128]{1,0:T(8,128)S(1)}, f32[256,128]{1,0:T(8,128)S(1)}, u32[]{:S(2)}, u32[]{:S(2)}) collective-permute-start(f32[256,128]{1,0:T(8,128)S(1)} %get-tuple-element.14), channel_id=1, source_target_pairs={{0,4},{4,0},{8,12},{12,8},{16,20},{20,16},{24,28},{28,24},{1,5},{5... | collective-permute-start | bytes 393224 | tf_op jit(solution)/shard_map/ppermute | solution.py:289
  6.7 7.8 %collective-permute-start.3 = (f32[256,128]{1,0:T(8,128)S(1)}, f32[256,128]{1,0:T(8,128)S(1)}, u32[]{:S(2)}, u32[]{:S(2)}) collective-permute-start(f32[256,128]{1,0:T(8,128)S(1)} %add.21), channel_id=1, source_target_pairs={{0,24},{4,28},{8,16},{12,20},{16,8},{20,12},{24,0},{28,4},{1,25},{... | collective-permute-start | bytes 393224 | tf_op jit(solution)/shard_map/ppermute | solution.py:293
  10.6 6.6 %collective-permute-start.2 = (f32[256,128]{1,0:T(8,128)S(1)}, f32[256,128]{1,0:T(8,128)S(1)}, u32[]{:S(2)}, u32[]{:S(2)}) collective-permute-start(f32[256,128]{1,0:T(8,128)S(1)} %add.21), channel_id=1, source_target_pairs={{0,16},{4,20},{8,24},{12,28},{16,0},{20,4},{24,8},{28,12},{1,17},{... | collective-permute-start | bytes 393224 | tf_op jit(solution)/shard_map/ppermute | solution.py:293
  11.1 6.4 %collective-permute-start.1 = (f32[256,128]{1,0:T(8,128)S(1)}, f32[256,128]{1,0:T(8,128)S(1)}, u32[]{:S(2)}, u32[]{:S(2)}) collective-permute-start(f32[256,128]{1,0:T(8,128)S(1)} %add.21), channel_id=1, source_target_pairs={{0,8},{4,12},{8,0},{12,4},{16,24},{20,28},{24,16},{28,20},{1,9},{5... | collective-permute-start | bytes 393224 | tf_op jit(solution)/shard_map/ppermute | solution.py:293
  17.6 4.5 %collective-permute-start.7 = (bf16[384,128]{1,0:T(8,128)(2,1)S(1)}, bf16[384,128]{1,0:T(8,128)(2,1)S(1)}, u32[]{:S(2)}, u32[]{:S(2)}) collective-permute-start(bf16[384,128]{1,0:T(8,128)(2,1)S(1)} %pad_maximum_fusion.refs_0_), channel_id=1, source_target_pairs={{0,4},{4,0},{8,12},{12,8},{16,20},{20,16},{24,28},{28,24},{1,5},{5... | collective-permute-start | bytes 294920 | tf_op jit(solution)/shard_map/ppermute | solution.py:303
  17.7 7.5 %collective-permute-start.6 = (bf16[384,128]{1,0:T(8,128)(2,1)S(1)}, bf16[384,128]{1,0:T(8,128)(2,1)S(1)}, u32[]{:S(2)}, u32[]{:S(2)}) collective-permute-start(bf16[384,128]{1,0:T(8,128)(2,1)S(1)} %pad_maximum_fusion.refs_0_), channel_id=1, source_target_pairs={{0,3},{1,2},{2,1},{3,0},{4,7},{5,6},{6,5},{7,4},{8,11},{9,10},{10,... | collective-permute-start | bytes 294920 | tf_op jit(solution)/shard_map/ppermute | solution.py:299
  21.3 8.0 %collective-permute-start.5 = (bf16[384,128]{1,0:T(8,128)(2,1)S(1)}, bf16[384,128]{1,0:T(8,128)(2,1)S(1)}, u32[]{:S(2)}, u32[]{:S(2)}) collective-permute-start(bf16[384,128]{1,0:T(8,128)(2,1)S(1)} %pad_maximum_fusion.refs_0_), channel_id=1, source_target_pairs={{0,1},{1,0},{2,3},{3,2},{4,5},{5,4},{6,7},{7,6},{8,9},{9,8},{10,11... | collective-permute-start | bytes 294920 | tf_op jit(solution)/shard_map/ppermute | solution.py:299
  21.3 8.9 %collective-permute-start.4 = (bf16[384,128]{1,0:T(8,128)(2,1)S(1)}, bf16[384,128]{1,0:T(8,128)(2,1)S(1)}, u32[]{:S(2)}, u32[]{:S(2)}) collective-permute-start(bf16[384,128]{1,0:T(8,128)(2,1)S(1)} %pad_maximum_fusion.refs_0_), channel_id=1, source_target_pairs={{0,2},{1,3},{2,0},{3,1},{4,6},{5,7},{6,4},{7,5},{8,10},{9,11},{10,... | collective-permute-start | bytes 294920 | tf_op jit(solution)/shard_map/ppermute | solution.py:299
  25.2 1.4 %collective-permute-start.8 = (bf16[384,128]{1,0:T(8,128)(2,1)S(1)}, bf16[384,128]{1,0:T(8,128)(2,1)S(1)}, u32[]{:S(2)}, u32[]{:S(2)}) collective-permute-start(bf16[384,128]{1,0:T(8,128)(2,1)S(1)} %add.26.refs_0_), channel_id=1, source_target_pairs={{0,4},{4,0},{8,12},{12,8},{16,20},{20,16},{24,28},{28,24},{1,5},{5... | collective-permute-start | bytes 294920 | tf_op jit(solution)/shard_map/ppermute | solution.py:305
  30.3 1.5 %collective-permute-start.9 = (bf16[768,128]{1,0:T(8,128)(2,1)S(1)}, bf16[768,128]{1,0:T(8,128)(2,1)S(1)}, u32[]{:S(2)}, u32[]{:S(2)}) collective-permute-start(bf16[768,128]{1,0:T(8,128)(2,1)S(1)} %maximum_add_fusion.refs_0_), channel_id=1, source_target_pairs={{0,4},{4,0},{8,12},{12,8},{16,20},{20,16},{24,28},{28,24},{1,5},{5... | collective-permute-start | bytes 589832 | tf_op jit(solution)/shard_map/ppermute | solution.py:308

commit v5 on v4

--- a/solution.py
+++ b/solution.py
@@ -275,6 +275,28 @@
     )(*operands)
 
 
+def encode(states, moments):
+    coded, exponents = [], []
+    for array in (states, lax.reduce_precision(moments, 8, 7)):
+        largest = jnp.max(jnp.abs(array), axis=0, keepdims=True)
+        exponents.append(jnp.ceil(jnp.log2(jnp.maximum(largest, 1e-37))))
+        coded.append(array * jnp.exp2(-exponents[-1]))
+    last = lax.broadcasted_iota(jnp.int32, (16, states.shape[1]), 0)
+    return jnp.concatenate([*coded, jnp.where(last == 0, *exponents)]).astype(jnp.float16)
+
+
+def decode(coded, rank):
+    coded = coded.astype(jnp.float32)
+    states = coded[:rank] * jnp.exp2(coded[2 * rank : 2 * rank + 1])
+    moments = coded[rank : 2 * rank] * jnp.exp2(coded[2 * rank + 1 : 2 * rank + 2])
+    return split(states, moments)
+
+
+def split(states, moments):
+    high = lax.reduce_precision(states, 8, 7)
+    return jnp.concatenate([high, states - high, moments]).astype(jnp.bfloat16)
+
+
 def per_device(snapshots, rates, basis):
     rank = basis.shape[1]
     width = rank + rank * (rank + 1) // 2
@@ -294,17 +316,24 @@
     *picks, zero = select(chip, *shape)
     total = total + zero
     states, moments = total[:rank], total[rank:]
-    high = lax.reduce_precision(states, 8, 7)
-    mine = jnp.concatenate([high, states - high, moments]).astype(jnp.bfloat16)
-    slabs = [mine] + [lax.ppermute(mine, "reg", perm) for perm in partners(size_reg)]
-
-    near, far = slabs[-1], slabs[-2:0:-1]
-    waiting = [(n * mine.shape[0], mine.shape[1]) for n in (1, len(far))]
-    *held, zero = add_up(picks, [], [mine, lax.ppermute(mine, "rows", swap)], [], [], None, waiting[0], LONG, *shape)
-    near = near + zero
+    mine, coded = split(states, moments), encode(states, moments)
+
+    own = [mine, lax.ppermute(mine, "rows", swap)]
+    near = lax.ppermute(coded, "reg", [(n, size_reg - 1 - n) for n in range(size_reg)])
+    places = [(row, reg) for row in range(size_rows) for reg in range(size_reg)]
+    high, low, moments = jnp.split(own[1].astype(jnp.float32), 3)
+    whole = jnp.concatenate([coded, encode(high + low, moments)])
+    far = []
+    for k in range(1, size_reg - 1, 2):
+        perm = [(n, row * size_reg + (reg ^ (k + row % 2))) for n, (row, reg) in enumerate(places)]
+        far.append(lax.ppermute(whole, ("rows", "reg"), perm))
+    *held, zero = add_up(picks, [], own, [], [], None, coded.shape, LONG, *shape)
+    near = decode(near + zero.astype(coded.dtype), rank)
+    waiting = (len(far) * whole.shape[0], whole.shape[1])
     pieces = [near, lax.ppermute(near, "rows", swap)]
-    *held, zero = add_up(picks, [place], pieces, held, [], None, waiting[1], FREE, *shape)
-    far = jnp.concatenate(far) + zero
+    *held, zero = add_up(picks, [place], pieces, held, [], None, waiting, FREE, *shape)
+    far = jnp.concatenate(far) + zero.astype(coded.dtype)
+    far = jnp.concatenate([decode(slab, rank) for slab in jnp.split(far, size_reg - 2)])
     other = lax.ppermute(far, "rows", swap)
     ready = prepare(picks, [far], [], FREE, *shape)
     return tuple(add_up(picks, [place], [other], held, ready, total_time, None, FREE, *shape))

time: 36.9 us -> 35.6 us (0.965)
  waiting for transfers between devices: 9 us -> 7.54 us
  other arithmetic: 0.24 us -> 0.84 us
  starting transfers between devices: 9.7 us -> 9.21 us
    ppermute x4 -> x3, waiting for transfers between devices: 1.27 us -> 0.1 us  [the longest x1 0.09 us: per_device(): lax.ppermute(coded, 'reg', [(n, size_reg - 1 - n) for n in range(size_reg)])]
    ppermute x4 -> x3, starting transfers between devices: 4.52 us -> 3.75 us  [the longest x1 3.67 us: per_device(): lax.ppermute(coded, 'reg', [(n, size_reg - 1 - n) for n in range(size_reg)])]
  transfers between devices with their start and end apart: 10 -> 9, of which waited for: 8 -> 7; matrix products, arithmetic and copies ran while one was open for 0% -> 2% of each run, Pallas kernels for 21% -> 21%
where the time goes in v5:
time: 35.6 us; the launch traced here: 35.5 us
  Pallas kernels  17 us (48%)
  starting transfers between devices  9.21 us (26%)
  waiting for transfers between devices  7.54 us (21%)
  between operations  0.86 us (2%)
  other arithmetic  0.84 us (2%)
    pallas_call x3, Pallas kernels, add_up(): pl.pallas_call(functools.partial(sum_kernel, len(pieces), len(place), boo...  10.3 us
    ppermute x3, waiting for transfers between devices, per_device(): total = total + lax.ppermute(chip, 'rows', perm)  5.14 us
    pallas_call x1, Pallas kernels, project(): pl.pallas_call(functools.partial(project_kernel, chunks), in_specs=[ANYWH...  4.56 us
    ppermute x3, starting transfers between devices, per_device(): total = total + lax.ppermute(chip, 'rows', perm)  4.52 us
    ppermute x1, starting transfers between devices, per_device(): lax.ppermute(coded, 'reg', [(n, size_reg - 1 - n) for n in range(size_reg)])  3.67 us
    ppermute x1, waiting for transfers between devices, per_device(): pieces = [near, lax.ppermute(near, 'rows', swap)]  1.08 us
    pallas_call x1, Pallas kernels, select(): pl.pallas_call(functools.partial(select_kernel, row_width, col_width), ou...  1.08 us
    pallas_call x1, Pallas kernels, prepare(): pl.pallas_call(functools.partial(prepare_kernel, len(pieces), row_width,...  1.05 us
  transfers between devices with their start and end apart: 9, of which 7 were waited for; matrix products, arithmetic and copies ran while one was open for 2% of the time, Pallas kernels for 21%

profile of v5, /device:TPU:0, one launch (start us, length us, event | category | flops | bytes accessed | tf_op | source)
XLA Modules:
  0.0 35.5 jit_solution(4553889584449649690)
XLA Ops:
  0.6 4.6 %project.1 = (f32[256,128]{1,0:T(8,128)S(1)}, f32[256,128]{1,0:T(8,128)S(1)}) custom-call(bf16[8192,128]{1,0:T(8,128)(2,1)} %basis_hbm.1, bf16[8192,256]{1,0:T(8,128)(2,1)} %snap_hbm.1, bf16[8192,256]{1,0:T(8,128)(2,1)} %rate_hbm.1), custom_call_target="tpu_custom_call" | custom-call | flops 1073741824 | bytes 10485760 | tf_op jit(solution)/shard_map/project/pallas_call | solution.py:79
  5.2 0.5 %collective-permute-start = (f32[256,128]{1,0:T(8,128)S(1)}, f32[256,128]{1,0:T(8,128)S(1)}, u32[]{:S(2)}, u32[]{:S(2)}) collective-permute-start(f32[256,128]{1,0:T(8,128)S(1)} %get-tuple-element.14), channel_id=1, source_target_pairs={{0,4},{4,0},{8,12},{12,8},{16,20},{20,16},{24,28},{28,24},{1,5},{5... | collective-permute-start | bytes 393224 | tf_op jit(solution)/shard_map/ppermute | solution.py:311
  5.7 1.0 %collective-permute-done = f32[256,128]{1,0:T(8,128)S(1)} collective-permute-done((f32[256,128]{1,0:T(8,128)S(1)}, f32[256,128]{1,0:T(8,128)S(1)}, u32[]{:S(2)}, u32[]{:S(2)}) %collective-permute-start) | collective-permute-done | bytes 131104 | tf_op jit(solution)/shard_map/ppermute | solution.py:311
  6.7 3.9 %collective-permute-start.3 = (f32[256,128]{1,0:T(8,128)S(1)}, f32[256,128]{1,0:T(8,128)S(1)}, u32[]{:S(2)}, u32[]{:S(2)}) collective-permute-start(f32[256,128]{1,0:T(8,128)S(1)} %add.24), channel_id=1, source_target_pairs={{0,24},{4,28},{8,16},{12,20},{16,8},{20,12},{24,0},{28,4},{1,25},{... | collective-permute-start | bytes 393224 | tf_op jit(solution)/shard_map/ppermute | solution.py:315
  10.6 0.5 %collective-permute-start.2 = (f32[256,128]{1,0:T(8,128)S(1)}, f32[256,128]{1,0:T(8,128)S(1)}, u32[]{:S(2)}, u32[]{:S(2)}) collective-permute-start(f32[256,128]{1,0:T(8,128)S(1)} %add.24), channel_id=1, source_target_pairs={{0,16},{4,20},{8,24},{12,28},{16,0},{20,4},{24,8},{28,12},{1,17},{... | collective-permute-start | bytes 393224 | tf_op jit(solution)/shard_map/ppermute | solution.py:315
  11.1 0.1 collective-permute-start.1
  11.2 1.1 %select.1 = (bf16[1056,256]{1,0:T(8,128)(2,1)S(1)}, bf16[2176,256]{1,0:T(8,128)(2,1)S(1)}, f32[256,128]{1,0:T(8,128)S(1)}) custom-call(), custom_call_target="tpu_custom_call" | custom-call | flops 20000000000 | tf_op jit(solution)/shard_map/select/pallas_call | solution.py:120
  12.3 2.2 %collective-permute-done.3 = f32[256,128]{1,0:T(8,128)S(1)} collective-permute-done((f32[256,128]{1,0:T(8,128)S(1)}, f32[256,128]{1,0:T(8,128)S(1)}, u32[]{:S(2)}, u32[]{:S(2)}) %collective-permute-start.3) | collective-permute-done | bytes 131104 | tf_op jit(solution)/shard_map/ppermute | solution.py:315
  14.5 2.7 %collective-permute-done.2 = f32[256,128]{1,0:T(8,128)S(1)} collective-permute-done((f32[256,128]{1,0:T(8,128)S(1)}, f32[256,128]{1,0:T(8,128)S(1)}, u32[]{:S(2)}, u32[]{:S(2)}) %collective-permute-start.2) | collective-permute-done | bytes 131104 | tf_op jit(solution)/shard_map/ppermute | solution.py:315
  17.2 0.3 collective-permute-done.1
  17.6 0.1 collective-permute-start.4
  17.7 0.1 select_convert_fusion.1
  17.8 0.1 constant_dynamic-update-slice_fusion.1
  17.9 3.7 %collective-permute-start.6 = (f16[272,128]{1,0:T(8,128)(2,1)S(1)}, f16[272,128]{1,0:T(8,128)(2,1)S(1)}, u32[]{:S(2)}, u32[]{:S(2)}) collective-permute-start(f16[272,128]{1,0:T(8,128)(2,1)S(1)} %pad_maximum_fusion.2), channel_id=1, source_target_pairs={{0,3},{1,2},{2,1},{3,0},{4,7},{5,6},{6,5},{7,4},{8,11},{9,10},{10,... | collective-permute-start | bytes 208904 | tf_op jit(solution)/shard_map/ppermute | solution.py:322
  21.6 0.0 collective-permute-done.4.refs_1_
  21.7 0.1 constant_dynamic-update-slice_fusion
  21.8 0.0 collective-permute-start.5
  21.8 2.6 %add_up.2 = (f32[1056,2304]{1,0:T(8,128)S(1)}, bf16[272,128]{1,0:T(8,128)(2,1)S(1)}) custom-call(bf16[384,128]{1,0:T(8,128)(2,1)S(1)} %pad_maximum_fusion.refs_0_, bf16[384,128]{1,0:T(8,128)(2,1)S(1)} %collective-permute-done.4.refs_1_, bf16[1056,256]{1,0:T(8,128)(2,1)S(1)} %get-tuple-element.16.refs_2_.refs_4_.refs_1_.refs_5_, ...), custom_call_target="tpu_custom_call" | custom-call | flops 20000000000 | tf_op jit(solution)/shard_map/add_up/pallas_call | solution.py:266
  24.5 0.1 collective-permute-done.6
  24.6 0.2 collective-permute-start.7
  24.8 0.1 pad_add_fusion.refs_3_.refs_4_
  24.9 1.1 %collective-permute-done.7.refs_1_ = bf16[384,128]{1,0:T(8,128)(2,1)S(1)} collective-permute-done((bf16[384,128]{1,0:T(8,128)(2,1)S(1)}, bf16[384,128]{1,0:T(8,128)(2,1)S(1)}, u32[]{:S(2)}, u32[]{:S(2)}) %collective-permute-start.7) | collective-permute-done | bytes 98336 | tf_op jit(solution)/shard_map/ppermute | solution.py:333
  26.0 2.8 %add_up.3 = (f32[1056,2304]{1,0:T(8,128)S(1)}, bf16[544,128]{1,0:T(8,128)(2,1)S(1)}) custom-call(bf16[384,128]{1,0:T(8,128)(2,1)S(1)} %pad_maximum_fusion.1.refs_0_, bf16[384,128]{1,0:T(8,128)(2,1)S(1)} %collective-permute-done.7.refs_1_, f32[1056,2304]{1,0:T(8,128)S(1)} %get-tuple-element.19.refs_2_, s32[2]{0:T(128)S(1)} %pad_add_fusion.refs_3_.refs_4_, ...), custom_call_target="tpu_custom_call" | custom-call | tf_op jit(solution)/shard_map/add_up/pallas_call | solution.py:266
  28.8 0.0 collective-permute-done.5
  28.8 0.1 convert_add_fusion
  29.0 0.2 collective-permute-start.8
  29.2 1.0 %prepare.1 = (bf16[1056,256]{1,0:T(8,128)(2,1)S(1)}, bf16[2304,256]{1,0:T(8,128)(2,1)S(1)}) custom-call(bf16[768,128]{1,0:T(8,128)(2,1)S(1)} %fusion.10.refs_0_, bf16[1056,256]{1,0:T(8,128)(2,1)S(1)} %get-tuple-element.16.refs_2_.refs_4_.refs_1_.refs_5_, bf16[2176,256]{1,0:T(8,128)(2,1)S(1)} %get-tuple-element.17.refs_3_.refs_5_.refs_2_.refs_6_), custom_call_target="tpu_custom_call" | custom-call | tf_op jit(solution)/shard_map/prepare/pallas_call | solution.py:185
  30.3 0.2 collective-permute-done.8.refs_0_
  30.5 4.9 %add_up_last.1 = (f32[1048,2096]{1,0:T(8,128)}, f32[1048,128]{1,0:T(8,128)}) custom-call(bf16[768,128]{1,0:T(8,128)(2,1)S(1)} %collective-permute-done.8.refs_0_, f32[1056,2304]{1,0:T(8,128)S(1)} %get-tuple-element.21.refs_1_, bf16[1056,256]{1,0:T(8,128)(2,1)S(1)} %get-tuple-element.22.refs_2_, bf16[2304,256]{1,0:T(8,128)(2,1)S(1)} %get-tuple-element.23.refs_3_, ...), custom_call_target="tpu_custom_call" | custom-call | tf_op jit(solution)/shard_map/add_up_last/pallas_call | solution.py:266
  (28 shorter events, 0.5 us)
Async XLA Ops:
  5.2 1.5 %collective-permute-start = (f32[256,128]{1,0:T(8,128)S(1)}, f32[256,128]{1,0:T(8,128)S(1)}, u32[]{:S(2)}, u32[]{:S(2)}) collective-permute-start(f32[256,128]{1,0:T(8,128)S(1)} %get-tuple-element.14), channel_id=1, source_target_pairs={{0,4},{4,0},{8,12},{12,8},{16,20},{20,16},{24,28},{28,24},{1,5},{5... | collective-permute-start | bytes 393224 | tf_op jit(solution)/shard_map/ppermute | solution.py:311
  6.7 7.8 %collective-permute-start.3 = (f32[256,128]{1,0:T(8,128)S(1)}, f32[256,128]{1,0:T(8,128)S(1)}, u32[]{:S(2)}, u32[]{:S(2)}) collective-permute-start(f32[256,128]{1,0:T(8,128)S(1)} %add.24), channel_id=1, source_target_pairs={{0,24},{4,28},{8,16},{12,20},{16,8},{20,12},{24,0},{28,4},{1,25},{... | collective-permute-start | bytes 393224 | tf_op jit(solution)/shard_map/ppermute | solution.py:315
  10.6 6.6 %collective-permute-start.2 = (f32[256,128]{1,0:T(8,128)S(1)}, f32[256,128]{1,0:T(8,128)S(1)}, u32[]{:S(2)}, u32[]{:S(2)}) collective-permute-start(f32[256,128]{1,0:T(8,128)S(1)} %add.24), channel_id=1, source_target_pairs={{0,16},{4,20},{8,24},{12,28},{16,0},{20,4},{24,8},{28,12},{1,17},{... | collective-permute-start | bytes 393224 | tf_op jit(solution)/shard_map/ppermute | solution.py:315
  11.1 6.4 %collective-permute-start.1 = (f32[256,128]{1,0:T(8,128)S(1)}, f32[256,128]{1,0:T(8,128)S(1)}, u32[]{:S(2)}, u32[]{:S(2)}) collective-permute-start(f32[256,128]{1,0:T(8,128)S(1)} %add.24), channel_id=1, source_target_pairs={{0,8},{4,12},{8,0},{12,4},{16,24},{20,28},{24,16},{28,20},{1,9},{5... | collective-permute-start | bytes 393224 | tf_op jit(solution)/shard_map/ppermute | solution.py:315
  17.6 4.0 %collective-permute-start.4 = (bf16[384,128]{1,0:T(8,128)(2,1)S(1)}, bf16[384,128]{1,0:T(8,128)(2,1)S(1)}, u32[]{:S(2)}, u32[]{:S(2)}) collective-permute-start(bf16[384,128]{1,0:T(8,128)(2,1)S(1)} %pad_maximum_fusion.refs_0_), channel_id=1, source_target_pairs={{0,4},{4,0},{8,12},{12,8},{16,20},{20,16},{24,28},{28,24},{1,5},{5... | collective-permute-start | bytes 294920 | tf_op jit(solution)/shard_map/ppermute | solution.py:321
  17.9 6.6 %collective-permute-start.6 = (f16[272,128]{1,0:T(8,128)(2,1)S(1)}, f16[272,128]{1,0:T(8,128)(2,1)S(1)}, u32[]{:S(2)}, u32[]{:S(2)}) collective-permute-start(f16[272,128]{1,0:T(8,128)(2,1)S(1)} %pad_maximum_fusion.2), channel_id=1, source_target_pairs={{0,3},{1,2},{2,1},{3,0},{4,7},{5,6},{6,5},{7,4},{8,11},{9,10},{10,... | collective-permute-start | bytes 208904 | tf_op jit(solution)/shard_map/ppermute | solution.py:322
  21.8 7.0 %collective-permute-start.5 = (f16[544,128]{1,0:T(8,128)(2,1)S(1)}, f16[544,128]{1,0:T(8,128)(2,1)S(1)}, u32[]{:S(2)}, u32[]{:S(2)}) collective-permute-start(f16[544,128]{1,0:T(8,128)(2,1)S(1)} %constant_dynamic-update-slice_fusion), channel_id=1, source_target_pairs={{0,1},{1,0},{2,3},{3,2},{4,6},{5,7},{6,4},{7,5},{8,9},{9,8},{10,11... | collective-permute-start | bytes 417800 | tf_op jit(solution)/shard_map/ppermute | solution.py:329
  24.6 1.4 %collective-permute-start.7 = (bf16[384,128]{1,0:T(8,128)(2,1)S(1)}, bf16[384,128]{1,0:T(8,128)(2,1)S(1)}, u32[]{:S(2)}, u32[]{:S(2)}) collective-permute-start(bf16[384,128]{1,0:T(8,128)(2,1)S(1)} %pad_maximum_fusion.1.refs_0_), channel_id=1, source_target_pairs={{0,4},{4,0},{8,12},{12,8},{16,20},{20,16},{24,28},{28,24},{1,5},{5... | collective-permute-start | bytes 294920 | tf_op jit(solution)/shard_map/ppermute | solution.py:333
  29.0 1.5 %collective-permute-start.8 = (bf16[768,128]{1,0:T(8,128)(2,1)S(1)}, bf16[768,128]{1,0:T(8,128)(2,1)S(1)}, u32[]{:S(2)}, u32[]{:S(2)}) collective-permute-start(bf16[768,128]{1,0:T(8,128)(2,1)S(1)} %fusion.10.refs_0_), channel_id=1, source_target_pairs={{0,4},{4,0},{8,12},{12,8},{16,20},{20,16},{24,28},{28,24},{1,5},{5... | collective-permute-start | bytes 589832 | tf_op jit(solution)/shard_map/ppermute | solution.py:337

commit v6 on v5

--- a/solution.py
+++ b/solution.py
@@ -8,9 +8,9 @@
 from jax.sharding import PartitionSpec as P
 
 TILE = 256
-ROWS = 352
-COLS = 768
-CHUNKS = 8
+BLOCK = (528, 1152)
+LAST_BLOCK = (352, 768)
+CHUNKS = (12,12,12,12,8,4,4)
 MIB = 1 << 20
 
 
@@ -39,10 +39,9 @@
 
 
 def project_kernel(chunks, basis_hbm, snap_hbm, rate_hbm, keep_ref, send_ref, basis, snap, rate, acc, sems):
-    rows = basis.shape[0] // chunks
     copies = []
-    for c in range(chunks):
-        part = pl.ds(c * rows, rows)
+    for c, chunk in enumerate(chunks):
+        part = pl.ds(*chunk)
         copies.append(
             [
                 pltpu.make_async_copy(source.at[part], target.at[part], sems.at[k, c])
@@ -51,10 +50,10 @@
         )
         for copy in copies[-1]:
             copy.start()
-    for c in range(chunks):
+    for c, chunk in enumerate(chunks):
         for copy in copies[c]:
             copy.wait()
-        part = pl.ds(c * rows, rows)
+        part = pl.ds(*chunk)
         left = basis[part, :].T
         for k, array in enumerate((snap, rate)):
             product = jnp.dot(left, array[part, :], preferred_element_type=jnp.float32)
@@ -74,7 +73,9 @@
 def project(basis, snapshots, rates):
     rows, rank = basis.shape
     times = snapshots.shape[1]
-    chunks = CHUNKS if rows % (16 * CHUNKS) == 0 else 1
+    chunks, unit = [(0, rows)], rows // sum(CHUNKS)
+    if unit * sum(CHUNKS) == rows and unit % 16 == 0:
+        chunks = [(unit * sum(CHUNKS[:c]), unit * size) for c, size in enumerate(CHUNKS)]
     out = pltpu.VMEM((2 * rank, times // 2), jnp.float32)
     return pl.pallas_call(
         functools.partial(project_kernel, chunks),
@@ -86,7 +87,7 @@
             pltpu.VMEM((rows, times), jnp.bfloat16),
             pltpu.VMEM((rows, times), jnp.bfloat16),
             pltpu.VMEM((2, rank, times), jnp.float32),
-            pltpu.SemaphoreType.DMA((3, chunks)),
+            pltpu.SemaphoreType.DMA((3, len(chunks))),
         ],
         compiler_params=pltpu.CompilerParams(vmem_limit_bytes=24 * MIB),
         cost_estimate=pl.CostEstimate(
@@ -158,13 +159,14 @@
 
 def fill_rows(row_width, pick, states, row_feat, columns):
     first = lax.axis_index("rows") * row_width
-    for low, size in spans(row_feat.shape[0], ROWS):
+    for low, size in spans(row_feat.shape[0], BLOCK[0]):
         row_feat[low : low + size, columns] = feature_rows(first + low, pick[low : low + size], states[...])
 
 
 def fill_columns(col_width, pick, states, moments, col_feat, left, right, columns):
     first, end = lax.axis_index("reg") * col_width, min(right, pick.shape[0])
-    col_feat[left:end, columns] = feature_rows(first + left, pick[left:end], states[...])
+    if left < end:
+        col_feat[left:end, columns] = feature_rows(first + left, pick[left:end], states[...])
     if end < right:
         col_feat[end:right, columns] = moments[...]
 
@@ -175,7 +177,7 @@
         ref[...] = jnp.zeros_like(ref)
     lay_out(pieces, states, moments)
     fill_rows(row_width, row_pick, states, row_feat, slice(None))
-    for left, width in spans(col_feat.shape[0], COLS):
+    for left, width in spans(col_feat.shape[0], BLOCK[1]):
         fill_columns(col_width, col_pick, states, moments, col_feat, left, left + width, slice(None))
 
 
@@ -208,12 +210,12 @@
     fill_rows(row_width, row_pick, states, row_feat, columns)
     if ready:
         row_feat[:, before] = row_ready[...]
-    copies = []
-    for left, width in spans(col_pad, COLS):
+    copies, block_size = [], LAST_BLOCK if total_time else BLOCK
+    for left, width in spans(col_pad, block_size[1]):
         fill_columns(col_width, col_pick, states, moments, col_feat, left, left + width, columns)
         if ready:
             col_feat[left : left + width, before] = col_ready[left : left + width]
-        for low, size in spans(row_pad, ROWS):
+        for low, size in spans(row_pad, block_size[0]):
             block = lax.dot_general(
                 row_feat[low : low + size], col_feat[left : left + width], (((1,), (1,)), ((), ())),
                 preferred_element_type=jnp.float32,
@@ -261,7 +263,7 @@
         scratch = [
             pltpu.VMEM((row_width, col_width), jnp.float32),
             pltpu.VMEM((row_width, rank), jnp.float32),
-            pltpu.SemaphoreType.DMA((len(spans(row_pad, ROWS)) * (len(spans(col_pad, COLS)) + 1),)),
+            pltpu.SemaphoreType.DMA((len(spans(row_pad, LAST_BLOCK[0])) * (len(spans(col_pad, LAST_BLOCK[1])) + 1),)),
         ] + scratch
     return pl.pallas_call(
         functools.partial(sum_kernel, len(pieces), len(place), bool(held), bool(ready), total_time, row_width, col_width),
@@ -286,15 +288,15 @@
 
 
 def decode(coded, rank):
-    coded = coded.astype(jnp.float32)
-    states = coded[:rank] * jnp.exp2(coded[2 * rank : 2 * rank + 1])
-    moments = coded[rank : 2 * rank] * jnp.exp2(coded[2 * rank + 1 : 2 * rank + 2])
-    return split(states, moments)
+    coded = coded.astype(jnp.float32).reshape(-1, 2 * rank + 16, coded.shape[1])
+    states = coded[:, :rank] * jnp.exp2(coded[:, 2 * rank : 2 * rank + 1])
+    moments = coded[:, rank : 2 * rank] * jnp.exp2(coded[:, 2 * rank + 1 : 2 * rank + 2])
+    return split(states, moments).reshape(-1, coded.shape[2])
 
 
 def split(states, moments):
     high = lax.reduce_precision(states, 8, 7)
-    return jnp.concatenate([high, states - high, moments]).astype(jnp.bfloat16)
+    return jnp.concatenate([high, states - high, moments], axis=-2).astype(jnp.bfloat16)
 
 
 def per_device(snapshots, rates, basis):
@@ -309,9 +311,11 @@
     swap = [(i, i ^ 1) for i in range(size_rows)]
     keep, send = project(basis, snapshots, rates)
     chip = keep + lax.ppermute(send, "rows", swap)
-    plane = [[(2 * a + c, 2 * b + c) for a, b in perm for c in range(2)] for perm in partners(size_rows // 2)]
+    chips = size_rows // 2
     total = chip
-    for perm in plane:
+    for k in range(1, chips):
+        turned = k ^ 3 if chips % 4 == 0 and k % 4 in (1, 2) else k
+        perm = [(n, n ^ 2 * (turned if n % 2 else k)) for n in range(size_rows)]
         total = total + lax.ppermute(chip, "rows", perm)
     *picks, zero = select(chip, *shape)
     total = total + zero
@@ -328,14 +332,13 @@
         perm = [(n, row * size_reg + (reg ^ (k + row % 2))) for n, (row, reg) in enumerate(places)]
         far.append(lax.ppermute(whole, ("rows", "reg"), perm))
     *held, zero = add_up(picks, [], own, [], [], None, coded.shape, LONG, *shape)
-    near = decode(near + zero.astype(coded.dtype), rank)
+    near = near + zero.astype(coded.dtype)
     waiting = (len(far) * whole.shape[0], whole.shape[1])
-    pieces = [near, lax.ppermute(near, "rows", swap)]
+    pieces = [decode(piece, rank) for piece in (near, lax.ppermute(near, "rows", swap))]
     *held, zero = add_up(picks, [place], pieces, held, [], None, waiting, FREE, *shape)
     far = jnp.concatenate(far) + zero.astype(coded.dtype)
-    far = jnp.concatenate([decode(slab, rank) for slab in jnp.split(far, size_reg - 2)])
-    other = lax.ppermute(far, "rows", swap)
-    ready = prepare(picks, [far], [], FREE, *shape)
+    other = decode(lax.ppermute(far, "rows", swap), rank)
+    ready = prepare(picks, [decode(far, rank)], [], FREE, *shape)
     return tuple(add_up(picks, [place], [other], held, ready, total_time, None, FREE, *shape))
 
 

time: 35.6 us -> 35.2 us (0.989)
  Pallas kernels: 17 us -> 16.5 us
    ppermute x3, waiting for transfers between devices: 5.14 us -> 6.28 us  [per_device(): total = total + lax.ppermute(chip, 'rows', perm)]
    ppermute x1, waiting for transfers between devices: 0.99 us -> 0.01 us  [per_device(): chip = keep + lax.ppermute(send, 'rows', swap)]
    pallas_call x3, Pallas kernels: 10.3 us -> 9.9 us  [add_up(): pl.pallas_call(functools.partial(sum_kernel, len(pieces), len(place), boo...]
  transfers between devices with their start and end apart: 9 -> 9, of which waited for: 7 -> 5; matrix products, arithmetic and copies ran while one was open for 2% -> 2% of each run, Pallas kernels for 21% -> 20%
where the time goes in v6:
time: 35.2 us; the launch traced here: 35 us
  Pallas kernels  16.5 us (47%)
  starting transfers between devices  8.94 us (25%)
  waiting for transfers between devices  7.8 us (22%)
  other arithmetic  0.94 us (3%)
  between operations  0.89 us (3%)
    pallas_call x3, Pallas kernels, add_up(): pl.pallas_call(functools.partial(sum_kernel, len(pieces), len(place), boo...  9.9 us
    ppermute x3, waiting for transfers between devices, per_device(): total = total + lax.ppermute(chip, 'rows', perm)  6.28 us
    pallas_call x1, Pallas kernels, project(): pl.pallas_call(functools.partial(project_kernel, chunks), in_specs=[ANYWH...  4.44 us
    ppermute x3, starting transfers between devices, per_device(): total = total + lax.ppermute(chip, 'rows', perm)  4.39 us
    ppermute x1, starting transfers between devices, per_device(): lax.ppermute(coded, 'reg', [(n, size_reg - 1 - n) for n in range(size_reg)])  3.66 us
    ppermute x1, waiting for transfers between devices, per_device(): lax.ppermute(near, 'rows', swap)  1.2 us
    pallas_call x1, Pallas kernels, select(): pl.pallas_call(functools.partial(select_kernel, row_width, col_width), ou...  1.08 us
    pallas_call x1, Pallas kernels, prepare(): pl.pallas_call(functools.partial(prepare_kernel, len(pieces), row_width,...  1.05 us
  transfers between devices with their start and end apart: 9, of which 5 were waited for; matrix products, arithmetic and copies ran while one was open for 2% of the time, Pallas kernels for 20%

profile of v6, /device:TPU:0, one launch (start us, length us, event | category | flops | bytes accessed | tf_op | source)
XLA Modules:
  0.0 35.0 jit_solution(9085108824972055795)
XLA Ops:
  0.6 4.4 %project.1 = (f32[256,128]{1,0:T(8,128)S(1)}, f32[256,128]{1,0:T(8,128)S(1)}) custom-call(bf16[8192,128]{1,0:T(8,128)(2,1)} %basis_hbm.1, bf16[8192,256]{1,0:T(8,128)(2,1)} %snap_hbm.1, bf16[8192,256]{1,0:T(8,128)(2,1)} %rate_hbm.1), custom_call_target="tpu_custom_call" | custom-call | flops 1073741824 | bytes 10485760 | tf_op jit(solution)/shard_map/project/pallas_call | solution.py:80
  5.1 0.5 %collective-permute-start = (f32[256,128]{1,0:T(8,128)S(1)}, f32[256,128]{1,0:T(8,128)S(1)}, u32[]{:S(2)}, u32[]{:S(2)}) collective-permute-start(f32[256,128]{1,0:T(8,128)S(1)} %get-tuple-element.14), channel_id=1, source_target_pairs={{0,4},{4,0},{8,12},{12,8},{16,20},{20,16},{24,28},{28,24},{1,5},{5... | collective-permute-start | bytes 393224 | tf_op jit(solution)/shard_map/ppermute | solution.py:313
  5.6 1.1 %select.1 = (bf16[1056,256]{1,0:T(8,128)(2,1)S(1)}, bf16[2176,256]{1,0:T(8,128)(2,1)S(1)}, f32[256,128]{1,0:T(8,128)S(1)}) custom-call(), custom_call_target="tpu_custom_call" | custom-call | flops 20000000000 | tf_op jit(solution)/shard_map/select/pallas_call | solution.py:121
  6.7 0.0 collective-permute-done
  6.7 3.7 %collective-permute-start.3 = (f32[256,128]{1,0:T(8,128)S(1)}, f32[256,128]{1,0:T(8,128)S(1)}, u32[]{:S(2)}, u32[]{:S(2)}) collective-permute-start(f32[256,128]{1,0:T(8,128)S(1)} %add.24), channel_id=1, source_target_pairs={{0,24},{4,28},{8,16},{12,20},{16,8},{20,12},{24,0},{28,4},{1,25},{... | collective-permute-start | bytes 393224 | tf_op jit(solution)/shard_map/ppermute | solution.py:319
  10.5 0.5 %collective-permute-start.2 = (f32[256,128]{1,0:T(8,128)S(1)}, f32[256,128]{1,0:T(8,128)S(1)}, u32[]{:S(2)}, u32[]{:S(2)}) collective-permute-start(f32[256,128]{1,0:T(8,128)S(1)} %add.24), channel_id=1, source_target_pairs={{0,16},{4,12},{8,24},{12,4},{16,0},{20,28},{24,8},{28,20},{1,17},{... | collective-permute-start | bytes 393224 | tf_op jit(solution)/shard_map/ppermute | solution.py:319
  11.0 0.1 collective-permute-start.1
  11.1 0.1 pad_add_fusion.refs_3_.refs_4_
  11.2 3.5 %collective-permute-done.3 = f32[256,128]{1,0:T(8,128)S(1)} collective-permute-done((f32[256,128]{1,0:T(8,128)S(1)}, f32[256,128]{1,0:T(8,128)S(1)}, u32[]{:S(2)}, u32[]{:S(2)}) %collective-permute-start.3) | collective-permute-done | bytes 131104 | tf_op jit(solution)/shard_map/ppermute | solution.py:319
  14.7 2.5 %collective-permute-done.2 = f32[256,128]{1,0:T(8,128)S(1)} collective-permute-done((f32[256,128]{1,0:T(8,128)S(1)}, f32[256,128]{1,0:T(8,128)S(1)}, u32[]{:S(2)}, u32[]{:S(2)}) %collective-permute-start.2) | collective-permute-done | bytes 131104 | tf_op jit(solution)/shard_map/ppermute | solution.py:319
  17.2 0.3 collective-permute-done.1
  17.6 0.1 collective-permute-start.4
  17.7 0.1 select_convert_fusion.1
  17.8 0.1 constant_dynamic-update-slice_fusion.1
  17.9 3.7 %collective-permute-start.6 = (f16[272,128]{1,0:T(8,128)(2,1)S(1)}, f16[272,128]{1,0:T(8,128)(2,1)S(1)}, u32[]{:S(2)}, u32[]{:S(2)}) collective-permute-start(f16[272,128]{1,0:T(8,128)(2,1)S(1)} %pad_maximum_fusion.5), channel_id=1, source_target_pairs={{0,3},{1,2},{2,1},{3,0},{4,7},{5,6},{6,5},{7,4},{8,11},{9,10},{10,... | collective-permute-start | bytes 208904 | tf_op jit(solution)/shard_map/ppermute | solution.py:326
  21.6 0.0 collective-permute-done.4.refs_1_
  21.7 0.1 constant_dynamic-update-slice_fusion
  21.8 0.0 collective-permute-start.5
  21.8 2.4 %add_up.2 = (f32[1056,2304]{1,0:T(8,128)S(1)}, bf16[272,128]{1,0:T(8,128)(2,1)S(1)}) custom-call(bf16[384,128]{1,0:T(8,128)(2,1)S(1)} %pad_maximum_fusion.2.refs_0_, bf16[384,128]{1,0:T(8,128)(2,1)S(1)} %collective-permute-done.4.refs_1_, bf16[1056,256]{1,0:T(8,128)(2,1)S(1)} %get-tuple-element.16.refs_2_.refs_4_.refs_1_.refs_5_, ...), custom_call_target="tpu_custom_call" | custom-call | flops 20000000000 | tf_op jit(solution)/shard_map/add_up/pallas_call | solution.py:268
  24.3 0.3 collective-permute-done.6
  24.6 0.1 collective-permute-start.7
  24.7 1.2 %collective-permute-done.7 = f16[272,128]{1,0:T(8,128)(2,1)S(1)} collective-permute-done((f16[272,128]{1,0:T(8,128)(2,1)S(1)}, f16[272,128]{1,0:T(8,128)(2,1)S(1)}, u32[]{:S(2)}, u32[]{:S(2)}) %collective-permute-start.7) | collective-permute-done | bytes 69664 | tf_op jit(solution)/shard_map/ppermute | solution.py:337
  26.0 2.5 %add_up.3 = (f32[1056,2304]{1,0:T(8,128)S(1)}, bf16[544,128]{1,0:T(8,128)(2,1)S(1)}) custom-call(bf16[384,128]{1,0:T(8,128)(2,1)S(1)} %pad_maximum_fusion.3.refs_0_, bf16[384,128]{1,0:T(8,128)(2,1)S(1)} %pad_maximum_fusion.4.refs_1_, f32[1056,2304]{1,0:T(8,128)S(1)} %get-tuple-element.19.refs_2_, s32[2]{0:T(128)S(1)} %pad_add_fusion.refs_3_.refs_4_, ...), custom_call_target="tpu_custom_call" | custom-call | tf_op jit(solution)/shard_map/add_up/pallas_call | solution.py:268
  28.5 0.0 collective-permute-done.5
  28.5 0.1 convert_add_fusion
  28.5 0.2 collective-permute-start.8
  28.9 1.1 %prepare.1 = (bf16[1056,256]{1,0:T(8,128)(2,1)S(1)}, bf16[2304,256]{1,0:T(8,128)(2,1)S(1)}) custom-call(bf16[768,128]{1,0:T(8,128)(2,1)S(1)} %bitcast.38, bf16[1056,256]{1,0:T(8,128)(2,1)S(1)} %get-tuple-element.16.refs_2_.refs_4_.refs_1_.refs_5_, bf16[2176,256]{1,0:T(8,128)(2,1)S(1)} %get-tuple-element.17.refs_3_.refs_5_.refs_2_.refs_6_), custom_call_target="tpu_custom_call" | custom-call | tf_op jit(solution)/shard_map/prepare/pallas_call | solution.py:187
  29.9 0.0 collective-permute-done.8
  30.1 5.0 %add_up_last.1 = (f32[1048,2096]{1,0:T(8,128)}, f32[1048,128]{1,0:T(8,128)}) custom-call(bf16[768,128]{1,0:T(8,128)(2,1)S(1)} %bitcast.39, f32[1056,2304]{1,0:T(8,128)S(1)} %get-tuple-element.21.refs_1_, bf16[1056,256]{1,0:T(8,128)(2,1)S(1)} %get-tuple-element.22.refs_2_, bf16[2304,256]{1,0:T(8,128)(2,1)S(1)} %get-tuple-element.23.refs_3_, ...), custom_call_target="tpu_custom_call" | custom-call | tf_op jit(solution)/shard_map/add_up_last/pallas_call | solution.py:268
  (31 shorter events, 0.6 us)
Async XLA Ops:
  5.1 1.6 %collective-permute-start = (f32[256,128]{1,0:T(8,128)S(1)}, f32[256,128]{1,0:T(8,128)S(1)}, u32[]{:S(2)}, u32[]{:S(2)}) collective-permute-start(f32[256,128]{1,0:T(8,128)S(1)} %get-tuple-element.14), channel_id=1, source_target_pairs={{0,4},{4,0},{8,12},{12,8},{16,20},{20,16},{24,28},{28,24},{1,5},{5... | collective-permute-start | bytes 393224 | tf_op jit(solution)/shard_map/ppermute | solution.py:313
  6.7 8.0 %collective-permute-start.3 = (f32[256,128]{1,0:T(8,128)S(1)}, f32[256,128]{1,0:T(8,128)S(1)}, u32[]{:S(2)}, u32[]{:S(2)}) collective-permute-start(f32[256,128]{1,0:T(8,128)S(1)} %add.24), channel_id=1, source_target_pairs={{0,24},{4,28},{8,16},{12,20},{16,8},{20,12},{24,0},{28,4},{1,25},{... | collective-permute-start | bytes 393224 | tf_op jit(solution)/shard_map/ppermute | solution.py:319
  10.5 6.7 %collective-permute-start.2 = (f32[256,128]{1,0:T(8,128)S(1)}, f32[256,128]{1,0:T(8,128)S(1)}, u32[]{:S(2)}, u32[]{:S(2)}) collective-permute-start(f32[256,128]{1,0:T(8,128)S(1)} %add.24), channel_id=1, source_target_pairs={{0,16},{4,12},{8,24},{12,4},{16,0},{20,28},{24,8},{28,20},{1,17},{... | collective-permute-start | bytes 393224 | tf_op jit(solution)/shard_map/ppermute | solution.py:319
  11.0 6.5 %collective-permute-start.1 = (f32[256,128]{1,0:T(8,128)S(1)}, f32[256,128]{1,0:T(8,128)S(1)}, u32[]{:S(2)}, u32[]{:S(2)}) collective-permute-start(f32[256,128]{1,0:T(8,128)S(1)} %add.24), channel_id=1, source_target_pairs={{0,8},{4,20},{8,0},{12,28},{16,24},{20,4},{24,16},{28,12},{1,9},{5... | collective-permute-start | bytes 393224 | tf_op jit(solution)/shard_map/ppermute | solution.py:319
  17.6 4.0 %collective-permute-start.4 = (bf16[384,128]{1,0:T(8,128)(2,1)S(1)}, bf16[384,128]{1,0:T(8,128)(2,1)S(1)}, u32[]{:S(2)}, u32[]{:S(2)}) collective-permute-start(bf16[384,128]{1,0:T(8,128)(2,1)S(1)} %pad_maximum_fusion.2.refs_0_), channel_id=1, source_target_pairs={{0,4},{4,0},{8,12},{12,8},{16,20},{20,16},{24,28},{28,24},{1,5},{5... | collective-permute-start | bytes 294920 | tf_op jit(solution)/shard_map/ppermute | solution.py:325
  17.9 6.6 %collective-permute-start.6 = (f16[272,128]{1,0:T(8,128)(2,1)S(1)}, f16[272,128]{1,0:T(8,128)(2,1)S(1)}, u32[]{:S(2)}, u32[]{:S(2)}) collective-permute-start(f16[272,128]{1,0:T(8,128)(2,1)S(1)} %pad_maximum_fusion.5), channel_id=1, source_target_pairs={{0,3},{1,2},{2,1},{3,0},{4,7},{5,6},{6,5},{7,4},{8,11},{9,10},{10,... | collective-permute-start | bytes 208904 | tf_op jit(solution)/shard_map/ppermute | solution.py:326
  21.8 6.7 %collective-permute-start.5 = (f16[544,128]{1,0:T(8,128)(2,1)S(1)}, f16[544,128]{1,0:T(8,128)(2,1)S(1)}, u32[]{:S(2)}, u32[]{:S(2)}) collective-permute-start(f16[544,128]{1,0:T(8,128)(2,1)S(1)} %constant_dynamic-update-slice_fusion), channel_id=1, source_target_pairs={{0,1},{1,0},{2,3},{3,2},{4,6},{5,7},{6,4},{7,5},{8,9},{9,8},{10,11... | collective-permute-start | bytes 417800 | tf_op jit(solution)/shard_map/ppermute | solution.py:333
  24.6 1.3 %collective-permute-start.7 = (f16[272,128]{1,0:T(8,128)(2,1)S(1)}, f16[272,128]{1,0:T(8,128)(2,1)S(1)}, u32[]{:S(2)}, u32[]{:S(2)}) collective-permute-start(f16[272,128]{1,0:T(8,128)(2,1)S(1)} %get-tuple-element.29), channel_id=1, source_target_pairs={{0,4},{4,0},{8,12},{12,8},{16,20},{20,16},{24,28},{28,24},{1,5},{5... | collective-permute-start | bytes 208904 | tf_op jit(solution)/shard_map/ppermute | solution.py:337
  28.5 1.4 %collective-permute-start.8 = (f16[544,128]{1,0:T(8,128)(2,1)S(1)}, f16[544,128]{1,0:T(8,128)(2,1)S(1)}, u32[]{:S(2)}, u32[]{:S(2)}) collective-permute-start(f16[544,128]{1,0:T(8,128)(2,1)S(1)} %convert_add_fusion), channel_id=1, source_target_pairs={{0,4},{4,0},{8,12},{12,8},{16,20},{20,16},{24,28},{28,24},{1,5},{5... | collective-permute-start | bytes 417800 | tf_op jit(solution)/shard_map/ppermute | solution.py:340

commit v7 on v6

--- a/solution.py
+++ b/solution.py
@@ -8,7 +8,7 @@
 from jax.sharding import PartitionSpec as P
 
 TILE = 256
-BLOCK = (528, 1152)
+BLOCK = (528, 2304)
 LAST_BLOCK = (352, 768)
 CHUNKS = (12,12,12,12,8,4,4)
 MIB = 1 << 20

time: 35.2 us -> 35.1 us (level)
  no operation moved by 1% of the time
where the time goes in v7:
time: 35.1 us; the launch traced here: 35 us
  Pallas kernels  16.3 us (46%)
  starting transfers between devices  8.94 us (25%)
  waiting for transfers between devices  7.94 us (23%)
  other arithmetic  0.94 us (3%)
  between operations  0.89 us (3%)
    pallas_call x3, Pallas kernels, add_up(): pl.pallas_call(functools.partial(sum_kernel, len(pieces), len(place), boo...  9.68 us
    ppermute x3, waiting for transfers between devices, per_device(): total = total + lax.ppermute(chip, 'rows', perm)  6.28 us
    pallas_call x1, Pallas kernels, project(): pl.pallas_call(functools.partial(project_kernel, chunks), in_specs=[ANYWH...  4.44 us
    ppermute x3, starting transfers between devices, per_device(): total = total + lax.ppermute(chip, 'rows', perm)  4.39 us
    ppermute x1, starting transfers between devices, per_device(): lax.ppermute(coded, 'reg', [(n, size_reg - 1 - n) for n in range(size_reg)])  3.66 us
    ppermute x1, waiting for transfers between devices, per_device(): lax.ppermute(near, 'rows', swap)  1.2 us
    pallas_call x1, Pallas kernels, select(): pl.pallas_call(functools.partial(select_kernel, row_width, col_width), ou...  1.08 us
    pallas_call x1, Pallas kernels, prepare(): pl.pallas_call(functools.partial(prepare_kernel, len(pieces), row_width,...  1.05 us
  transfers between devices with their start and end apart: 9, of which 5 were waited for; matrix products, arithmetic and copies ran while one was open for 2% of the time, Pallas kernels for 20%

profile of v7, /device:TPU:0, one launch (start us, length us, event | category | flops | bytes accessed | tf_op | source)
XLA Modules:
  0.0 35.0 jit_solution(10034306904123970609)
XLA Ops:
  0.6 4.4 %project.1 = (f32[256,128]{1,0:T(8,128)S(1)}, f32[256,128]{1,0:T(8,128)S(1)}) custom-call(bf16[8192,128]{1,0:T(8,128)(2,1)} %basis_hbm.1, bf16[8192,256]{1,0:T(8,128)(2,1)} %snap_hbm.1, bf16[8192,256]{1,0:T(8,128)(2,1)} %rate_hbm.1), custom_call_target="tpu_custom_call" | custom-call | flops 1073741824 | bytes 10485760 | tf_op jit(solution)/shard_map/project/pallas_call | solution.py:80
  5.1 0.5 %collective-permute-start = (f32[256,128]{1,0:T(8,128)S(1)}, f32[256,128]{1,0:T(8,128)S(1)}, u32[]{:S(2)}, u32[]{:S(2)}) collective-permute-start(f32[256,128]{1,0:T(8,128)S(1)} %get-tuple-element.14), channel_id=1, source_target_pairs={{0,4},{4,0},{8,12},{12,8},{16,20},{20,16},{24,28},{28,24},{1,5},{5... | collective-permute-start | bytes 393224 | tf_op jit(solution)/shard_map/ppermute | solution.py:313
  5.6 1.1 %select.1 = (bf16[1056,256]{1,0:T(8,128)(2,1)S(1)}, bf16[2176,256]{1,0:T(8,128)(2,1)S(1)}, f32[256,128]{1,0:T(8,128)S(1)}) custom-call(), custom_call_target="tpu_custom_call" | custom-call | flops 20000000000 | tf_op jit(solution)/shard_map/select/pallas_call | solution.py:121
  6.7 0.0 collective-permute-done
  6.7 3.7 %collective-permute-start.3 = (f32[256,128]{1,0:T(8,128)S(1)}, f32[256,128]{1,0:T(8,128)S(1)}, u32[]{:S(2)}, u32[]{:S(2)}) collective-permute-start(f32[256,128]{1,0:T(8,128)S(1)} %add.24), channel_id=1, source_target_pairs={{0,24},{4,28},{8,16},{12,20},{16,8},{20,12},{24,0},{28,4},{1,25},{... | collective-permute-start | bytes 393224 | tf_op jit(solution)/shard_map/ppermute | solution.py:319
  10.5 0.5 %collective-permute-start.2 = (f32[256,128]{1,0:T(8,128)S(1)}, f32[256,128]{1,0:T(8,128)S(1)}, u32[]{:S(2)}, u32[]{:S(2)}) collective-permute-start(f32[256,128]{1,0:T(8,128)S(1)} %add.24), channel_id=1, source_target_pairs={{0,16},{4,12},{8,24},{12,4},{16,0},{20,28},{24,8},{28,20},{1,17},{... | collective-permute-start | bytes 393224 | tf_op jit(solution)/shard_map/ppermute | solution.py:319
  11.0 0.1 collective-permute-start.1
  11.1 0.1 pad_add_fusion.refs_3_.refs_4_
  11.2 3.5 %collective-permute-done.3 = f32[256,128]{1,0:T(8,128)S(1)} collective-permute-done((f32[256,128]{1,0:T(8,128)S(1)}, f32[256,128]{1,0:T(8,128)S(1)}, u32[]{:S(2)}, u32[]{:S(2)}) %collective-permute-start.3) | collective-permute-done | bytes 131104 | tf_op jit(solution)/shard_map/ppermute | solution.py:319
  14.7 2.5 %collective-permute-done.2 = f32[256,128]{1,0:T(8,128)S(1)} collective-permute-done((f32[256,128]{1,0:T(8,128)S(1)}, f32[256,128]{1,0:T(8,128)S(1)}, u32[]{:S(2)}, u32[]{:S(2)}) %collective-permute-start.2) | collective-permute-done | bytes 131104 | tf_op jit(solution)/shard_map/ppermute | solution.py:319
  17.2 0.3 collective-permute-done.1
  17.6 0.1 collective-permute-start.4
  17.7 0.1 select_convert_fusion.1
  17.8 0.1 constant_dynamic-update-slice_fusion.1
  17.9 3.7 %collective-permute-start.6 = (f16[272,128]{1,0:T(8,128)(2,1)S(1)}, f16[272,128]{1,0:T(8,128)(2,1)S(1)}, u32[]{:S(2)}, u32[]{:S(2)}) collective-permute-start(f16[272,128]{1,0:T(8,128)(2,1)S(1)} %pad_maximum_fusion.5), channel_id=1, source_target_pairs={{0,3},{1,2},{2,1},{3,0},{4,7},{5,6},{6,5},{7,4},{8,11},{9,10},{10,... | collective-permute-start | bytes 208904 | tf_op jit(solution)/shard_map/ppermute | solution.py:326
  21.6 0.0 collective-permute-done.4.refs_1_
  21.7 0.1 constant_dynamic-update-slice_fusion
  21.8 0.0 collective-permute-start.5
  21.8 2.3 %add_up.2 = (f32[1056,2304]{1,0:T(8,128)S(1)}, bf16[272,128]{1,0:T(8,128)(2,1)S(1)}) custom-call(bf16[384,128]{1,0:T(8,128)(2,1)S(1)} %pad_maximum_fusion.2.refs_0_, bf16[384,128]{1,0:T(8,128)(2,1)S(1)} %collective-permute-done.4.refs_1_, bf16[1056,256]{1,0:T(8,128)(2,1)S(1)} %get-tuple-element.16.refs_2_.refs_4_.refs_1_.refs_5_, ...), custom_call_target="tpu_custom_call" | custom-call | flops 20000000000 | tf_op jit(solution)/shard_map/add_up/pallas_call | solution.py:268
  24.1 0.4 %collective-permute-done.6 = f16[272,128]{1,0:T(8,128)(2,1)S(1)} collective-permute-done((f16[272,128]{1,0:T(8,128)(2,1)S(1)}, f16[272,128]{1,0:T(8,128)(2,1)S(1)}, u32[]{:S(2)}, u32[]{:S(2)}) %collective-permute-start.6) | collective-permute-done | bytes 69664 | tf_op jit(solution)/shard_map/ppermute | solution.py:326
  24.6 0.1 collective-permute-start.7
  24.7 1.2 %collective-permute-done.7 = f16[272,128]{1,0:T(8,128)(2,1)S(1)} collective-permute-done((f16[272,128]{1,0:T(8,128)(2,1)S(1)}, f16[272,128]{1,0:T(8,128)(2,1)S(1)}, u32[]{:S(2)}, u32[]{:S(2)}) %collective-permute-start.7) | collective-permute-done | bytes 69664 | tf_op jit(solution)/shard_map/ppermute | solution.py:337
  26.0 2.4 %add_up.3 = (f32[1056,2304]{1,0:T(8,128)S(1)}, bf16[544,128]{1,0:T(8,128)(2,1)S(1)}) custom-call(bf16[384,128]{1,0:T(8,128)(2,1)S(1)} %pad_maximum_fusion.3.refs_0_, bf16[384,128]{1,0:T(8,128)(2,1)S(1)} %pad_maximum_fusion.4.refs_1_, f32[1056,2304]{1,0:T(8,128)S(1)} %get-tuple-element.19.refs_2_, s32[2]{0:T(128)S(1)} %pad_add_fusion.refs_3_.refs_4_, ...), custom_call_target="tpu_custom_call" | custom-call | tf_op jit(solution)/shard_map/add_up/pallas_call | solution.py:268
  28.4 0.0 collective-permute-done.5
  28.4 0.1 convert_add_fusion
  28.5 0.2 collective-permute-start.8
  28.8 1.1 %prepare.1 = (bf16[1056,256]{1,0:T(8,128)(2,1)S(1)}, bf16[2304,256]{1,0:T(8,128)(2,1)S(1)}) custom-call(bf16[768,128]{1,0:T(8,128)(2,1)S(1)} %bitcast.38, bf16[1056,256]{1,0:T(8,128)(2,1)S(1)} %get-tuple-element.16.refs_2_.refs_4_.refs_1_.refs_5_, bf16[2176,256]{1,0:T(8,128)(2,1)S(1)} %get-tuple-element.17.refs_3_.refs_5_.refs_2_.refs_6_), custom_call_target="tpu_custom_call" | custom-call | tf_op jit(solution)/shard_map/prepare/pallas_call | solution.py:187
  29.9 0.0 collective-permute-done.8
  30.0 5.0 %add_up_last.1 = (f32[1048,2096]{1,0:T(8,128)}, f32[1048,128]{1,0:T(8,128)}) custom-call(bf16[768,128]{1,0:T(8,128)(2,1)S(1)} %bitcast.39, f32[1056,2304]{1,0:T(8,128)S(1)} %get-tuple-element.21.refs_1_, bf16[1056,256]{1,0:T(8,128)(2,1)S(1)} %get-tuple-element.22.refs_2_, bf16[2304,256]{1,0:T(8,128)(2,1)S(1)} %get-tuple-element.23.refs_3_, ...), custom_call_target="tpu_custom_call" | custom-call | tf_op jit(solution)/shard_map/add_up_last/pallas_call | solution.py:268
  (31 shorter events, 0.6 us)
Async XLA Ops:
  5.1 1.6 %collective-permute-start = (f32[256,128]{1,0:T(8,128)S(1)}, f32[256,128]{1,0:T(8,128)S(1)}, u32[]{:S(2)}, u32[]{:S(2)}) collective-permute-start(f32[256,128]{1,0:T(8,128)S(1)} %get-tuple-element.14), channel_id=1, source_target_pairs={{0,4},{4,0},{8,12},{12,8},{16,20},{20,16},{24,28},{28,24},{1,5},{5... | collective-permute-start | bytes 393224 | tf_op jit(solution)/shard_map/ppermute | solution.py:313
  6.7 8.0 %collective-permute-start.3 = (f32[256,128]{1,0:T(8,128)S(1)}, f32[256,128]{1,0:T(8,128)S(1)}, u32[]{:S(2)}, u32[]{:S(2)}) collective-permute-start(f32[256,128]{1,0:T(8,128)S(1)} %add.24), channel_id=1, source_target_pairs={{0,24},{4,28},{8,16},{12,20},{16,8},{20,12},{24,0},{28,4},{1,25},{... | collective-permute-start | bytes 393224 | tf_op jit(solution)/shard_map/ppermute | solution.py:319
  10.5 6.7 %collective-permute-start.2 = (f32[256,128]{1,0:T(8,128)S(1)}, f32[256,128]{1,0:T(8,128)S(1)}, u32[]{:S(2)}, u32[]{:S(2)}) collective-permute-start(f32[256,128]{1,0:T(8,128)S(1)} %add.24), channel_id=1, source_target_pairs={{0,16},{4,12},{8,24},{12,4},{16,0},{20,28},{24,8},{28,20},{1,17},{... | collective-permute-start | bytes 393224 | tf_op jit(solution)/shard_map/ppermute | solution.py:319
  11.0 6.5 %collective-permute-start.1 = (f32[256,128]{1,0:T(8,128)S(1)}, f32[256,128]{1,0:T(8,128)S(1)}, u32[]{:S(2)}, u32[]{:S(2)}) collective-permute-start(f32[256,128]{1,0:T(8,128)S(1)} %add.24), channel_id=1, source_target_pairs={{0,8},{4,20},{8,0},{12,28},{16,24},{20,4},{24,16},{28,12},{1,9},{5... | collective-permute-start | bytes 393224 | tf_op jit(solution)/shard_map/ppermute | solution.py:319
  17.6 4.0 %collective-permute-start.4 = (bf16[384,128]{1,0:T(8,128)(2,1)S(1)}, bf16[384,128]{1,0:T(8,128)(2,1)S(1)}, u32[]{:S(2)}, u32[]{:S(2)}) collective-permute-start(bf16[384,128]{1,0:T(8,128)(2,1)S(1)} %pad_maximum_fusion.2.refs_0_), channel_id=1, source_target_pairs={{0,4},{4,0},{8,12},{12,8},{16,20},{20,16},{24,28},{28,24},{1,5},{5... | collective-permute-start | bytes 294920 | tf_op jit(solution)/shard_map/ppermute | solution.py:325
  17.9 6.6 %collective-permute-start.6 = (f16[272,128]{1,0:T(8,128)(2,1)S(1)}, f16[272,128]{1,0:T(8,128)(2,1)S(1)}, u32[]{:S(2)}, u32[]{:S(2)}) collective-permute-start(f16[272,128]{1,0:T(8,128)(2,1)S(1)} %pad_maximum_fusion.5), channel_id=1, source_target_pairs={{0,3},{1,2},{2,1},{3,0},{4,7},{5,6},{6,5},{7,4},{8,11},{9,10},{10,... | collective-permute-start | bytes 208904 | tf_op jit(solution)/shard_map/ppermute | solution.py:326
  21.8 6.6 %collective-permute-start.5 = (f16[544,128]{1,0:T(8,128)(2,1)S(1)}, f16[544,128]{1,0:T(8,128)(2,1)S(1)}, u32[]{:S(2)}, u32[]{:S(2)}) collective-permute-start(f16[544,128]{1,0:T(8,128)(2,1)S(1)} %constant_dynamic-update-slice_fusion), channel_id=1, source_target_pairs={{0,1},{1,0},{2,3},{3,2},{4,6},{5,7},{6,4},{7,5},{8,9},{9,8},{10,11... | collective-permute-start | bytes 417800 | tf_op jit(solution)/shard_map/ppermute | solution.py:333
  24.6 1.3 %collective-permute-start.7 = (f16[272,128]{1,0:T(8,128)(2,1)S(1)}, f16[272,128]{1,0:T(8,128)(2,1)S(1)}, u32[]{:S(2)}, u32[]{:S(2)}) collective-permute-start(f16[272,128]{1,0:T(8,128)(2,1)S(1)} %get-tuple-element.29), channel_id=1, source_target_pairs={{0,4},{4,0},{8,12},{12,8},{16,20},{20,16},{24,28},{28,24},{1,5},{5... | collective-permute-start | bytes 208904 | tf_op jit(solution)/shard_map/ppermute | solution.py:337
  28.5 1.4 %collective-permute-start.8 = (f16[544,128]{1,0:T(8,128)(2,1)S(1)}, f16[544,128]{1,0:T(8,128)(2,1)S(1)}, u32[]{:S(2)}, u32[]{:S(2)}) collective-permute-start(f16[544,128]{1,0:T(8,128)(2,1)S(1)} %convert_add_fusion), channel_id=1, source_target_pairs={{0,4},{4,0},{8,12},{12,8},{16,20},{20,16},{24,28},{28,24},{1,5},{5... | collective-permute-start | bytes 417800 | tf_op jit(solution)/shard_map/ppermute | solution.py:340

commit v8 on v7

--- a/solution.py
+++ b/solution.py
@@ -313,7 +313,7 @@
     chip = keep + lax.ppermute(send, "rows", swap)
     chips = size_rows // 2
     total = chip
-    for k in range(1, chips):
+    for k in sorted(range(1, chips), key=lambda k: (k % 2, k)):
         turned = k ^ 3 if chips % 4 == 0 and k % 4 in (1, 2) else k
         perm = [(n, n ^ 2 * (turned if n % 2 else k)) for n in range(size_rows)]
         total = total + lax.ppermute(chip, "rows", perm)

time: 35.1 us -> 35.1 us (level)
  transfers between devices with their start and end apart: 9 -> 9, of which waited for: 5 -> 4; matrix products, arithmetic and copies ran while one was open for 2% -> 2% of each run, Pallas kernels for 20% -> 20%
where the time goes in v8:
time: 35.1 us; the launch traced here: 35 us
  Pallas kernels  16.2 us (46%)
  starting transfers between devices  8.95 us (25%)
  waiting for transfers between devices  7.97 us (23%)
  other arithmetic  0.94 us (3%)
  between operations  0.89 us (3%)
    pallas_call x3, Pallas kernels, add_up(): pl.pallas_call(functools.partial(sum_kernel, len(pieces), len(place), boo...  9.67 us
    ppermute x3, waiting for transfers between devices, per_device(): total = total + lax.ppermute(chip, 'rows', perm)  6.3 us
    pallas_call x1, Pallas kernels, project(): pl.pallas_call(functools.partial(project_kernel, chunks), in_specs=[ANYWH...  4.44 us
    ppermute x3, starting transfers between devices, per_device(): total = total + lax.ppermute(chip, 'rows', perm)  4.39 us
    ppermute x1, starting transfers between devices, per_device(): lax.ppermute(coded, 'reg', [(n, size_reg - 1 - n) for n in range(size_reg)])  3.67 us
    ppermute x1, waiting for transfers between devices, per_device(): lax.ppermute(near, 'rows', swap)  1.2 us
    pallas_call x1, Pallas kernels, select(): pl.pallas_call(functools.partial(select_kernel, row_width, col_width), ou...  1.08 us
    pallas_call x1, Pallas kernels, prepare(): pl.pallas_call(functools.partial(prepare_kernel, len(pieces), row_width,...  1.05 us
  transfers between devices with their start and end apart: 9, of which 4 were waited for; matrix products, arithmetic and copies ran while one was open for 2% of the time, Pallas kernels for 20%

profile of v8, /device:TPU:0, one launch (start us, length us, event | category | flops | bytes accessed | tf_op | source)
XLA Modules:
  0.0 35.0 jit_solution(15290204269582618691)
XLA Ops:
  0.6 4.4 %project.1 = (f32[256,128]{1,0:T(8,128)S(1)}, f32[256,128]{1,0:T(8,128)S(1)}) custom-call(bf16[8192,128]{1,0:T(8,128)(2,1)} %basis_hbm.1, bf16[8192,256]{1,0:T(8,128)(2,1)} %snap_hbm.1, bf16[8192,256]{1,0:T(8,128)(2,1)} %rate_hbm.1), custom_call_target="tpu_custom_call" | custom-call | flops 1073741824 | bytes 10485760 | tf_op jit(solution)/shard_map/project/pallas_call | solution.py:80
  5.1 0.5 %collective-permute-start = (f32[256,128]{1,0:T(8,128)S(1)}, f32[256,128]{1,0:T(8,128)S(1)}, u32[]{:S(2)}, u32[]{:S(2)}) collective-permute-start(f32[256,128]{1,0:T(8,128)S(1)} %get-tuple-element.14), channel_id=1, source_target_pairs={{0,4},{4,0},{8,12},{12,8},{16,20},{20,16},{24,28},{28,24},{1,5},{5... | collective-permute-start | bytes 393224 | tf_op jit(solution)/shard_map/ppermute | solution.py:313
  5.6 1.1 %select.1 = (bf16[1056,256]{1,0:T(8,128)(2,1)S(1)}, bf16[2176,256]{1,0:T(8,128)(2,1)S(1)}, f32[256,128]{1,0:T(8,128)S(1)}) custom-call(), custom_call_target="tpu_custom_call" | custom-call | flops 20000000000 | tf_op jit(solution)/shard_map/select/pallas_call | solution.py:121
  6.7 0.0 collective-permute-done
  6.7 3.7 %collective-permute-start.3 = (f32[256,128]{1,0:T(8,128)S(1)}, f32[256,128]{1,0:T(8,128)S(1)}, u32[]{:S(2)}, u32[]{:S(2)}) collective-permute-start(f32[256,128]{1,0:T(8,128)S(1)} %add.24), channel_id=1, source_target_pairs={{0,24},{4,28},{8,16},{12,20},{16,8},{20,12},{24,0},{28,4},{1,25},{... | collective-permute-start | bytes 393224 | tf_op jit(solution)/shard_map/ppermute | solution.py:319
  10.5 0.5 %collective-permute-start.2 = (f32[256,128]{1,0:T(8,128)S(1)}, f32[256,128]{1,0:T(8,128)S(1)}, u32[]{:S(2)}, u32[]{:S(2)}) collective-permute-start(f32[256,128]{1,0:T(8,128)S(1)} %add.24), channel_id=1, source_target_pairs={{0,8},{4,20},{8,0},{12,28},{16,24},{20,4},{24,16},{28,12},{1,9},{5... | collective-permute-start | bytes 393224 | tf_op jit(solution)/shard_map/ppermute | solution.py:319
  11.0 0.1 collective-permute-start.1
  11.1 0.1 pad_add_fusion.refs_3_.refs_4_
  11.2 3.3 %collective-permute-done.3 = f32[256,128]{1,0:T(8,128)S(1)} collective-permute-done((f32[256,128]{1,0:T(8,128)S(1)}, f32[256,128]{1,0:T(8,128)S(1)}, u32[]{:S(2)}, u32[]{:S(2)}) %collective-permute-start.3) | collective-permute-done | bytes 131104 | tf_op jit(solution)/shard_map/ppermute | solution.py:319
  14.5 3.0 %collective-permute-done.2 = f32[256,128]{1,0:T(8,128)S(1)} collective-permute-done((f32[256,128]{1,0:T(8,128)S(1)}, f32[256,128]{1,0:T(8,128)S(1)}, u32[]{:S(2)}, u32[]{:S(2)}) %collective-permute-start.2) | collective-permute-done | bytes 131104 | tf_op jit(solution)/shard_map/ppermute | solution.py:319
  17.5 0.0 collective-permute-done.1
  17.6 0.1 collective-permute-start.4
  17.8 0.1 select_convert_fusion.1
  17.8 0.1 constant_dynamic-update-slice_fusion.1
  17.9 3.7 %collective-permute-start.6 = (f16[272,128]{1,0:T(8,128)(2,1)S(1)}, f16[272,128]{1,0:T(8,128)(2,1)S(1)}, u32[]{:S(2)}, u32[]{:S(2)}) collective-permute-start(f16[272,128]{1,0:T(8,128)(2,1)S(1)} %pad_maximum_fusion.5), channel_id=1, source_target_pairs={{0,3},{1,2},{2,1},{3,0},{4,7},{5,6},{6,5},{7,4},{8,11},{9,10},{10,... | collective-permute-start | bytes 208904 | tf_op jit(solution)/shard_map/ppermute | solution.py:326
  21.6 0.0 collective-permute-done.4.refs_1_
  21.7 0.1 constant_dynamic-update-slice_fusion
  21.8 0.0 collective-permute-start.5
  21.8 2.3 %add_up.2 = (f32[1056,2304]{1,0:T(8,128)S(1)}, bf16[272,128]{1,0:T(8,128)(2,1)S(1)}) custom-call(bf16[384,128]{1,0:T(8,128)(2,1)S(1)} %pad_maximum_fusion.2.refs_0_, bf16[384,128]{1,0:T(8,128)(2,1)S(1)} %collective-permute-done.4.refs_1_, bf16[1056,256]{1,0:T(8,128)(2,1)S(1)} %get-tuple-element.16.refs_2_.refs_4_.refs_1_.refs_5_, ...), custom_call_target="tpu_custom_call" | custom-call | flops 20000000000 | tf_op jit(solution)/shard_map/add_up/pallas_call | solution.py:268
  24.1 0.4 %collective-permute-done.6 = f16[272,128]{1,0:T(8,128)(2,1)S(1)} collective-permute-done((f16[272,128]{1,0:T(8,128)(2,1)S(1)}, f16[272,128]{1,0:T(8,128)(2,1)S(1)}, u32[]{:S(2)}, u32[]{:S(2)}) %collective-permute-start.6) | collective-permute-done | bytes 69664 | tf_op jit(solution)/shard_map/ppermute | solution.py:326
  24.6 0.1 collective-permute-start.7
  24.7 1.2 %collective-permute-done.7 = f16[272,128]{1,0:T(8,128)(2,1)S(1)} collective-permute-done((f16[272,128]{1,0:T(8,128)(2,1)S(1)}, f16[272,128]{1,0:T(8,128)(2,1)S(1)}, u32[]{:S(2)}, u32[]{:S(2)}) %collective-permute-start.7) | collective-permute-done | bytes 69664 | tf_op jit(solution)/shard_map/ppermute | solution.py:337
  26.0 2.4 %add_up.3 = (f32[1056,2304]{1,0:T(8,128)S(1)}, bf16[544,128]{1,0:T(8,128)(2,1)S(1)}) custom-call(bf16[384,128]{1,0:T(8,128)(2,1)S(1)} %pad_maximum_fusion.3.refs_0_, bf16[384,128]{1,0:T(8,128)(2,1)S(1)} %pad_maximum_fusion.4.refs_1_, f32[1056,2304]{1,0:T(8,128)S(1)} %get-tuple-element.19.refs_2_, s32[2]{0:T(128)S(1)} %pad_add_fusion.refs_3_.refs_4_, ...), custom_call_target="tpu_custom_call" | custom-call | tf_op jit(solution)/shard_map/add_up/pallas_call | solution.py:268
  28.4 0.0 collective-permute-done.5
  28.4 0.1 convert_add_fusion
  28.5 0.2 collective-permute-start.8
  28.8 1.1 %prepare.1 = (bf16[1056,256]{1,0:T(8,128)(2,1)S(1)}, bf16[2304,256]{1,0:T(8,128)(2,1)S(1)}) custom-call(bf16[768,128]{1,0:T(8,128)(2,1)S(1)} %bitcast.38, bf16[1056,256]{1,0:T(8,128)(2,1)S(1)} %get-tuple-element.16.refs_2_.refs_4_.refs_1_.refs_5_, bf16[2176,256]{1,0:T(8,128)(2,1)S(1)} %get-tuple-element.17.refs_3_.refs_5_.refs_2_.refs_6_), custom_call_target="tpu_custom_call" | custom-call | tf_op jit(solution)/shard_map/prepare/pallas_call | solution.py:187
  29.9 0.0 collective-permute-done.8
  30.0 5.0 %add_up_last.1 = (f32[1048,2096]{1,0:T(8,128)}, f32[1048,128]{1,0:T(8,128)}) custom-call(bf16[768,128]{1,0:T(8,128)(2,1)S(1)} %bitcast.39, f32[1056,2304]{1,0:T(8,128)S(1)} %get-tuple-element.21.refs_1_, bf16[1056,256]{1,0:T(8,128)(2,1)S(1)} %get-tuple-element.22.refs_2_, bf16[2304,256]{1,0:T(8,128)(2,1)S(1)} %get-tuple-element.23.refs_3_, ...), custom_call_target="tpu_custom_call" | custom-call | tf_op jit(solution)/shard_map/add_up_last/pallas_call | solution.py:268
  (31 shorter events, 0.6 us)
Async XLA Ops:
  5.1 1.6 %collective-permute-start = (f32[256,128]{1,0:T(8,128)S(1)}, f32[256,128]{1,0:T(8,128)S(1)}, u32[]{:S(2)}, u32[]{:S(2)}) collective-permute-start(f32[256,128]{1,0:T(8,128)S(1)} %get-tuple-element.14), channel_id=1, source_target_pairs={{0,4},{4,0},{8,12},{12,8},{16,20},{20,16},{24,28},{28,24},{1,5},{5... | collective-permute-start | bytes 393224 | tf_op jit(solution)/shard_map/ppermute | solution.py:313
  6.7 7.8 %collective-permute-start.3 = (f32[256,128]{1,0:T(8,128)S(1)}, f32[256,128]{1,0:T(8,128)S(1)}, u32[]{:S(2)}, u32[]{:S(2)}) collective-permute-start(f32[256,128]{1,0:T(8,128)S(1)} %add.24), channel_id=1, source_target_pairs={{0,24},{4,28},{8,16},{12,20},{16,8},{20,12},{24,0},{28,4},{1,25},{... | collective-permute-start | bytes 393224 | tf_op jit(solution)/shard_map/ppermute | solution.py:319
  10.5 7.0 %collective-permute-start.2 = (f32[256,128]{1,0:T(8,128)S(1)}, f32[256,128]{1,0:T(8,128)S(1)}, u32[]{:S(2)}, u32[]{:S(2)}) collective-permute-start(f32[256,128]{1,0:T(8,128)S(1)} %add.24), channel_id=1, source_target_pairs={{0,8},{4,20},{8,0},{12,28},{16,24},{20,4},{24,16},{28,12},{1,9},{5... | collective-permute-start | bytes 393224 | tf_op jit(solution)/shard_map/ppermute | solution.py:319
  11.0 6.5 %collective-permute-start.1 = (f32[256,128]{1,0:T(8,128)S(1)}, f32[256,128]{1,0:T(8,128)S(1)}, u32[]{:S(2)}, u32[]{:S(2)}) collective-permute-start(f32[256,128]{1,0:T(8,128)S(1)} %add.24), channel_id=1, source_target_pairs={{0,16},{4,12},{8,24},{12,4},{16,0},{20,28},{24,8},{28,20},{1,17},{... | collective-permute-start | bytes 393224 | tf_op jit(solution)/shard_map/ppermute | solution.py:319
  17.6 4.0 %collective-permute-start.4 = (bf16[384,128]{1,0:T(8,128)(2,1)S(1)}, bf16[384,128]{1,0:T(8,128)(2,1)S(1)}, u32[]{:S(2)}, u32[]{:S(2)}) collective-permute-start(bf16[384,128]{1,0:T(8,128)(2,1)S(1)} %pad_maximum_fusion.2.refs_0_), channel_id=1, source_target_pairs={{0,4},{4,0},{8,12},{12,8},{16,20},{20,16},{24,28},{28,24},{1,5},{5... | collective-permute-start | bytes 294920 | tf_op jit(solution)/shard_map/ppermute | solution.py:325
  17.9 6.6 %collective-permute-start.6 = (f16[272,128]{1,0:T(8,128)(2,1)S(1)}, f16[272,128]{1,0:T(8,128)(2,1)S(1)}, u32[]{:S(2)}, u32[]{:S(2)}) collective-permute-start(f16[272,128]{1,0:T(8,128)(2,1)S(1)} %pad_maximum_fusion.5), channel_id=1, source_target_pairs={{0,3},{1,2},{2,1},{3,0},{4,7},{5,6},{6,5},{7,4},{8,11},{9,10},{10,... | collective-permute-start | bytes 208904 | tf_op jit(solution)/shard_map/ppermute | solution.py:326
  21.8 6.6 %collective-permute-start.5 = (f16[544,128]{1,0:T(8,128)(2,1)S(1)}, f16[544,128]{1,0:T(8,128)(2,1)S(1)}, u32[]{:S(2)}, u32[]{:S(2)}) collective-permute-start(f16[544,128]{1,0:T(8,128)(2,1)S(1)} %constant_dynamic-update-slice_fusion), channel_id=1, source_target_pairs={{0,1},{1,0},{2,3},{3,2},{4,6},{5,7},{6,4},{7,5},{8,9},{9,8},{10,11... | collective-permute-start | bytes 417800 | tf_op jit(solution)/shard_map/ppermute | solution.py:333
  24.6 1.3 %collective-permute-start.7 = (f16[272,128]{1,0:T(8,128)(2,1)S(1)}, f16[272,128]{1,0:T(8,128)(2,1)S(1)}, u32[]{:S(2)}, u32[]{:S(2)}) collective-permute-start(f16[272,128]{1,0:T(8,128)(2,1)S(1)} %get-tuple-element.29), channel_id=1, source_target_pairs={{0,4},{4,0},{8,12},{12,8},{16,20},{20,16},{24,28},{28,24},{1,5},{5... | collective-permute-start | bytes 208904 | tf_op jit(solution)/shard_map/ppermute | solution.py:337
  28.5 1.4 %collective-permute-start.8 = (f16[544,128]{1,0:T(8,128)(2,1)S(1)}, f16[544,128]{1,0:T(8,128)(2,1)S(1)}, u32[]{:S(2)}, u32[]{:S(2)}) collective-permute-start(f16[544,128]{1,0:T(8,128)(2,1)S(1)} %convert_add_fusion), channel_id=1, source_target_pairs={{0,4},{4,0},{8,12},{12,8},{16,20},{20,16},{24,28},{28,24},{1,5},{5... | collective-permute-start | bytes 417800 | tf_op jit(solution)/shard_map/ppermute | solution.py:340
